TPU v7x, 128 devices: a whole 4x4x4 slice. The times are simulated.
128 devices in a mesh: ctx: 8 (over z, core), img: 16 (over y, x).
Axes of the slice: x: 4, y: 4, z: 4, core: 2. Of those that a mesh axis runs over, the one named last changes fastest.
Arguments:
- queries: bfloat16 [16384, 4096], P(('ctx', 'img')), may hold values from -110 to 110
- tile_ids: int32 [16384, 1], P(('ctx', 'img')), may hold values from 0 to 15; in each aligned block of 128 rows (0 to 127, 128 to 255, ...) at most 9 rows name the same one
- keys: bfloat16 [16, 1664, 512], P('img'), may hold values from -6 to 6
- values: bfloat16 [16, 1664, 512], P('img'), may hold values from -6 to 6
- patch_counts: int32 [16], P('img'), may hold values from 801 to 1601, as said below
- output_gradient: bfloat16 [16384, 4096], P(('ctx', 'img')), may hold values from -6 to 6
Outputs:
- attended: bfloat16 [16384, 4096], P(('ctx', 'img'))
- query_grad: bfloat16 [16384, 4096], P(('ctx', 'img'))
- key_grad: float32 [16, 1664, 512], P('img', 'ctx')
- value_grad: float32 [16, 1664, 512], P('img', 'ctx')
Inputs may be any that keep to these rules, and one draw needn't show every extreme that they name: `tile_ids`: each token names one tile; among the 128 tokens of one device no tile is named by more than 9 tokens, a bound that some block reaches. `patch_counts`: some tile has all 1601 patches valid.
All inputs are finite; a program needn't handle non-finite values.
Results may differ from a plain program's by a relative error of at most 0.038.
Values may be sent and summed in bfloat16 or wider, within the bound.
No kernel may reach another device: no remote copies, remote signals or barrier semaphores. Data moves between devices by JAX's collectives and lax.ppermute only.
A program may use at most 128 MiB of HBM per device.

v0:
```python
import math

import jax
import jax.numpy as jnp
from jax import lax
from jax.sharding import PartitionSpec as P

HQ = 32
HEAD_WIDTH = 128
LIST = 1


def multiply(pattern, left_operand, right_op):
    return jnp.einsum(pattern, left_operand, right_op, preferred_element_type=jnp.float32)


def route_slots(tile_ids, tile_num, capacity):
    onehot = (tile_ids[:, :, None] == jnp.arange(tile_num, dtype=jnp.int32)[None, None, :]).astype(
        jnp.int32
    )
    flagged = jnp.sum(onehot, axis=1)
    before = jnp.cumsum(flagged, axis=0) - flagged
    slot_of = jnp.sum(onehot * before[:, None, :], axis=2)
    return tile_ids * capacity + slot_of


def dispatch_index(flat_slot, total):
    token_num = flat_slot.shape[0]
    owner_ids = jnp.arange(token_num, dtype=jnp.int32)[:, None]
    filled = jnp.full((total,), token_num, jnp.int32)
    return filled.at[flat_slot.reshape(-1)].set(owner_ids.reshape(-1))


def padded_take(source, index_map):
    extended = jnp.concatenate([source, jnp.zeros((1,) + source.shape[1:], source.dtype)], axis=0)
    return extended[index_map]


def tile_forward(query_rows, key_tile, value_tile, counts):
    tile_num, row_num, row_width = query_rows.shape
    key_heads = key_tile.shape[2] // HEAD_WIDTH
    group_size = row_width // HEAD_WIDTH // key_heads
    inv_root = 1.0 / math.sqrt(HEAD_WIDTH)
    live_keys = jnp.arange(key_tile.shape[1], dtype=jnp.int32)[None, :] < counts[:, None]
    out_list, max_list, total_list = ([], [], [])
    for head_group in range(key_heads):
        query_start = head_group * group_size * HEAD_WIDTH
        query_part = query_rows[:, :, query_start : query_start + group_size * HEAD_WIDTH].reshape(
            tile_num, row_num, group_size, HEAD_WIDTH
        )
        key_part = key_tile[:, :, head_group * HEAD_WIDTH : (head_group + 1) * HEAD_WIDTH]
        value_part = value_tile[:, :, head_group * HEAD_WIDTH : (head_group + 1) * HEAD_WIDTH]
        scores = multiply("trhd,tkd->trhk", query_part, key_part) * inv_root
        scores = jnp.where(live_keys[:, None, None, :], scores, -jnp.inf)
        part_peak = jnp.max(scores, axis=3)
        weights = jnp.exp(scores - part_peak[..., None])
        total_list.append(jnp.sum(weights, axis=3))
        max_list.append(part_peak)
        mixed = multiply("trhk,tkd->trhd", weights.astype(jnp.bfloat16), value_part)
        out_list.append(mixed.reshape(tile_num, row_num, group_size * HEAD_WIDTH))
    return (
        jnp.concatenate(out_list, axis=2),
        jnp.concatenate(max_list, axis=2),
        jnp.concatenate(total_list, axis=2),
    )


def tile_backward(query_rows, grad_rows, total_rows, dot_rows, key_tile, value_tile, counts):
    tile_num, row_num, row_width = query_rows.shape
    key_heads = key_tile.shape[2] // HEAD_WIDTH
    group_size = row_width // HEAD_WIDTH // key_heads
    inv_root = 1.0 / math.sqrt(HEAD_WIDTH)
    live_keys = jnp.arange(key_tile.shape[1], dtype=jnp.int32)[None, :] < counts[:, None]
    query_list, key_list, value_list = ([], [], [])
    for head_group in range(key_heads):
        query_start = head_group * group_size * HEAD_WIDTH
        head_start = head_group * group_size
        query_part = query_rows[:, :, query_start : query_start + group_size * HEAD_WIDTH].reshape(
            tile_num, row_num, group_size, HEAD_WIDTH
        )
        grad_part = grad_rows[:, :, query_start : query_start + group_size * HEAD_WIDTH].reshape(
            tile_num, row_num, group_size, HEAD_WIDTH
        )
        total_part = total_rows[:, :, head_start : head_start + group_size]
        dot_part = dot_rows[:, :, head_start : head_start + group_size]
        key_part = key_tile[:, :, head_group * HEAD_WIDTH : (head_group + 1) * HEAD_WIDTH]
        value_part = value_tile[:, :, head_group * HEAD_WIDTH : (head_group + 1) * HEAD_WIDTH]
        scores = multiply("trhd,tkd->trhk", query_part, key_part) * inv_root
        scores = jnp.where(live_keys[:, None, None, :], scores, -jnp.inf)
        prob_full = jnp.exp(scores - total_part[..., None])
        value_list.append(multiply("trhk,trhd->tkd", prob_full.astype(jnp.bfloat16), grad_part))
        prob_grad = multiply("trhd,tkd->trhk", grad_part, value_part)
        score_grad = (prob_full * (prob_grad - dot_part[..., None])).astype(jnp.bfloat16)
        query_term = multiply("trhk,tkd->trhd", score_grad, key_part) * inv_root
        query_list.append(query_term.reshape(tile_num, row_num, group_size * HEAD_WIDTH))
        key_list.append(multiply("trhk,trhd->tkd", score_grad, query_part) * inv_root)
    return (
        jnp.concatenate(query_list, axis=2),
        jnp.concatenate(key_list, axis=2),
        jnp.concatenate(value_list, axis=2),
    )


def merge_partials(part_out, part_max, part_total):
    token_num = part_out.shape[0]
    highest = jnp.max(part_max, axis=1)
    factor = jnp.exp(part_max - highest[:, None, :])
    denominator = jnp.sum(factor * part_total, axis=1)
    heads_out = part_out.reshape(token_num, LIST, HQ, HEAD_WIDTH)
    numerator = jnp.sum(factor[..., None] * heads_out, axis=1)
    attended = (
        (numerator / denominator[..., None])
        .reshape(token_num, HQ * HEAD_WIDTH)
        .astype(jnp.bfloat16)
    )
    return (attended, highest + jnp.log(denominator))


def head_dot(output_gradient, attended):
    token_num = output_gradient.shape[0]
    joined = output_gradient.astype(jnp.float32) * attended.astype(jnp.float32)
    return jnp.sum(joined.reshape(token_num, HQ, HEAD_WIDTH), axis=2)


def local(queries, tile_ids, keys, values, patch_counts, output_gradient):
    img_count = lax.axis_size("img")
    token_num, row_width = queries.shape
    capacity = 9 * token_num * LIST // (8 * img_count)
    slot_total = img_count * capacity
    flat_slot = route_slots(tile_ids, img_count, capacity)
    index_map = dispatch_index(flat_slot, slot_total)
    sent_rows = padded_take(queries, index_map).reshape(img_count, capacity, row_width)
    received = lax.all_to_all(sent_rows, "img", split_axis=0, concat_axis=0, tiled=True)
    item_num = received.shape[1]
    part_out, part_max, part_total = tile_forward(
        received.reshape(1, img_count * item_num, row_width), keys, values, patch_counts
    )
    attended, log_total = merge_partials(
        lax.all_to_all(
            part_out.reshape(img_count, item_num, row_width),
            "img",
            split_axis=0,
            concat_axis=0,
            tiled=True,
        ).reshape(slot_total, row_width)[flat_slot],
        lax.all_to_all(
            part_max.reshape(img_count, item_num, HQ),
            "img",
            split_axis=0,
            concat_axis=0,
            tiled=True,
        ).reshape(slot_total, HQ)[flat_slot],
        lax.all_to_all(
            part_total.reshape(img_count, item_num, HQ),
            "img",
            split_axis=0,
            concat_axis=0,
            tiled=True,
        ).reshape(slot_total, HQ)[flat_slot],
    )
    grad_dot = head_dot(output_gradient, attended)
    grad_rows = padded_take(output_gradient, index_map).reshape(img_count, capacity, row_width)
    total_out = padded_take(log_total, index_map).reshape(img_count, capacity, HQ)
    dot_out = padded_take(grad_dot, index_map).reshape(img_count, capacity, HQ)
    total_in, dot_in = (
        lax.all_to_all(total_out, "img", split_axis=0, concat_axis=0, tiled=True),
        lax.all_to_all(dot_out, "img", split_axis=0, concat_axis=0, tiled=True),
    )
    query_in, incoming_gradient = (
        lax.all_to_all(sent_rows, "img", split_axis=0, concat_axis=0, tiled=True),
        lax.all_to_all(grad_rows, "img", split_axis=0, concat_axis=0, tiled=True),
    )
    query_terms, key_terms, value_terms = tile_backward(
        query_in.reshape(1, slot_total, row_width),
        incoming_gradient.reshape(1, slot_total, row_width),
        total_in.reshape(1, slot_total, HQ),
        dot_in.reshape(1, slot_total, HQ),
        keys,
        values,
        patch_counts,
    )
    grad_back = lax.all_to_all(
        query_terms.reshape(img_count, capacity, row_width).astype(jnp.bfloat16),
        "img",
        split_axis=0,
        concat_axis=0,
        tiled=True,
    ).astype(jnp.float32)
    query_grad = jnp.sum(grad_back.reshape(slot_total, row_width)[flat_slot], axis=1).astype(
        jnp.bfloat16
    )
    summed = lax.psum((key_terms, value_terms), "ctx")
    share_rows = keys.shape[1] // lax.axis_size("ctx")
    first_row = lax.axis_index("ctx") * share_rows
    key_grad = lax.dynamic_slice_in_dim(summed[0], first_row, share_rows, 1)
    value_grad = lax.dynamic_slice_in_dim(summed[1], first_row, share_rows, 1)
    return (attended, query_grad, key_grad, value_grad)


def solution(mesh):
    in_specs = (
        P(("ctx", "img"), None),
        P(("ctx", "img"), None),
        P("img", None, None),
        P("img", None, None),
        P("img"),
        P(("ctx", "img"), None),
    )
    out_specs = (
        P(("ctx", "img"), None),
        P(("ctx", "img"), None),
        P("img", "ctx", None),
        P("img", "ctx", None),
    )
    return jax.shard_map(local, mesh=mesh, in_specs=in_specs, out_specs=out_specs, check_vma=False)
```

profile of v0, /device:TPU:0, one launch (start us, length us, event | category | flops | bytes accessed | tf_op | source)
XLA Modules:
  0.0 385.5 jit_solution(37465173910203461)
XLA Ops:
  7.2 3.4 fusion.101
  14.8 1.6 reshape.503
  16.4 7.1 %all-to-all-start = ((bf16[16,9,4096]{2,1,0:T(8,128)(2,1)}), bf16[16,9,4096]{2,1,0:T(8,128)(2,1)S(1)}, u32[]{:S(2)}, u32[]{:S(2)}) async-start(bf16[16,9,4096]{2,1,0:T(8,128)(2,1)} %reshape.503), calls=%async_computation | async-start | bytes 4194304 | tf_op jit(solution)/shard_map/all_to_all | solution.py:133
  25.5 2.3 gather_fusion.5
  27.8 2.6 reshape.523
  30.5 24.7 %all-to-all-done = bf16[16,9,4096]{2,1,0:T(8,128)(2,1)S(1)} async-done(((bf16[16,9,4096]{2,1,0:T(8,128)(2,1)}), bf16[16,9,4096]{2,1,0:T(8,128)(2,1)S(1)}, u32[]{:S(2)}, u32[]{:S(2)}) %all-to-all-start) | async-done | bytes 1179680 | tf_op jit(solution)/shard_map/all_to_all | solution.py:133
  55.2 1.3 copy-done.7
  56.6 3.7 all-to-all-start.5
  60.3 2.0 reshape.504
  63.3 5.6 %fusion.104 = (f32[144,8]{1,0:T(8,128)S(1)}, f32[144,8,1664]{2,1,0:T(8,128)}) fusion(bf16[144,8,128]{2,1,0:T(8,128)(2,1)S(1)} %bitcast.228, bf16[1,1664,512]{2,1,0:T(8,128)(2,1)} %param.8, pred[1664]{0:T(1024)(128)(4,1)S(1)} %iota_compare_fusion), kind=kOutput, calls=%fused_computation.157 | convolution fusion | flops 496483200 | bytes 8394880 | tf_op jit(solution)/shard_map/trhd,tkd->trhk/dot_general | solution.py:14
  69.0 4.5 %fusion.2 = f32[144,8]{1,0:T(8,128)S(1)} fusion(f32[144,8,1664]{2,1,0:T(8,128)} %get-tuple-element.48, f32[144,8]{1,0:T(8,128)S(1)} %get-tuple-element.47), kind=kLoop, calls=%fused_computation.27 | loop fusion | flops 3832704 | bytes 7676928 | tf_op jit(solution)/shard_map/reduce_sum | solution.py:57
  74.4 3.2 fusion.24
  77.6 5.4 %fusion.103 = (f32[144,8]{1,0:T(8,128)S(1)}, f32[144,8,1664]{2,1,0:T(8,128)}) fusion(bf16[144,8,128]{2,1,0:T(8,128)(2,1)S(1)} %bitcast.224, bf16[1,1664,512]{2,1,0:T(8,128)(2,1)} %param.8, pred[1664]{0:T(1024)(128)(4,1)S(1)} %iota_compare_fusion), kind=kOutput, calls=%fused_computation.156 | convolution fusion | flops 496483200 | bytes 8394880 | tf_op jit(solution)/shard_map/trhd,tkd->trhk/dot_general | solution.py:14
  83.0 4.5 %fusion.4 = f32[144,8]{1,0:T(8,128)S(1)} fusion(f32[144,8,1664]{2,1,0:T(8,128)} %get-tuple-element.46, f32[144,8]{1,0:T(8,128)S(1)} %get-tuple-element.45), kind=kLoop, calls=%fused_computation.29 | loop fusion | flops 3832704 | bytes 7676928 | tf_op jit(solution)/shard_map/reduce_sum | solution.py:57
  88.4 3.3 fusion.22
  92.3 5.4 %fusion.102 = (f32[144,8]{1,0:T(8,128)S(1)}, f32[144,8,1664]{2,1,0:T(8,128)}) fusion(bf16[144,8,128]{2,1,0:T(8,128)(2,1)S(1)} %bitcast.230, bf16[1,1664,512]{2,1,0:T(8,128)(2,1)} %param.8, pred[1664]{0:T(1024)(128)(4,1)S(1)} %iota_compare_fusion), kind=kOutput, calls=%fused_computation.155 | convolution fusion | flops 496483200 | bytes 8394880 | tf_op jit(solution)/shard_map/trhd,tkd->trhk/dot_general | solution.py:14
  97.9 4.3 %fusion.6 = f32[144,8]{1,0:T(8,128)S(1)} fusion(f32[144,8,1664]{2,1,0:T(8,128)} %get-tuple-element.44, f32[144,8]{1,0:T(8,128)S(1)} %get-tuple-element.43), kind=kLoop, calls=%fused_computation.31 | loop fusion | flops 3832704 | bytes 7676928 | tf_op jit(solution)/shard_map/reduce_sum | solution.py:57
  102.4 5.6 %fusion.105 = (f32[144,8]{1,0:T(8,128)S(1)}, f32[144,8,1664]{2,1,0:T(8,128)}) fusion(bf16[144,8,128]{2,1,0:T(8,128)(2,1)S(1)} %bitcast.226, bf16[1,1664,512]{2,1,0:T(8,128)(2,1)} %param.8, pred[1664]{0:T(1024)(128)(4,1)S(1)} %iota_compare_fusion), kind=kOutput, calls=%fused_computation.158 | convolution fusion | flops 496483200 | bytes 8394880 | tf_op jit(solution)/shard_map/trhd,tkd->trhk/dot_general | solution.py:14
  108.1 4.3 %fusion = f32[144,8]{1,0:T(8,128)S(1)} fusion(f32[144,8,1664]{2,1,0:T(8,128)} %get-tuple-element.50, f32[144,8]{1,0:T(8,128)S(1)} %get-tuple-element.49), kind=kLoop, calls=%fused_computation.25 | loop fusion | flops 3832704 | bytes 7676928 | tf_op jit(solution)/shard_map/reduce_sum | solution.py:57
  113.6 5.5 %fusion.20 = f32[144,8,128]{2,1,0:T(8,128)} fusion(f32[144,8,1664]{2,1,0:T(8,128)} %get-tuple-element.44, f32[144,8]{1,0:T(8,128)S(1)} %get-tuple-element.43, bf16[1,1664,512]{2,1,0:T(8,128)(2,1)} %param.9), kind=kOutput, calls=%fused_computation.42 | convolution fusion | flops 494567424 | bytes 8688128 | tf_op jit(solution)/shard_map/trhk,tkd->trhd/dot_general | solution.py:14
  119.1 3.2 fusion.26
  122.2 7.2 %all-to-all-start.1 = ((f32[16,1,288]{2,1,0:T(1,128)}), f32[16,1,288]{2,1,0:T(1,128)}, u32[]{:S(2)}, u32[]{:S(2)}) async-start(f32[16,1,288]{2,1,0:T(1,128)} %reshape.641), calls=%async_computation.1 | async-start | bytes 49152 | tf_op jit(solution)/shard_map/all_to_all | solution.py:146
  130.6 2.1 concatenate.75
  132.7 2.1 concatenate.76
  135.8 2.1 concatenate.73
  137.9 7.2 %all-to-all-start.3 = ((f32[16,1,288]{2,1,0:T(1,128)}), f32[16,1,288]{2,1,0:T(1,128)S(1)}, u32[]{:S(2)}, u32[]{:S(2)}) async-start(f32[16,1,288]{2,1,0:T(1,128)} %reshape.639), calls=%async_computation.3 | async-start | bytes 49152 | tf_op jit(solution)/shard_map/all_to_all | solution.py:153
  145.1 4.2 %pad_maximum_fusion = f32[16,9,4096]{2,1,0:T(8,128)} fusion(f32[16,9,1024]{2,1,0:T(8,128)} %concatenate.76, f32[16,9,1024]{2,1,0:T(8,128)} %concatenate.75, f32[16,9,1024]{2,1,0:T(8,128)S(1)} %concatenate.74, f32[16,9,1024]{2,1,0:T(8,128)} %concatenate.73), kind=kLoop, calls=%fused_computation.37 | loop fusion | flops 1769472 | bytes 4718592 | tf_op jit(solution)/shard_map/concatenate | solution.py:62
  149.3 3.4 all-to-all-done.3
  152.7 4.5 %all-to-all-start.2 = ((f32[16,9,4096]{2,1,0:T(8,128)}), f32[16,9,4096]{2,1,0:T(8,128)}, u32[]{:S(2)}, u32[]{:S(2)}) async-start(f32[16,9,4096]{2,1,0:T(8,128)} %pad_maximum_fusion), calls=%async_computation.2 | async-start | bytes 8388608 | tf_op jit(solution)/shard_map/all_to_all | solution.py:139
  157.2 1.4 reshape.524
  160.0 1.4 reduce.17
  164.2 47.6 %all-to-all-done.2 = f32[16,9,4096]{2,1,0:T(8,128)} async-done(((f32[16,9,4096]{2,1,0:T(8,128)}), f32[16,9,4096]{2,1,0:T(8,128)}, u32[]{:S(2)}, u32[]{:S(2)}) %all-to-all-start.2) | async-done | bytes 2359328 | tf_op jit(solution)/shard_map/all_to_all | solution.py:139
  211.8 4.5 %all-to-all-start.4 = ((f32[16,1,288]{2,1,0:T(1,128)}), f32[16,1,288]{2,1,0:T(1,128)S(1)}, u32[]{:S(2)}, u32[]{:S(2)}) async-start(f32[16,1,288]{2,1,0:T(1,128)} %reshape.645), calls=%async_computation.4 | async-start | bytes 49152 | tf_op jit(solution)/shard_map/all_to_all | solution.py:166
  216.4 2.4 reshape.518
  218.8 2.5 gather_fusion.2
  223.2 5.0 %multiply_bitcast_fusion = (f32[16,8,32,128]{3,1,2,0:T(8,128)S(1)}, bf16[128,4096]{1,0:T(8,128)(2,1)}) fusion(bf16[128,4096]{1,0:T(8,128)(2,1)S(1)} %copy-done.11, f32[16,8,32,128]{3,2,1,0:T(8,128)S(1)} %bitcast.221, f32[128,4096]{1,0:T(8,128)S(1)} %copy-done.8, f32[16,8,32,128]{3,2,1,0:T(8,128)S(1)} %bitcast.222), kind=kLoop, calls=%fused_computation.76 | loop fusion | flops 3145728 | bytes 10485760
  230.6 7.4 %all-to-all-start.6 = ((f32[16,1,288]{2,1,0:T(1,128)}), f32[16,1,288]{2,1,0:T(1,128)}, u32[]{:S(2)}, u32[]{:S(2)}) async-start(f32[16,1,288]{2,1,0:T(1,128)} %reshape.643), calls=%async_computation.6 | async-start | bytes 49152 | tf_op jit(solution)/shard_map/all_to_all | solution.py:167
  238.0 1.5 slice_bitcast_fusion.3
  245.6 2.0 reduce.19
  247.6 1.5 reshape.644
  249.1 1.5 reshape.528
  250.6 1.9 slice_bitcast_fusion.14
  252.5 4.8 %fusion.47 = f32[1,1664,128]{1,2,0:T(8,128)S(1)} fusion(bf16[144,8,128]{2,1,0:T(8,128)(2,1)} %bitcast.238, f32[144,8,1664]{2,1,0:T(8,128)} %get-tuple-element.48, f32[144,8]{1,0:T(8,128)S(1)} %get-tuple-element.51), kind=kOutput, calls=%fused_computation.69 | convolution fusion | flops 494567424 | bytes 8819200 | tf_op jit(solution)/shard_map/trhk,trhd->tkd/dot_general | solution.py:14
  257.4 2.0 multiply_convert_fusion.2
  261.3 1.4 fusion.50
  262.8 2.1 multiply_convert_fusion.1
  266.8 1.5 fusion.53
  268.3 2.1 multiply_convert_fusion
  272.4 1.5 fusion.44
  273.9 2.3 multiply_convert_fusion.3
  278.0 2.1 pad_maximum_fusion.2
  280.1 2.1 pad_maximum_fusion.1
  282.2 1.4 copy-done.9
  283.6 3.2 fusion.58
  287.0 3.2 fusion.59
  290.4 4.3 %fusion.60 = bf16[144,8,128]{2,1,0:T(8,128)(2,1)} fusion(bf16[144,8,1664]{2,1,0:T(8,128)(2,1)} %copy-done.5, bf16[1,1664,512]{2,1,0:T(8,128)(2,1)S(1)} %copy-done.9), kind=kOutput, calls=%fused_computation.84 | convolution fusion | flops 491028480 | bytes 4554752 | tf_op jit(solution)/shard_map/trhk,tkd->trhd/dot_general | solution.py:14
  295.8 4.0 %fusion.57 = bf16[144,8,128]{2,1,0:T(8,128)(2,1)} fusion(bf16[144,8,1664]{2,1,0:T(8,128)(2,1)} %copy-done.6, bf16[1,1664,512]{2,1,0:T(8,128)(2,1)S(1)} %copy-done.9), kind=kOutput, calls=%fused_computation.81 | convolution fusion | flops 491028480 | bytes 4554752 | tf_op jit(solution)/shard_map/trhk,tkd->trhd/dot_general | solution.py:14
  300.9 1.6 pad_maximum_fusion.3
  302.6 6.1 %all-to-all-start.7 = ((bf16[16,9,4096]{2,1,0:T(8,128)(2,1)}), bf16[16,9,4096]{2,1,0:T(8,128)(2,1)S(1)}, u32[]{:S(2)}, u32[]{:S(2)}) async-start(bf16[16,9,4096]{2,1,0:T(8,128)(2,1)} %pad_maximum_fusion.3), calls=%async_computation.7 | async-start | bytes 4194304 | tf_op jit(solution)/shard_map/all_to_all | solution.py:182
  308.7 27.5 %all-to-all-done.7 = bf16[16,9,4096]{2,1,0:T(8,128)(2,1)S(1)} async-done(((bf16[16,9,4096]{2,1,0:T(8,128)(2,1)}), bf16[16,9,4096]{2,1,0:T(8,128)(2,1)S(1)}, u32[]{:S(2)}, u32[]{:S(2)}) %all-to-all-start.7) | async-done | bytes 1179680 | tf_op jit(solution)/shard_map/all_to_all | solution.py:182
  336.8 2.2 gather_fusion.7
  338.9 34.9 %all-reduce.7.cloned.1.call-done = (f32[1,1664,512]{1,2,0:T(8,128)}, f32[1,1664,512]{1,2,0:T(8,128)}) async-done(((f32[1,1664,512]{1,2,0:T(8,128)}, f32[1,1664,512]{1,2,0:T(8,128)}), (f32[1,1664,512]{1,2,0:T(8,128)}, f32[1,1664,512]{1,2,0:T(8,128)})) %all-reduce.7.cloned.1.call-update) | async-done | bytes 6815760 | tf_op jit(solution)/shard_map/psum | solution.py:192
  373.9 1.3 constant_dynamic-slice_fusion
  375.2 1.3 constant_dynamic-slice_fusion.1
  (157 shorter events, 39.7 us)
Async XLA Ops:
  16.4 38.8 %all-to-all-start = ((bf16[16,9,4096]{2,1,0:T(8,128)(2,1)}), bf16[16,9,4096]{2,1,0:T(8,128)(2,1)S(1)}, u32[]{:S(2)}, u32[]{:S(2)}) async-start(bf16[16,9,4096]{2,1,0:T(8,128)(2,1)} %reshape.503), calls=%async_computation | async-start | bytes 4194304 | tf_op jit(solution)/shard_map/all_to_all | solution.py:133
  55.2 1.3 copy-start.7
  56.6 65.7 %all-to-all-start.5 = ((bf16[16,9,4096]{2,1,0:T(8,128)(2,1)}), bf16[16,9,4096]{2,1,0:T(8,128)(2,1)S(1)}, u32[]{:S(2)}, u32[]{:S(2)}) async-start(bf16[16,9,4096]{2,1,0:T(8,128)(2,1)} %reshape.523), calls=%async_computation.5 | async-start | bytes 4194304 | tf_op jit(solution)/shard_map/all_to_all | solution.py:171
  63.2 14.3 %copy-start.12 = (bf16[18,8,8,128]{3,2,1,0:T(8,128)(2,1)}, bf16[18,8,8,128]{3,2,1,0:T(8,128)(2,1)S(1)}, u32[]{:S(2)}) copy-start(bf16[18,8,8,128]{3,2,1,0:T(8,128)(2,1)S(1)} %copy.86) | copy-start | bytes 884740
  63.3 5.6 %copy-start.16 = (bf16[18,8,8,128]{3,2,1,0:T(8,128)(2,1)}, bf16[18,8,8,128]{3,2,1,0:T(8,128)(2,1)S(1)}, u32[]{:S(2)}) copy-start(bf16[18,8,8,128]{3,2,1,0:T(8,128)(2,1)S(1)} %copy.85) | copy-start | bytes 884740
  69.0 5.4 %copy-start = (f32[144,8,1664]{2,1,0:T(8,128)S(1)}, f32[144,8,1664]{2,1,0:T(8,128)}, u32[]{:S(2)}) copy-start(f32[144,8,1664]{2,1,0:T(8,128)} %get-tuple-element.48) | copy-start | bytes 23003140
  83.0 5.4 %copy-start.1 = (f32[144,8,1664]{2,1,0:T(8,128)S(1)}, f32[144,8,1664]{2,1,0:T(8,128)}, u32[]{:S(2)}) copy-start(f32[144,8,1664]{2,1,0:T(8,128)} %get-tuple-element.46) | copy-start | bytes 23003140
  88.4 3.3 copy-start.25
  88.4 3.3 copy-start.24
  91.7 10.7 %copy-start.14 = (bf16[18,8,8,128]{3,2,1,0:T(8,128)(2,1)}, bf16[18,8,8,128]{3,2,1,0:T(8,128)(2,1)S(1)}, u32[]{:S(2)}) copy-start(bf16[18,8,8,128]{3,2,1,0:T(8,128)(2,1)S(1)} %copy.84) | copy-start | bytes 884740
  91.8 6.0 %copy-start.18 = (bf16[18,8,8,128]{3,2,1,0:T(8,128)(2,1)}, bf16[18,8,8,128]{3,2,1,0:T(8,128)(2,1)S(1)}, u32[]{:S(2)}) copy-start(bf16[18,8,8,128]{3,2,1,0:T(8,128)(2,1)S(1)} %copy.87) | copy-start | bytes 884740
  113.6 5.5 %copy-start.2 = (f32[144,8,1664]{2,1,0:T(8,128)S(1)}, f32[144,8,1664]{2,1,0:T(8,128)}, u32[]{:S(2)}) copy-start(f32[144,8,1664]{2,1,0:T(8,128)} %get-tuple-element.50) | copy-start | bytes 23003140
  122.2 15.7 %all-to-all-start.1 = ((f32[16,1,288]{2,1,0:T(1,128)}), f32[16,1,288]{2,1,0:T(1,128)}, u32[]{:S(2)}, u32[]{:S(2)}) async-start(f32[16,1,288]{2,1,0:T(1,128)} %reshape.641), calls=%async_computation.1 | async-start | bytes 49152 | tf_op jit(solution)/shard_map/all_to_all | solution.py:146
  137.9 14.8 %all-to-all-start.3 = ((f32[16,1,288]{2,1,0:T(1,128)}), f32[16,1,288]{2,1,0:T(1,128)S(1)}, u32[]{:S(2)}, u32[]{:S(2)}) async-start(f32[16,1,288]{2,1,0:T(1,128)} %reshape.639), calls=%async_computation.3 | async-start | bytes 49152 | tf_op jit(solution)/shard_map/all_to_all | solution.py:153
  152.7 59.1 %all-to-all-start.2 = ((f32[16,9,4096]{2,1,0:T(8,128)}), f32[16,9,4096]{2,1,0:T(8,128)}, u32[]{:S(2)}, u32[]{:S(2)}) async-start(f32[16,9,4096]{2,1,0:T(8,128)} %pad_maximum_fusion), calls=%async_computation.2 | async-start | bytes 8388608 | tf_op jit(solution)/shard_map/all_to_all | solution.py:139
  211.8 18.8 %all-to-all-start.4 = ((f32[16,1,288]{2,1,0:T(1,128)}), f32[16,1,288]{2,1,0:T(1,128)S(1)}, u32[]{:S(2)}, u32[]{:S(2)}) async-start(f32[16,1,288]{2,1,0:T(1,128)} %reshape.645), calls=%async_computation.4 | async-start | bytes 49152 | tf_op jit(solution)/shard_map/all_to_all | solution.py:166
  221.3 1.6 copy-start.8
  221.3 1.9 copy-start.11
  230.6 15.0 %all-to-all-start.6 = ((f32[16,1,288]{2,1,0:T(1,128)}), f32[16,1,288]{2,1,0:T(1,128)}, u32[]{:S(2)}, u32[]{:S(2)}) async-start(f32[16,1,288]{2,1,0:T(1,128)} %reshape.643), calls=%async_computation.6 | async-start | bytes 49152 | tf_op jit(solution)/shard_map/all_to_all | solution.py:167
  237.9 135.9 %all-reduce.7.cloned.1.call-start = ((), (), s32[]{:S(2)}) async-start(), calls=%async_computation.8 | async-start | bytes 13631488 | tf_op jit(solution)/shard_map/psum | solution.py:192
  238.0 19.3 %slice-start = ((s8[7667712]{0:T(1024)(128)(4,1)}), s8[3473408]{0:T(1024)(128)(4,1)S(1)}, s32[]{:S(2)}) async-start(s8[7667712]{0:T(1024)(128)(4,1)} %bitcast.213), calls=%async_computation.9 | async-start | bytes 6946816
  250.6 6.7 %copy-start.10 = (bf16[1,1664,512]{2,1,0:T(8,128)(2,1)S(1)}, bf16[1,1664,512]{2,1,0:T(8,128)(2,1)}, u32[]{:S(2)}) copy-start(bf16[1,1664,512]{2,1,0:T(8,128)(2,1)} %param.9) | copy-start | bytes 5111812
  250.6 6.7 %copy-start.23 = (bf16[18,8,8,128]{3,2,1,0:T(8,128)(2,1)S(1)}, bf16[18,8,8,128]{3,2,1,0:T(8,128)(2,1)}, u32[]{:S(2)}) copy-start(bf16[18,8,8,128]{3,2,1,0:T(8,128)(2,1)} %copy.92) | copy-start | bytes 884740
  252.5 4.8 %slice-start.1 = ((s8[7667712]{0:T(1024)(128)(4,1)}), s8[4194304]{0:T(1024)(128)(4,1)S(1)}, s32[]{:S(2)}) async-start(s8[7667712]{0:T(1024)(128)(4,1)} %bitcast.213), calls=%async_computation.10 | async-start | bytes 8388608
  252.5 8.8 %slice-start.2 = ((s8[7667712]{0:T(1024)(128)(4,1)}), s8[4194304]{0:T(1024)(128)(4,1)S(1)}, s32[]{:S(2)}) async-start(s8[7667712]{0:T(1024)(128)(4,1)} %bitcast.215), calls=%async_computation.11 | async-start | bytes 8388608
  257.3 2.0 copy-start.17
  257.4 3.9 %slice-start.3 = ((s8[7667712]{0:T(1024)(128)(4,1)}), s8[3473408]{0:T(1024)(128)(4,1)S(1)}, s32[]{:S(2)}) async-start(s8[7667712]{0:T(1024)(128)(4,1)} %bitcast.215), calls=%async_computation.12 | async-start | bytes 6946816
  259.3 1.9 copy-start.3
  259.4 1.9 copy-start.22
  261.3 5.5 %slice-start.4 = ((s8[7667712]{0:T(1024)(128)(4,1)}), s8[4194304]{0:T(1024)(128)(4,1)S(1)}, s32[]{:S(2)}) async-start(s8[7667712]{0:T(1024)(128)(4,1)} %bitcast.217), calls=%async_computation.13 | async-start | bytes 8388608
  262.8 2.1 copy-start.13
  262.8 4.0 %slice-start.5 = ((s8[7667712]{0:T(1024)(128)(4,1)}), s8[3473408]{0:T(1024)(128)(4,1)S(1)}, s32[]{:S(2)}) async-start(s8[7667712]{0:T(1024)(128)(4,1)} %bitcast.217), calls=%async_computation.14 | async-start | bytes 6946816
  264.9 1.9 copy-start.4
  264.9 1.9 copy-start.21
  266.8 1.5 copy-start.27
  266.8 5.6 %slice-start.6 = ((s8[7667712]{0:T(1024)(128)(4,1)}), s8[4194304]{0:T(1024)(128)(4,1)S(1)}, s32[]{:S(2)}) async-start(s8[7667712]{0:T(1024)(128)(4,1)} %bitcast.219), calls=%async_computation.15 | async-start | bytes 8388608
  268.3 2.1 copy-start.19
  268.3 4.1 %slice-start.7 = ((s8[7667712]{0:T(1024)(128)(4,1)}), s8[3473408]{0:T(1024)(128)(4,1)S(1)}, s32[]{:S(2)}) async-start(s8[7667712]{0:T(1024)(128)(4,1)} %bitcast.219), calls=%async_computation.16 | async-start | bytes 6946816
  270.4 1.9 copy-start.5
  270.4 1.9 copy-start.20
  272.4 1.5 copy-start.26
  273.9 2.3 copy-start.15
  276.2 1.8 copy-start.6
  282.1 1.5 copy-start.9
  302.6 33.6 %all-to-all-start.7 = ((bf16[16,9,4096]{2,1,0:T(8,128)(2,1)}), bf16[16,9,4096]{2,1,0:T(8,128)(2,1)S(1)}, u32[]{:S(2)}, u32[]{:S(2)}) async-start(bf16[16,9,4096]{2,1,0:T(8,128)(2,1)} %pad_maximum_fusion.3), calls=%async_computation.7 | async-start | bytes 4194304 | tf_op jit(solution)/shard_map/all_to_all | solution.py:182
Sparse Core Ops, SparseCore 0:
  282.3 91.5 all-reduce.6
where the time goes:
time: 392 us; the launch traced here: 386 us
  waiting for transfers between devices  139 us (35%)
  matrix products  72.7 us (19%)
  local copies, waits for them, and re-layouts  68.3 us (17%)
  starting transfers between devices  47.8 us (12%)
  other arithmetic  42.2 us (11%)
  between operations  15.8 us (4%)
    dot_general x24, matrix products, multiply(): jnp.einsum(pattern, left_operand, right_op, preferred_element_type=jnp.fl...  72.7 us
    all_to_all x1, waiting for transfers between devices, local(): lax.all_to_all(part_out.reshape(img_count, item_num, row_width), 'img', s...  47.6 us
    psum x1, waiting for transfers between devices, local(): summed = lax.psum((key_terms, value_terms), 'ctx')  34.9 us
    all_to_all x1, waiting for transfers between devices, local(): lax.all_to_all(query_terms.reshape(img_count, capacity, row_width).astype...  27.5 us
    all_to_all x1, waiting for transfers between devices, local(): lax.all_to_all(sent_rows, 'img', split_axis=0, concat_axis=0, tiled=True)  24.7 us
    unnamed x93, local copies, waits for them, and re-layouts  22.6 us
    reduce_sum x4, other arithmetic, tile_forward(): total_list.append(jnp.sum(weights, axis=3))  17.6 us
  transfers between devices with their start and end apart: 9, of which 6 were waited for; matrix products, arithmetic and copies ran while one was open for 33% of the time, Pallas kernels for 0%

commit v1 on v0

v1 whole, which is shorter than its diff:
```python
import functools
import math

import jax
import jax.numpy as jnp
from jax import lax
from jax.experimental import pallas as pl
from jax.experimental.pallas import tpu as pltpu
from jax.sharding import Mesh, PartitionSpec as P

HEAD_WIDTH = 128
GROUP = 8
CAP = 9
MAIN = 8
F32 = jnp.float32
BF16 = jnp.bfloat16
ROWS_LAST = (((1,), (1,)), ((), ()))


def token_slots(ids, tile_num):
    tokens = ids.shape[0]
    lane = lax.broadcasted_iota(jnp.int32, (tokens, 128), 1)
    chosen = jnp.where(ids == lane, 1.0, 0.0).T
    row = lax.broadcasted_iota(jnp.int32, (tokens, tokens), 0)
    column = lax.broadcasted_iota(jnp.int32, (tokens, tokens), 1)
    earlier = jnp.where(row < column, 1.0, 0.0).astype(BF16)
    before = jnp.dot(chosen.astype(BF16), earlier, preferred_element_type=F32)
    place = jnp.where(chosen > 0.0, before, -1.0).astype(BF16)
    slots = tile_num * CAP
    slot = lax.broadcasted_iota(jnp.int32, (slots, 128), 0)
    ninth = slot >= tile_num * MAIN
    tile = jnp.where(ninth, slot - tile_num * MAIN, slot // MAIN)
    spread = jnp.where(tile == lax.broadcasted_iota(jnp.int32, (slots, 128), 1), 1.0, 0.0)
    held = jnp.dot(spread.astype(BF16), place, preferred_element_type=F32)
    turn = jnp.where(ninth, MAIN, slot % MAIN).astype(F32)
    return jnp.where(held == turn, 1.0, 0.0)


def dispatch_kernel(ids_ref, query_ref, grad_ref, sent_ref, slots_ref, ninth_ref):
    tile_num = sent_ref.shape[0]

    @pl.when(pl.program_id(0) == 0)
    def _():
        slots_ref[...] = token_slots(ids_ref[...], tile_num).astype(BF16)

    for first, source in ((0, query_ref), (HEAD_WIDTH, grad_ref)):
        lanes = slice(first, first + HEAD_WIDTH)
        rows = jnp.dot(slots_ref[...], source[...], preferred_element_type=F32)
        heads = [rows[:, h * HEAD_WIDTH : (h + 1) * HEAD_WIDTH] for h in range(GROUP)]
        for h in range(GROUP):
            ninth_ref[pl.ds(h, tile_num, stride=GROUP), :] = heads[h][tile_num * MAIN :]
        for t in range(tile_num):
            parts = [head[t * MAIN : (t + 1) * MAIN] for head in heads]
            parts.append(ninth_ref[t * GROUP : (t + 1) * GROUP, :])
            sent_ref[t, :, lanes] = jnp.concatenate(parts, axis=0).astype(BF16)


def dispatch(tile_ids, queries, output_gradient, part, tile_num):
    tokens = queries.shape[0]
    width = GROUP * HEAD_WIDTH
    block = pl.BlockSpec((tokens, width), lambda i: (0, 2 * i + part))
    return pl.pallas_call(
        dispatch_kernel,
        grid=(2,),
        in_specs=[pl.BlockSpec((tokens, 1), lambda i: (0, 0)), block, block],
        out_specs=pl.BlockSpec((tile_num, CAP * GROUP, 2 * HEAD_WIDTH), lambda i: (i, 0, 0)),
        out_shape=jax.ShapeDtypeStruct((2 * tile_num, CAP * GROUP, 2 * HEAD_WIDTH), BF16),
        scratch_shapes=[
            pltpu.VMEM((tile_num * CAP, tokens), BF16),
            pltpu.VMEM((tile_num * GROUP, HEAD_WIDTH), F32),
        ],
        compiler_params=pltpu.CompilerParams(vmem_limit_bytes=24 * 2**20),
        cost_estimate=pl.CostEstimate(flops=2 * 10**8, bytes_accessed=3 * 10**6, transcendentals=0),
        name="dispatch",
    )(tile_ids, queries, output_gradient)


def combine_kernel(ids_ref, back_ref, *refs):
    attended_ref, query_grad_ref, slots_ref, ninth_ref = refs[-4:]
    tile_num = back_ref.shape[0]

    @pl.when(pl.program_id(0) == 0)
    def _():
        slots_ref[...] = token_slots(ids_ref[...], tile_num).T.astype(BF16)

    for t in range(tile_num):
        last = back_ref[t, MAIN * GROUP :, :].astype(F32)
        ninth_ref[0, t * GROUP : (t + 1) * GROUP, :] = last[:, :HEAD_WIDTH]
        ninth_ref[1, t * GROUP : (t + 1) * GROUP, :] = last[:, HEAD_WIDTH:]
    for h in range(GROUP):
        lanes = slice(h * HEAD_WIDTH, (h + 1) * HEAD_WIDTH)
        parts = [back_ref[t, h * MAIN : (h + 1) * MAIN, :].astype(F32) for t in range(tile_num)]
        main = jnp.concatenate(parts, axis=0)
        for side, target in ((0, attended_ref), (1, query_grad_ref)):
            ninth = ninth_ref[side, pl.ds(h, tile_num, stride=GROUP), :]
            half = main[:, side * HEAD_WIDTH : (side + 1) * HEAD_WIDTH]
            rows = jnp.concatenate([half, ninth], axis=0).astype(BF16)
            target[:, lanes] = jnp.dot(
                slots_ref[...], rows, preferred_element_type=F32
            ).astype(BF16)


def combine(tile_ids, back, part, earlier, shape):
    tokens = shape[0]
    tile_num = back.shape[0] // 2
    width = GROUP * HEAD_WIDTH
    block = pl.BlockSpec((tokens, width), lambda i: (0, 2 * i + part))
    whole = pl.BlockSpec(memory_space=pl.ANY)
    return pl.pallas_call(
        combine_kernel,
        grid=(2,),
        in_specs=[
            pl.BlockSpec((tokens, 1), lambda i: (0, 0)),
            pl.BlockSpec((tile_num, CAP * GROUP, 2 * HEAD_WIDTH), lambda i: (i, 0, 0)),
        ]
        + [whole] * len(earlier),
        out_specs=[block, block],
        out_shape=[jax.ShapeDtypeStruct(shape, BF16)] * 2,
        scratch_shapes=[
            pltpu.VMEM((tokens, tile_num * CAP), BF16),
            pltpu.VMEM((2, tile_num * GROUP, HEAD_WIDTH), F32),
        ],
        input_output_aliases={2: 0, 3: 1} if earlier else {},
        compiler_params=pltpu.CompilerParams(vmem_limit_bytes=24 * 2**20),
        cost_estimate=pl.CostEstimate(flops=2 * 10**8, bytes_accessed=3 * 10**6, transcendentals=0),
        name="combine",
    )(tile_ids, back, *earlier)


def attend_kernel(
    info, rows_ref, key_ref, value_ref, back_ref, grads_ref,
    query_s, grad_s, out_s, query_grad_s, key_fill, key_zero, value_ones,
    score_s, prob_s, slope_s, key_grad_s, value_grad_s, *, block_rows,
):
    count = info[1]
    device_num, slot_rows, _ = rows_ref.shape
    patches = key_ref.shape[1]
    width = HEAD_WIDTH
    inv_root = 1.0 / math.sqrt(width)
    to_power = math.log2(math.e) * inv_root

    live = lax.broadcasted_iota(jnp.int32, (patches, width), 0) < count
    key, value = key_ref[0].astype(F32), value_ref[0].astype(F32)
    key_fill[...] = jnp.where(live, key, key[0:1, :]).astype(BF16)
    key_zero[...] = jnp.where(live, key, 0.0).astype(BF16)
    value_ones[:, :width] = jnp.where(live, value, 0.0).astype(BF16)
    value_ones[:, width:] = jnp.where(live, 1.0, 0.0).astype(BF16)
    for i in range(0, device_num, 2):
        for first, target in ((0, query_s), (width, grad_s)):
            pair = [rows_ref[i + j, :, first : first + width].astype(F32) for j in range(2)]
            target[i * slot_rows : (i + 2) * slot_rows, :] = jnp.concatenate(pair, axis=0).astype(BF16)
    key_grad_s[...] = jnp.zeros_like(key_grad_s)
    value_grad_s[...] = jnp.zeros_like(value_grad_s)

    @pl.loop(0, query_s.shape[0] // block_rows)
    def _(step):
        here = pl.ds(pl.multiple_of(step * block_rows, block_rows), block_rows)
        query = query_s[here, :]
        score = lax.dot_general(query, key_fill[...], ROWS_LAST, preferred_element_type=F32)
        score_s[...] = score
        peak = jnp.max(score, axis=1, keepdims=True) * to_power
        prob_s[...] = jnp.exp2(score_s[...] * to_power - peak).astype(BF16)
        mixed = jnp.dot(prob_s[...], value_ones[...], preferred_element_type=F32)
        scale = 1.0 / mixed[:, width:]
        attended = (mixed[:, :width] * scale).astype(BF16).astype(F32)
        out_s[here, :] = attended
        grad = (grad_s[here, :].astype(F32) * scale).astype(BF16)
        grad_dot = jnp.sum(grad.astype(F32) * attended, axis=1, keepdims=True)
        prob_grad = lax.dot_general(
            grad, value_ones[:, :width], ROWS_LAST, preferred_element_type=F32
        )
        slope_s[...] = (prob_grad - grad_dot).astype(BF16) * prob_s[...]
        query_grad_s[here, :] = inv_root * jnp.dot(
            slope_s[...], key_zero[...], preferred_element_type=F32
        )
        grad_turned = grad.astype(F32).T.astype(BF16)
        query_turned = query.astype(F32).T.astype(BF16)
        value_grad_s[...] += jnp.dot(grad_turned, prob_s[...], preferred_element_type=F32)
        key_grad_s[...] += jnp.dot(query_turned, slope_s[...], preferred_element_type=F32)

    for i in range(device_num):
        own = slice(i * slot_rows, (i + 1) * slot_rows)
        back_ref[i, :, :width] = out_s[own, :].astype(BF16)
        back_ref[i, :, width:] = query_grad_s[own, :].astype(BF16)
    grads_ref[:, :width] = jnp.where(live, key_grad_s[...].T * inv_root, 0.0).astype(BF16)
    grads_ref[:, width:] = jnp.where(live, value_grad_s[...].T, 0.0).astype(BF16)


def attend(info, rows, keys, values):
    device_num, slot_rows, both = rows.shape
    patches = keys.shape[1]
    total = device_num * slot_rows
    width = HEAD_WIDTH
    block_rows = total // 3
    tile = pl.BlockSpec((1, patches, width), lambda i, info: (0, 0, info[0]))
    whole = pl.BlockSpec(rows.shape, lambda i, info: (0, 0, 0))
    return pl.pallas_call(
        functools.partial(attend_kernel, block_rows=block_rows),
        grid_spec=pltpu.PrefetchScalarGridSpec(
            num_scalar_prefetch=1,
            grid=(1,),
            in_specs=[whole, tile, tile],
            out_specs=[whole, pl.BlockSpec((patches, both), lambda i, info: (0, 0))],
            scratch_shapes=[
                pltpu.VMEM((total, width), BF16),
                pltpu.VMEM((total, width), BF16),
                pltpu.VMEM((total, width), F32),
                pltpu.VMEM((total, width), F32),
                pltpu.VMEM((patches, width), BF16),
                pltpu.VMEM((patches, width), BF16),
                pltpu.VMEM((patches, both), BF16),
                pltpu.VMEM((block_rows, patches), F32),
                pltpu.VMEM((block_rows, patches), BF16),
                pltpu.VMEM((block_rows, patches), BF16),
                pltpu.VMEM((width, patches), F32),
                pltpu.VMEM((width, patches), F32),
            ],
        ),
        out_shape=[
            jax.ShapeDtypeStruct(rows.shape, BF16),
            jax.ShapeDtypeStruct((patches, both), BF16),
        ],
        compiler_params=pltpu.CompilerParams(vmem_limit_bytes=40 * 2**20),
        cost_estimate=pl.CostEstimate(
            flops=12 * total * patches * width,
            bytes_accessed=4 * 10**6,
            transcendentals=total * patches,
        ),
        name="attend",
    )(info, rows, keys, values)


def local(queries, tile_ids, keys, values, patch_counts, output_gradient):
    tile_num = lax.axis_size("img")
    core = lax.axis_index("core")
    exchange = functools.partial(
        lax.all_to_all, axis_name=("core", "img"), split_axis=0, concat_axis=0, tiled=True
    )
    rows = [
        exchange(dispatch(tile_ids, queries, output_gradient, part, tile_num)) for part in range(2)
    ]
    outputs, sums = (), []
    for part in range(2):
        info = jnp.stack([2 * core + part, patch_counts[0]]).astype(jnp.int32)
        back, grads = attend(info, rows[part], keys, values)
        sums.append(lax.psum_scatter(grads, "z", scatter_dimension=0, tiled=True))
        outputs = combine(tile_ids, exchange(back), part, outputs, queries.shape)
    both = jnp.concatenate(sums, axis=1)
    half = both.shape[0] // 2
    mine = lax.dynamic_slice_in_dim(both, core * half, half, 0)
    theirs = lax.dynamic_slice_in_dim(both, (1 - core) * half, half, 0)
    other = lax.ppermute(theirs, "core", [(0, 1), (1, 0)])
    first = jnp.where(core == 0, mine, other).astype(F32)
    second = jnp.where(core == 0, other, mine).astype(F32)
    width = HEAD_WIDTH
    grads = [
        jnp.concatenate([side[:, a : a + width] for side in (first, second) for a in (b, b + 2 * width)], axis=1)[None]
        for b in (0, width)
    ]
    return (*outputs, *grads)


def solution(mesh):
    ctx, img = mesh.devices.shape
    fine = Mesh(mesh.devices.reshape(ctx // 2, 2, img), ("z", "core", "img"))
    rows = P(("z", "core", "img"), None)
    grads = P("img", ("z", "core"), None)
    tiles = P("img", None, None)
    return jax.shard_map(
        local,
        mesh=fine,
        in_specs=(rows, rows, tiles, tiles, P("img"), rows),
        out_specs=(rows, rows, grads, grads),
        check_vma=False,
    )
```

time: 392 us -> 156 us (0.40)
  waiting for transfers between devices: 139 us -> 54.6 us
  matrix products: 72.7 us -> 0 us
  local copies, waits for them, and re-layouts: 68.3 us -> 12.9 us
  Pallas kernels: 0 us -> 46.2 us
  other arithmetic: 42.2 us -> 1.83 us
  starting transfers between devices: 47.8 us -> 22.9 us
    dot_general x24 -> x0, matrix products: 72.7 us -> none  [multiply(): jnp.einsum(pattern, left_operand, right_op, preferred_element_type=jnp.fl...]
    all_to_all x8 -> x4, waiting for transfers between devices: 104 us -> 37.5 us  [the longest x2 37.5 us: local(): exchange(dispatch(tile_ids, queries, output_gradient, part, tile_num))]
    pallas_call x0 -> x6, Pallas kernels: none -> 46.2 us  [the longest x2 37.8 us: attend(): pl.pallas_call(functools.partial(attend_kernel, block_rows=block_rows), g...]
    psum x1 -> x0, waiting for transfers between devices: 34.9 us -> none  [local(): summed = lax.psum((key_terms, value_terms), 'ctx')]
    all_to_all x8 -> x4, starting transfers between devices: 47.8 us -> 22.6 us  [the longest x2 11.3 us: local(): exchange(dispatch(tile_ids, queries, output_gradient, part, tile_num))]
    reduce_sum x5 -> x0, other arithmetic: 18.2 us -> none  [the longest x4 17.6 us: tile_forward(): total_list.append(jnp.sum(weights, axis=3))]
    reduce_scatter x0 -> x2, waiting for transfers between devices: none -> 17.1 us  [local(): sums.append(lax.psum_scatter(grads, 'z', scatter_dimension=0, tiled=True))]
    reshape x12 -> x0, local copies, waits for them, and re-layouts: 13.1 us -> none  [the longest x1 2.63 us: local(): padded_take(output_gradient, index_map)]
  transfers between devices with their start and end apart: 9 -> 7, of which waited for: 6 -> 3; matrix products, arithmetic and copies ran while one was open for 33% -> 1% of each run, Pallas kernels for 0% -> 16%
where the time goes in v1:
time: 156 us; the launch traced here: 153 us
  waiting for transfers between devices  54.6 us (35%)
  Pallas kernels  46.2 us (30%)
  starting transfers between devices  22.9 us (15%)
  between operations  14.8 us (9%)
  local copies, waits for them, and re-layouts  12.9 us (8%)
  other arithmetic  1.83 us (1%)
    pallas_call x2, Pallas kernels, attend(): pl.pallas_call(functools.partial(attend_kernel, block_rows=block_rows), g...  37.8 us
    all_to_all x2, waiting for transfers between devices, local(): exchange(dispatch(tile_ids, queries, output_gradient, part, tile_num))  37.5 us
    reduce_scatter x2, waiting for transfers between devices, local(): sums.append(lax.psum_scatter(grads, 'z', scatter_dimension=0, tiled=True))  17.1 us
    unnamed x22, local copies, waits for them, and re-layouts  11.9 us
    all_to_all x2, starting transfers between devices, local(): exchange(dispatch(tile_ids, queries, output_gradient, part, tile_num))  11.3 us
    all_to_all x2, starting transfers between devices, local(): outputs = combine(tile_ids, exchange(back), part, outputs, queries.shape)  11.3 us
    pallas_call x2, Pallas kernels, combine(): pl.pallas_call(combine_kernel, grid=(2,), in_specs=[pl.BlockSpec((tokens,...  4.42 us
    pallas_call x2, Pallas kernels, dispatch(): pl.pallas_call(dispatch_kernel, grid=(2,), in_specs=[pl.BlockSpec((tokens...  4.02 us
  transfers between devices with their start and end apart: 7, of which 3 were waited for; matrix products, arithmetic and copies ran while one was open for 1% of the time, Pallas kernels for 16%

profile of v1, /device:TPU:0, one launch (start us, length us, event | category | flops | bytes accessed | tf_op | source)
XLA Modules:
  0.0 153.4 jit_solution(9197901232491878831)
XLA Ops:
  7.2 0.8 copy.15.ids_ref
  7.9 0.0 copy-start
  7.9 1.2 copy-done
  9.2 0.0 copy-start.2
  9.2 1.2 copy-done.2
  10.4 2.0 %dispatch.3 = bf16[32,72,256]{2,1,0:T(8,128)(2,1)} custom-call(s32[128,1]{1,0:T(8,128)S(1)} %copy.15.ids_ref, bf16[128,4096]{1,0:T(8,128)(2,1)S(1)} %copy-done, bf16[128,4096]{1,0:T(8,128)(2,1)S(1)} %copy-done.2), custom_call_target="tpu_custom_call" | custom-call | flops 200000000 | bytes 3000000 | tf_op jit(solution)/shard_map/dispatch/pallas_call | solution.py:62
  12.4 7.4 %all-to-all-start.2 = ((bf16[32,72,256]{2,1,0:T(8,128)(2,1)}), bf16[32,72,256]{2,1,0:T(8,128)(2,1)S(1)}, u32[]{:S(2)}, u32[]{:S(2)}) async-start(bf16[32,72,256]{2,1,0:T(8,128)(2,1)} %dispatch.3), calls=%async_computation.2 | async-start | bytes 2359296 | tf_op jit(solution)/shard_map/all_to_all | solution.py:240
  19.8 0.0 reduce-scatter.3.cloned.1.call-start
  20.5 0.1 pad_add_fusion.1.info
  20.6 18.4 %all-to-all-done.2.rows_ref = bf16[32,72,256]{2,1,0:T(8,128)(2,1)S(1)} async-done(((bf16[32,72,256]{2,1,0:T(8,128)(2,1)}), bf16[32,72,256]{2,1,0:T(8,128)(2,1)S(1)}, u32[]{:S(2)}, u32[]{:S(2)}) %all-to-all-start.2) | async-done | bytes 1179680 | tf_op jit(solution)/shard_map/all_to_all | solution.py:240
  39.0 0.0 copy-start.6
  39.0 1.5 copy-done.6
  40.4 0.0 copy-start.8
  40.4 1.5 copy-done.8
  41.9 0.0 copy-start.1
  41.9 0.0 copy-start.3
  41.9 19.0 %attend.3 = (bf16[32,72,256]{2,1,0:T(8,128)(2,1)}, bf16[1664,256]{1,0:T(8,128)(2,1)S(1)}) custom-call(s32[2]{0:T(128)S(1)} %pad_add_fusion.1.info, bf16[32,72,256]{2,1,0:T(8,128)(2,1)S(1)} %all-to-all-done.2.rows_ref, bf16[1,1664,512]{2,1,0:T(8,128)(2,1)S(1)} %copy-done.6, bf16[1,1664,512]{2,1,0:T(8,128)(2,1)S(1)} %copy-done.8), custom_call_target="tpu_custom_call" | custom-call | flops 5888802816 | bytes 4000000 | tf_op jit(solution)/shard_map/attend/pallas_call | solution.py:197
  60.9 0.0 copy-start.5
  60.9 0.9 copy-done.5
  61.8 0.0 reduce-scatter.3.cloned.1.call-update
  61.8 0.0 copy-done.1
  61.8 0.0 copy-done.3
  61.9 2.0 %dispatch.2 = bf16[32,72,256]{2,1,0:T(8,128)(2,1)} custom-call(s32[128,1]{1,0:T(8,128)S(1)} %copy.15.ids_ref, bf16[128,4096]{1,0:T(8,128)(2,1)S(1)} %copy-done.1, bf16[128,4096]{1,0:T(8,128)(2,1)S(1)} %copy-done.3), custom_call_target="tpu_custom_call" | custom-call | flops 200000000 | bytes 3000000 | tf_op jit(solution)/shard_map/dispatch/pallas_call | solution.py:62
  63.9 3.9 %all-to-all-start = ((bf16[32,72,256]{2,1,0:T(8,128)(2,1)}), bf16[32,72,256]{2,1,0:T(8,128)(2,1)S(1)}, u32[]{:S(2)}, u32[]{:S(2)}) async-start(bf16[32,72,256]{2,1,0:T(8,128)(2,1)} %dispatch.2), calls=%async_computation | async-start | bytes 2359296 | tf_op jit(solution)/shard_map/all_to_all | solution.py:240
  67.8 0.1 pad_add_fusion.info
  67.9 19.1 %all-to-all-done.rows_ref = bf16[32,72,256]{2,1,0:T(8,128)(2,1)S(1)} async-done(((bf16[32,72,256]{2,1,0:T(8,128)(2,1)}), bf16[32,72,256]{2,1,0:T(8,128)(2,1)S(1)}, u32[]{:S(2)}, u32[]{:S(2)}) %all-to-all-start) | async-done | bytes 1179680 | tf_op jit(solution)/shard_map/all_to_all | solution.py:240
  87.0 3.9 %all-to-all-start.3 = ((bf16[32,72,256]{2,1,0:T(8,128)(2,1)}), bf16[32,72,256]{2,1,0:T(8,128)(2,1)S(1)}, u32[]{:S(2)}, u32[]{:S(2)}) async-start(bf16[32,72,256]{2,1,0:T(8,128)(2,1)} %get-tuple-element.13), calls=%async_computation.3 | async-start | bytes 2359296 | tf_op jit(solution)/shard_map/all_to_all | solution.py:247
  90.9 0.2 reduce-scatter.5.cloned.1.call-start
  91.2 0.0 copy-start.7
  91.2 1.4 copy-done.7
  92.6 0.0 copy-start.9
  92.6 1.5 copy-done.9
  94.1 18.8 %attend.2 = (bf16[32,72,256]{2,1,0:T(8,128)(2,1)S(1)}, bf16[1664,256]{1,0:T(8,128)(2,1)}) custom-call(s32[2]{0:T(128)S(1)} %pad_add_fusion.info, bf16[32,72,256]{2,1,0:T(8,128)(2,1)S(1)} %all-to-all-done.rows_ref, bf16[1,1664,512]{2,1,0:T(8,128)(2,1)S(1)} %copy-done.7, bf16[1,1664,512]{2,1,0:T(8,128)(2,1)S(1)} %copy-done.9), custom_call_target="tpu_custom_call" | custom-call | flops 5888802816 | bytes 4000000 | tf_op jit(solution)/shard_map/attend/pallas_call | solution.py:197
  112.8 0.0 copy-start.4
  112.8 1.0 copy-done.4
  113.8 0.0 reduce-scatter.5.cloned.1.call-update
  113.9 0.0 all-to-all-done.3.back_ref
  113.9 7.3 %all-to-all-start.1 = ((bf16[32,72,256]{2,1,0:T(8,128)(2,1)}), bf16[32,72,256]{2,1,0:T(8,128)(2,1)S(1)}, u32[]{:S(2)}, u32[]{:S(2)}) async-start(bf16[32,72,256]{2,1,0:T(8,128)(2,1)} %copy-done.4), calls=%async_computation.1 | async-start | bytes 2359296 | tf_op jit(solution)/shard_map/all_to_all | solution.py:247
  121.2 0.0 reduce-scatter.3.cloned.1.call-done
  121.2 0.9 constant_dynamic-update-slice_fusion.1
  122.2 17.1 %reduce-scatter.5.cloned.1.call-done = bf16[416,256]{1,0:T(8,128)(2,1)} async-done(((bf16[1664,256]{1,0:T(8,128)(2,1)}), bf16[416,256]{1,0:T(8,128)(2,1)}) %reduce-scatter.5.cloned.1.call-update) | async-done | bytes 213008 | tf_op jit(solution)/shard_map/reduce_scatter | solution.py:246
  139.3 0.9 constant_dynamic-update-slice_fusion
  140.3 0.1 collective-permute-start
  140.4 2.2 %combine.2 = (bf16[128,4096]{1,0:T(8,128)(2,1)}, bf16[128,4096]{1,0:T(8,128)(2,1)}) custom-call(s32[128,1]{1,0:T(8,128)S(1)} %copy.15.ids_ref, bf16[32,72,256]{2,1,0:T(8,128)(2,1)S(1)} %all-to-all-done.3.back_ref), custom_call_target="tpu_custom_call" | custom-call | flops 200000000 | bytes 3000000 | tf_op jit(solution)/shard_map/combine/pallas_call | solution.py:109
  142.6 0.0 all-to-all-done.1.back_ref
  142.6 2.2 %combine.3 = (bf16[128,4096]{1,0:T(8,128)(2,1)}, bf16[128,4096]{1,0:T(8,128)(2,1)}) custom-call(s32[128,1]{1,0:T(8,128)S(1)} %copy.15.ids_ref, bf16[32,72,256]{2,1,0:T(8,128)(2,1)S(1)} %all-to-all-done.1.back_ref, bf16[128,4096]{1,0:T(8,128)(2,1)} %get-tuple-element.14.refs_0_, ...), custom_call_target="tpu_custom_call", output_to_operand_aliasing={{0}: (2, {}), {1}: (3, {})} | custom-call | flops 200000000 | bytes 3000000 | tf_op jit(solution)/shard_map/combine/pallas_call | solution.py:109
  144.8 0.0 collective-permute-done
  144.8 0.1 select_convert_fusion.1
  144.9 0.1 fusion
  145.0 0.8 maximum_bitcast_fusion.1
  145.8 0.8 maximum_bitcast_fusion
  (1 shorter events, 0.0 us)
Async XLA Ops:
  7.9 1.2 copy-start
  9.2 1.2 copy-start.2
  12.4 26.6 %all-to-all-start.2 = ((bf16[32,72,256]{2,1,0:T(8,128)(2,1)}), bf16[32,72,256]{2,1,0:T(8,128)(2,1)S(1)}, u32[]{:S(2)}, u32[]{:S(2)}) async-start(bf16[32,72,256]{2,1,0:T(8,128)(2,1)} %dispatch.3), calls=%async_computation.2 | async-start | bytes 2359296 | tf_op jit(solution)/shard_map/all_to_all | solution.py:240
  19.8 101.4 %reduce-scatter.3.cloned.1.call-start = ((), (), s32[]{:S(2)}) async-start(), calls=%async_computation.6 | async-start | bytes 1064960 | tf_op jit(solution)/shard_map/reduce_scatter | solution.py:246
  39.0 1.5 copy-start.6
  40.4 1.5 copy-start.8
  41.9 20.0 %copy-start.1 = (bf16[128,4096]{1,0:T(8,128)(2,1)S(1)}, bf16[128,4096]{1,0:T(8,128)(2,1)}, u32[]{:S(2)}) copy-start(bf16[128,4096]{1,0:T(8,128)(2,1)} %query_ref.3) | copy-start | bytes 3145732
  41.9 20.0 %copy-start.3 = (bf16[128,4096]{1,0:T(8,128)(2,1)S(1)}, bf16[128,4096]{1,0:T(8,128)(2,1)}, u32[]{:S(2)}) copy-start(bf16[128,4096]{1,0:T(8,128)(2,1)} %grad_ref.3) | copy-start | bytes 3145732
  60.9 0.9 copy-start.5
  63.9 23.1 %all-to-all-start = ((bf16[32,72,256]{2,1,0:T(8,128)(2,1)}), bf16[32,72,256]{2,1,0:T(8,128)(2,1)S(1)}, u32[]{:S(2)}, u32[]{:S(2)}) async-start(bf16[32,72,256]{2,1,0:T(8,128)(2,1)} %dispatch.2), calls=%async_computation | async-start | bytes 2359296 | tf_op jit(solution)/shard_map/all_to_all | solution.py:240
  87.0 26.9 %all-to-all-start.3 = ((bf16[32,72,256]{2,1,0:T(8,128)(2,1)}), bf16[32,72,256]{2,1,0:T(8,128)(2,1)S(1)}, u32[]{:S(2)}, u32[]{:S(2)}) async-start(bf16[32,72,256]{2,1,0:T(8,128)(2,1)} %get-tuple-element.13), calls=%async_computation.3 | async-start | bytes 2359296 | tf_op jit(solution)/shard_map/all_to_all | solution.py:247
  90.9 48.4 %reduce-scatter.5.cloned.1.call-start = ((), (), s32[]{:S(2)}) async-start(), calls=%async_computation.7 | async-start | bytes 1064960 | tf_op jit(solution)/shard_map/reduce_scatter | solution.py:246
  91.2 1.5 copy-start.7
  92.6 1.5 copy-start.9
  112.8 1.0 copy-start.4
  113.9 28.7 %all-to-all-start.1 = ((bf16[32,72,256]{2,1,0:T(8,128)(2,1)}), bf16[32,72,256]{2,1,0:T(8,128)(2,1)S(1)}, u32[]{:S(2)}, u32[]{:S(2)}) async-start(bf16[32,72,256]{2,1,0:T(8,128)(2,1)} %copy-done.4), calls=%async_computation.1 | async-start | bytes 2359296 | tf_op jit(solution)/shard_map/all_to_all | solution.py:247
  140.3 4.5 %collective-permute-start = (bf16[208,512]{1,0:T(8,128)(2,1)S(1)}, bf16[208,512]{1,0:T(8,128)(2,1)S(1)}, u32[]{:S(2)}, u32[]{:S(2)}) collective-permute-start(bf16[208,512]{1,0:T(8,128)(2,1)S(1)} %constant_dynamic-slice_fusion), channel_id=1, source_target_pairs={{0,16},{16,0},{1,17},{17,1},{2,18},{18,2},{3,19},{19,3},{4,20},{20... | collective-permute-start | bytes 638984 | tf_op jit(solution)/shard_map/ppermute | solution.py:252
Sparse Core Ops, SparseCore 0:
  62.0 21.1 reduce-scatter.2
  114.0 25.2 reduce-scatter.4

commit v2 on v1

v2 whole, which is shorter than its diff:
```python
import functools
import math

import jax
import jax.numpy as jnp
from jax import lax
from jax.experimental import pallas as pl
from jax.experimental.pallas import tpu as pltpu
from jax.sharding import Mesh, PartitionSpec as P

HEAD_WIDTH = 128
GROUP = 8
CAP = 9
MAIN = 8
F32 = jnp.float32
BF16 = jnp.bfloat16
ROWS_LAST = (((1,), (1,)), ((), ()))
LIMIT = 60 * 2**20
WAYS = 9


def token_slots(ids, tile_num):
    tokens = ids.shape[1]
    chosen = jnp.where(ids == lax.broadcasted_iota(jnp.int32, (128, tokens), 0), 1.0, 0.0)
    row = lax.broadcasted_iota(jnp.int32, (tokens, tokens), 0)
    column = lax.broadcasted_iota(jnp.int32, (tokens, tokens), 1)
    earlier = jnp.where(row < column, 1.0, 0.0).astype(BF16)
    before = jnp.dot(chosen.astype(BF16), earlier, preferred_element_type=F32)
    place = jnp.where(chosen > 0.0, before, -1.0).astype(BF16)
    slots = tile_num * CAP
    slot = lax.broadcasted_iota(jnp.int32, (slots, 128), 0)
    ninth = slot >= tile_num * MAIN
    tile = jnp.where(ninth, slot - tile_num * MAIN, slot // MAIN)
    spread = jnp.where(tile == lax.broadcasted_iota(jnp.int32, (slots, 128), 1), 1.0, 0.0)
    held = jnp.dot(spread.astype(BF16), place, preferred_element_type=F32)
    turn = jnp.where(ninth, MAIN, slot % MAIN).astype(F32)
    return jnp.where(held == turn, 1.0, 0.0)


def route_kernel(ids_ref, query_ref, grad_ref, sent_ref, slots_ref, turned_ref, ninth_ref):
    @pl.when(pl.program_id(0) == 0)
    def _():
        slots = token_slots(ids_ref[...], sent_ref.shape[0])
        slots_ref[...] = slots.astype(BF16)
        turned_ref[...] = slots.T.astype(BF16)

    dispatch_kernel(slots_ref, query_ref, grad_ref, sent_ref, ninth_ref)


def dispatch_kernel(slots_ref, query_ref, grad_ref, sent_ref, ninth_ref):
    tile_num = sent_ref.shape[0]
    for first, source in ((0, query_ref), (HEAD_WIDTH, grad_ref)):
        lanes = slice(first, first + HEAD_WIDTH)
        rows = jnp.dot(slots_ref[...], source[...], preferred_element_type=F32)
        heads = [rows[:, h * HEAD_WIDTH : (h + 1) * HEAD_WIDTH] for h in range(GROUP)]
        for h in range(GROUP):
            ninth_ref[pl.ds(h, tile_num, stride=GROUP), :] = heads[h][tile_num * MAIN :]
        for t in range(tile_num):
            parts = [head[t * MAIN : (t + 1) * MAIN] for head in heads]
            parts.append(ninth_ref[t * GROUP : (t + 1) * GROUP, :])
            sent_ref[t, :, lanes] = jnp.concatenate(parts, axis=0).astype(BF16)


def dispatch(routing, queries, output_gradient, part, tile_num):
    tokens = queries.shape[0]
    width = GROUP * HEAD_WIDTH
    block = pl.BlockSpec((tokens, width), lambda i: (0, 2 * i + part))
    fixed = lambda shape: pl.BlockSpec(shape, lambda i: (0, 0))
    out_specs = [pl.BlockSpec((tile_num, CAP * GROUP, 2 * HEAD_WIDTH), lambda i: (i, 0, 0))]
    out_shape = [jax.ShapeDtypeStruct((2 * tile_num, CAP * GROUP, 2 * HEAD_WIDTH), BF16)]
    if part == 0:
        for shape in ((tile_num * CAP, tokens), (tokens, tile_num * CAP)):
            out_specs.append(fixed(shape))
            out_shape.append(jax.ShapeDtypeStruct(shape, BF16))
    return pl.pallas_call(
        route_kernel if part == 0 else dispatch_kernel,
        grid=(2,),
        in_specs=[fixed(routing.shape), block, block],
        out_specs=out_specs,
        out_shape=out_shape,
        scratch_shapes=[pltpu.VMEM((tile_num * GROUP, HEAD_WIDTH), F32)],
        compiler_params=pltpu.CompilerParams(vmem_limit_bytes=LIMIT),
        cost_estimate=pl.CostEstimate(flops=10**9, bytes_accessed=3 * 10**6, transcendentals=0),
        name="dispatch",
    )(routing, queries, output_gradient)


def combine_kernel(turned_ref, back_ref, *refs):
    attended_ref, query_grad_ref, ninth_ref = refs[-3:]
    tile_num = back_ref.shape[0]
    for t in range(tile_num):
        last = back_ref[t, MAIN * GROUP :, :].astype(F32)
        ninth_ref[0, t * GROUP : (t + 1) * GROUP, :] = last[:, :HEAD_WIDTH]
        ninth_ref[1, t * GROUP : (t + 1) * GROUP, :] = last[:, HEAD_WIDTH:]
    for h in range(GROUP):
        lanes = slice(h * HEAD_WIDTH, (h + 1) * HEAD_WIDTH)
        parts = [back_ref[t, h * MAIN : (h + 1) * MAIN, :].astype(F32) for t in range(tile_num)]
        main = jnp.concatenate(parts, axis=0)
        for side, target in ((0, attended_ref), (1, query_grad_ref)):
            ninth = ninth_ref[side, pl.ds(h, tile_num, stride=GROUP), :]
            half = main[:, side * HEAD_WIDTH : (side + 1) * HEAD_WIDTH]
            rows = jnp.concatenate([half, ninth], axis=0).astype(BF16)
            target[:, lanes] = jnp.dot(
                turned_ref[...], rows, preferred_element_type=F32
            ).astype(BF16)


def combine(turned, back, part, earlier, shape):
    tokens = shape[0]
    tile_num = back.shape[0] // 2
    width = GROUP * HEAD_WIDTH
    block = pl.BlockSpec((tokens, width), lambda i: (0, 2 * i + part))
    whole = pl.BlockSpec(memory_space=pl.ANY)
    return pl.pallas_call(
        combine_kernel,
        grid=(2,),
        in_specs=[
            pl.BlockSpec(turned.shape, lambda i: (0, 0)),
            pl.BlockSpec((tile_num, CAP * GROUP, 2 * HEAD_WIDTH), lambda i: (i, 0, 0)),
        ]
        + [whole] * len(earlier),
        out_specs=[block, block],
        out_shape=[jax.ShapeDtypeStruct(shape, BF16)] * 2,
        scratch_shapes=[pltpu.VMEM((2, tile_num * GROUP, HEAD_WIDTH), F32)],
        input_output_aliases={2: 0, 3: 1} if earlier else {},
        compiler_params=pltpu.CompilerParams(vmem_limit_bytes=LIMIT),
        cost_estimate=pl.CostEstimate(flops=10**9, bytes_accessed=3 * 10**6, transcendentals=0),
        name="combine",
    )(turned, back, *earlier)


def attend_kernel(info, rows_ref, key_ref, value_ref, back_ref, *refs, ways):
    scratch = refs[-(10 + 3 * ways) :]
    shares = refs[: -len(scratch)]
    query_s, grad_s, out_s, query_grad_s, key_fill, key_zero, value_ones = scratch[:7]
    key_grad_s, value_grad_s, grads_s = scratch[7:10]
    score_s, prob_s, slope_s = (scratch[10 + i * ways : 10 + (i + 1) * ways] for i in range(3))
    device_num, slot_rows, _ = rows_ref.shape
    patches = key_ref.shape[1]
    width = HEAD_WIDTH
    block_rows = query_s.shape[0] // ways
    inv_root = 1.0 / math.sqrt(width)
    to_power = math.log2(math.e) * inv_root

    live = lax.broadcasted_iota(jnp.int32, (patches, width), 0) < info[2]
    key, value = key_ref[0].astype(F32), value_ref[0].astype(F32)
    key_fill[...] = jnp.where(live, key, key[0:1, :]).astype(BF16)
    key_zero[...] = jnp.where(live, key, 0.0).astype(BF16)
    value_ones[:, :width] = jnp.where(live, value, 0.0).astype(BF16)
    value_ones[:, width:] = jnp.where(live, 1.0, 0.0).astype(BF16)
    for i in range(0, device_num, 2):
        for first, target in ((0, query_s), (width, grad_s)):
            pair = [rows_ref[i + j, :, first : first + width].astype(F32) for j in range(2)]
            target[i * slot_rows : (i + 2) * slot_rows, :] = jnp.concatenate(pair, axis=0).astype(BF16)
    key_grad_s[...] = jnp.zeros_like(key_grad_s)
    value_grad_s[...] = jnp.zeros_like(value_grad_s)

    here = [slice(w * block_rows, (w + 1) * block_rows) for w in range(ways)]
    peak, grad, grad_dot = {}, {}, {}

    def scores(w):
        score = lax.dot_general(
            query_s[here[w], :], key_fill[...], ROWS_LAST, preferred_element_type=F32
        )
        score_s[w][...] = score
        peak[w] = jnp.max(score, axis=1, keepdims=True) * to_power

    def weights(w):
        prob_s[w][...] = jnp.exp2(score_s[w][...] * to_power - peak[w]).astype(BF16)

    def output(w):
        mixed = jnp.dot(prob_s[w][...], value_ones[...], preferred_element_type=F32)
        scale = 1.0 / mixed[:, width:]
        attended = (mixed[:, :width] * scale).astype(BF16).astype(F32)
        out_s[here[w], :] = attended
        grad[w] = (grad_s[here[w], :].astype(F32) * scale).astype(BF16)
        grad_dot[w] = jnp.sum(grad[w].astype(F32) * attended, axis=1, keepdims=True)

    def slopes(w):
        prob_grad = lax.dot_general(
            grad[w], value_ones[:, :width], ROWS_LAST, preferred_element_type=F32
        )
        slope_s[w][...] = (prob_grad - grad_dot[w]).astype(BF16) * prob_s[w][...]

    def value_term(w):
        turned = grad[w].astype(F32).T.astype(BF16)
        value_grad_s[...] += jnp.dot(turned, prob_s[w][...], preferred_element_type=F32)

    def query_term(w):
        query_grad_s[here[w], :] = inv_root * jnp.dot(
            slope_s[w][...], key_zero[...], preferred_element_type=F32
        )

    def key_term(w):
        turned = query_s[here[w], :].astype(F32).T.astype(BF16)
        key_grad_s[...] += jnp.dot(turned, slope_s[w][...], preferred_element_type=F32)

    steps = (scores, weights, output, slopes, value_term, query_term, key_term)
    for now in range(len(steps) + ways - 1):
        for w in range(ways):
            if 0 <= now - w < len(steps):
                steps[now - w](w)

    for i in range(device_num):
        own = slice(i * slot_rows, (i + 1) * slot_rows)
        back_ref[i, :, :width] = out_s[own, :].astype(BF16)
        back_ref[i, :, width:] = query_grad_s[own, :].astype(BF16)
    live = lax.broadcasted_iota(jnp.int32, (width, patches), 1) < info[2]
    key_grad_s[...] = jnp.where(live, key_grad_s[...] * inv_root, 0.0)
    value_grad_s[...] = jnp.where(live, value_grad_s[...], 0.0)
    grads_s[:, :width] = key_grad_s[...].T
    grads_s[:, width:] = value_grad_s[...].T
    for i, share in enumerate(shares):
        part = lax.rem(info[1] + i, len(shares))
        size = share.shape[0]
        share[...] = grads_s[pl.ds(pl.multiple_of(part * size, size), size), :].astype(BF16)


def attend(info, rows, keys, values, part, share_num):
    device_num, slot_rows, both = rows.shape
    patches = keys.shape[1]
    total = device_num * slot_rows
    width = HEAD_WIDTH
    share = patches // share_num
    ways = WAYS
    block_rows = total // ways
    tile = pl.BlockSpec((1, patches, width), lambda i, info: (0, 0, 2 * info[0] + part))
    whole = pl.BlockSpec(rows.shape, lambda i, info: (0, 0, 0))
    return pl.pallas_call(
        functools.partial(attend_kernel, ways=ways),
        grid_spec=pltpu.PrefetchScalarGridSpec(
            num_scalar_prefetch=1,
            grid=(1,),
            in_specs=[whole, tile, tile],
            out_specs=[whole] + [pl.BlockSpec((share, both), lambda i, info: (0, 0))] * share_num,
            scratch_shapes=[
                pltpu.VMEM((total, width), BF16),
                pltpu.VMEM((total, width), BF16),
                pltpu.VMEM((total, width), F32),
                pltpu.VMEM((total, width), F32),
                pltpu.VMEM((patches, width), BF16),
                pltpu.VMEM((patches, width), BF16),
                pltpu.VMEM((patches, both), BF16),
                pltpu.VMEM((width, patches), F32),
                pltpu.VMEM((width, patches), F32),
                pltpu.VMEM((patches, both), F32),
            ]
            + [pltpu.VMEM((block_rows, patches), F32)] * ways
            + [pltpu.VMEM((block_rows, patches), BF16)] * (2 * ways),
        ),
        out_shape=[jax.ShapeDtypeStruct(rows.shape, BF16)]
        + [jax.ShapeDtypeStruct((share, both), BF16)] * share_num,
        compiler_params=pltpu.CompilerParams(vmem_limit_bytes=LIMIT),
        cost_estimate=pl.CostEstimate(
            flops=60 * total * patches * width,
            bytes_accessed=4 * 10**6,
            transcendentals=total * patches,
        ),
        name="attend",
    )(info, rows, keys, values)


def add_kernel(info, *refs):
    shares, (mine_ref, theirs_ref) = refs[:-2], refs[-2:]
    half, both = mine_ref.shape[0], shares[0].shape[1]
    for part in range(2):
        of_part = shares[part * len(shares) // 2 : (part + 1) * len(shares) // 2]
        lanes = slice(part * both, (part + 1) * both)
        for target, core in ((mine_ref, info[0]), (theirs_ref, 1 - info[0])):
            rows = pl.ds(pl.multiple_of(core * half, half), half)
            total = sum(share[rows, :].astype(F32) for share in of_part)
            target[:, lanes] = total.astype(target.dtype)


def add_shares(info, shares):
    rows, both = shares[0].shape
    half = rows // 2
    return pl.pallas_call(
        add_kernel,
        grid_spec=pltpu.PrefetchScalarGridSpec(
            num_scalar_prefetch=1,
            grid=(1,),
            in_specs=[pl.BlockSpec((rows, both), lambda i, info: (0, 0))] * len(shares),
            out_specs=[pl.BlockSpec((half, 2 * both), lambda i, info: (0, 0))] * 2,
        ),
        out_shape=[
            jax.ShapeDtypeStruct((half, 2 * both), F32),
            jax.ShapeDtypeStruct((half, 2 * both), BF16),
        ],
        compiler_params=pltpu.CompilerParams(vmem_limit_bytes=LIMIT),
        cost_estimate=pl.CostEstimate(flops=10**8, bytes_accessed=10**6, transcendentals=0),
        name="add_shares",
    )(info, *shares)


def local(queries, tile_ids, keys, values, patch_counts, output_gradient):
    tile_num = lax.axis_size("img")
    depth = lax.axis_size("z")
    info = jnp.stack([lax.axis_index("core"), lax.axis_index("z"), patch_counts[0]]).astype(jnp.int32)
    exchange = functools.partial(
        lax.all_to_all, axis_name=("core", "img"), split_axis=0, concat_axis=0, tiled=True
    )
    ids = tile_ids.reshape(1, -1)
    sent, slots, turned = dispatch(ids, queries, output_gradient, 0, tile_num)
    (later,) = dispatch(slots, queries, output_gradient, 1, tile_num)
    rows, later = lax.optimization_barrier((exchange(sent), later))
    rows = [rows, exchange(later)]
    along_z = lambda shares: [
        lax.ppermute(shares[s], "z", [(i, (i + s) % depth) for i in range(depth)])
        for s in range(1, depth)
    ]
    back, own, *shares = attend(info, rows[0], keys, values, 0, depth)
    sums = [own, *along_z([own, *shares])]
    first_back = exchange(back)
    back, own, *shares = attend(info, rows[1], keys, values, 1, depth)
    back, sums = lax.optimization_barrier((back, sums))
    second_back = exchange(back)
    outputs = combine(turned, first_back, 0, (), queries.shape)
    sums = sums + [own, *along_z([own, *shares])]
    sums, outputs = lax.optimization_barrier((sums, outputs))
    mine, given = add_shares(info, sums)
    other = lax.ppermute(given, "core", [(0, 1), (1, 0)]).astype(F32)
    outputs = combine(turned, second_back, 1, outputs, queries.shape)
    core = lax.axis_index("core")
    sides = (jnp.where(core == 0, mine, other), jnp.where(core == 0, other, mine))
    width = HEAD_WIDTH
    grads = [
        jnp.concatenate(
            [side[:, a : a + width] for side in sides for a in (first, first + 2 * width)], axis=1
        )[None]
        for first in (0, width)
    ]
    return (*outputs, *grads)


def solution(mesh):
    ctx, img = mesh.devices.shape
    fine = Mesh(mesh.devices.reshape(ctx // 2, 2, img), ("z", "core", "img"))
    rows = P(("z", "core", "img"), None)
    grads = P("img", ("z", "core"), None)
    tiles = P("img", None, None)
    return jax.shard_map(
        local,
        mesh=fine,
        in_specs=(rows, rows, tiles, tiles, P("img"), rows),
        out_specs=(rows, rows, grads, grads),
        check_vma=False,
    )
```

time: 156 us -> 115 us (0.74); the launches traced: 153 us -> 115 us
  waiting for transfers between devices: 54.6 us -> 24.8 us
  starting transfers between devices: 22.9 us -> 36.5 us
  between operations: 14.8 us -> 1.43 us
  local copies, waits for them, and re-layouts: 12.9 us -> 3.61 us
    reduce_scatter x2 -> x0, waiting for transfers between devices: 17.1 us -> none  [local(): sums.append(lax.psum_scatter(grads, 'z', scatter_dimension=0, tiled=True))]
    all_to_all x4, waiting for transfers between devices: 37.5 us -> 23.4 us  [the longest x1 15.4 us: local(): rows, later = lax.optimization_barrier((exchange(sent), later))]
    ppermute x1 -> x7, starting transfers between devices: 0.09 us -> 10.5 us  [the longest x6 10.2 us: local(): lax.ppermute(shares[s], 'z', [(i, (i + s) % depth) for i in range(depth)])]
    unnamed x22 -> x20, local copies, waits for them, and re-layouts: 11.9 us -> 3.56 us
    all_to_all x4, starting transfers between devices: 22.6 us -> 26 us  [the longest x1 7.41 us: local(): rows, later = lax.optimization_barrier((exchange(sent), later))]
    pallas_call x6 -> x7, Pallas kernels: 46.2 us -> 45 us  [the longest x2 30.9 us: attend(): pl.pallas_call(functools.partial(attend_kernel, ways=ways), grid_spec=plt...]
  transfers between devices with their start and end apart: 7 -> 11, of which waited for: 3 -> 3; matrix products, arithmetic and copies ran while one was open for 1% -> 3% of each run, Pallas kernels for 16% -> 34%
where the time goes in v2:
time: 115 us
  Pallas kernels  45 us (39%)
  starting transfers between devices  36.5 us (32%)
  waiting for transfers between devices  24.8 us (22%)
  local copies, waits for them, and re-layouts  3.61 us (3%)
  other arithmetic  3.26 us (3%)
  between operations  1.43 us (1%)
    pallas_call x2, Pallas kernels, attend(): pl.pallas_call(functools.partial(attend_kernel, ways=ways), grid_spec=plt...  30.9 us
    all_to_all x1, waiting for transfers between devices, local(): rows, later = lax.optimization_barrier((exchange(sent), later))  15.4 us
    ppermute x6, starting transfers between devices, local(): lax.ppermute(shares[s], 'z', [(i, (i + s) % depth) for i in range(depth)])  10.2 us
    all_to_all x1, waiting for transfers between devices, local(): second_back = exchange(back)  8 us
    all_to_all x1, starting transfers between devices, local(): rows, later = lax.optimization_barrier((exchange(sent), later))  7.41 us
    all_to_all x1, starting transfers between devices, local(): second_back = exchange(back)  7.37 us
    all_to_all x1, starting transfers between devices, local(): first_back = exchange(back)  7.31 us
    pallas_call x2, Pallas kernels, dispatch(): pl.pallas_call(route_kernel if part == 0 else dispatch_kernel, grid=(2,),...  5.49 us
  transfers between devices with their start and end apart: 11, of which 3 were waited for; matrix products, arithmetic and copies ran while one was open for 3% of the time, Pallas kernels for 34%

profile of v2, /device:TPU:0, one launch (start us, length us, event | category | flops | bytes accessed | tf_op | source)
XLA Modules:
  0.0 114.7 jit_solution(1354007206108535282)
XLA Ops:
  0.6 3.0 %dispatch.2 = (bf16[32,72,256]{2,1,0:T(8,128)(2,1)}, bf16[144,128]{1,0:T(8,128)(2,1)}, bf16[128,144]{1,0:T(8,128)(2,1)}) custom-call(s32[1,128]{1,0:T(1,128)} %bitcast.7, bf16[128,4096]{1,0:T(8,128)(2,1)} %query_ref.3, bf16[128,4096]{1,0:T(8,128)(2,1)} %grad_ref.3), custom_call_target="tpu_custom_call" | custom-call | flops 1000000000 | bytes 3000000 | tf_op jit(solution)/shard_map/dispatch/pallas_call | solution.py:75
  3.6 7.4 %all-to-all-start = ((bf16[32,72,256]{2,1,0:T(8,128)(2,1)}), bf16[32,72,256]{2,1,0:T(8,128)(2,1)S(1)}, u32[]{:S(2)}, u32[]{:S(2)}) async-start(bf16[32,72,256]{2,1,0:T(8,128)(2,1)} %get-tuple-element.41), calls=%async_computation | async-start | bytes 2359296 | tf_op jit(solution)/shard_map/all_to_all | solution.py:306
  11.7 2.5 %dispatch.3 = bf16[32,72,256]{2,1,0:T(8,128)(2,1)} custom-call(bf16[144,128]{1,0:T(8,128)(2,1)} %get-tuple-element.42.slots_ref, bf16[128,4096]{1,0:T(8,128)(2,1)} %query_ref.3, bf16[128,4096]{1,0:T(8,128)(2,1)} %grad_ref.3), custom_call_target="tpu_custom_call" | custom-call | flops 1000000000 | bytes 3000000 | tf_op jit(solution)/shard_map/dispatch/pallas_call | solution.py:75
  14.2 0.6 pad_add_fusion.info
  14.8 15.4 %all-to-all-done.rows_ref = bf16[32,72,256]{2,1,0:T(8,128)(2,1)S(1)} async-done(((bf16[32,72,256]{2,1,0:T(8,128)(2,1)}), bf16[32,72,256]{2,1,0:T(8,128)(2,1)S(1)}, u32[]{:S(2)}, u32[]{:S(2)}) %all-to-all-start) | async-done | bytes 1179680 | tf_op jit(solution)/shard_map/all_to_all | solution.py:306
  30.2 0.0 copy-start.2
  30.2 3.9 %all-to-all-start.1 = ((bf16[32,72,256]{2,1,0:T(8,128)(2,1)}), bf16[32,72,256]{2,1,0:T(8,128)(2,1)S(1)}, u32[]{:S(2)}, u32[]{:S(2)}) async-start(bf16[32,72,256]{2,1,0:T(8,128)(2,1)} %dispatch.3), calls=%async_computation.1 | async-start | bytes 2359296 | tf_op jit(solution)/shard_map/all_to_all | solution.py:307
  34.1 0.0 copy-done.2
  34.1 15.4 %attend.3 = (bf16[32,72,256]{2,1,0:T(8,128)(2,1)}, bf16[416,256]{1,0:T(8,128)(2,1)}, bf16[416,256]{1,0:T(8,128)(2,1)}, bf16[416,256]{1,0:T(8,128)(2,1)}, bf16[416,256]{1,0:T(8,128)(2,1)}) custom-call(s32[3]{0:T(128)} %pad_add_fusion.info, bf16[32,72,256]{2,1,0:T(8,128)(2,1)} %copy-done.2, bf16[1,1664,512]{2,1,0:T(8,128)(2,1)} %key_ref.3, ...), custom_call_target="tpu_custom_call" | custom-call | flops 29444014080 | bytes 4000000 | tf_op jit(solution)/shard_map/attend/pallas_call | solution.py:229
  49.6 1.9 %collective-permute-start = (bf16[416,256]{1,0:T(8,128)(2,1)}, bf16[416,256]{1,0:T(8,128)(2,1)S(1)}, u32[]{:S(2)}, u32[]{:S(2)}) collective-permute-start(bf16[416,256]{1,0:T(8,128)(2,1)} %get-tuple-element.47), channel_id=1, source_target_pairs={{0,32},{32,64},{64,96},{96,0},{1,33},{33,65},{65,97},{97,1},{2,34}... | collective-permute-start | bytes 638984 | tf_op jit(solution)/shard_map/ppermute | solution.py:309
  51.5 3.6 %collective-permute-start.1 = (bf16[416,256]{1,0:T(8,128)(2,1)}, bf16[416,256]{1,0:T(8,128)(2,1)S(1)}, u32[]{:S(2)}, u32[]{:S(2)}) collective-permute-start(bf16[416,256]{1,0:T(8,128)(2,1)} %get-tuple-element.48), channel_id=1, source_target_pairs={{0,64},{32,96},{64,0},{96,32},{1,65},{33,97},{65,1},{97,33},{2,66}... | collective-permute-start | bytes 638984 | tf_op jit(solution)/shard_map/ppermute | solution.py:309
  55.1 1.0 collective-permute-start.2
  56.1 0.0 all-to-all-done.1.rows_ref
  56.1 0.0 copy-start.3
  56.1 1.0 copy-done.3
  57.1 7.3 %all-to-all-start.3 = ((bf16[32,72,256]{2,1,0:T(8,128)(2,1)}), bf16[32,72,256]{2,1,0:T(8,128)(2,1)S(1)}, u32[]{:S(2)}, u32[]{:S(2)}) async-start(bf16[32,72,256]{2,1,0:T(8,128)(2,1)} %get-tuple-element.59), calls=%async_computation.3 | async-start | bytes 2359296 | tf_op jit(solution)/shard_map/all_to_all | solution.py:314
  64.4 15.5 %attend.2 = (bf16[32,72,256]{2,1,0:T(8,128)(2,1)}, bf16[416,256]{1,0:T(8,128)(2,1)}, bf16[416,256]{1,0:T(8,128)(2,1)}, bf16[416,256]{1,0:T(8,128)(2,1)}, bf16[416,256]{1,0:T(8,128)(2,1)}) custom-call(s32[3]{0:T(128)} %pad_add_fusion.info, bf16[32,72,256]{2,1,0:T(8,128)(2,1)} %copy-done.3, bf16[1,1664,512]{2,1,0:T(8,128)(2,1)} %key_ref.3, ...), custom_call_target="tpu_custom_call" | custom-call | flops 29444014080 | bytes 4000000 | tf_op jit(solution)/shard_map/attend/pallas_call | solution.py:229
  79.9 1.0 collective-permute-start.3
  80.9 0.4 collective-permute-start.4
  81.4 0.0 collective-permute-done.refs_1_
  81.4 0.0 copy-start.4
  81.4 2.2 %collective-permute-start.5 = (bf16[416,256]{1,0:T(8,128)(2,1)}, bf16[416,256]{1,0:T(8,128)(2,1)S(1)}, u32[]{:S(2)}, u32[]{:S(2)}) collective-permute-start(bf16[416,256]{1,0:T(8,128)(2,1)} %get-tuple-element.58), channel_id=1, source_target_pairs={{0,96},{32,0},{64,32},{96,64},{1,97},{33,1},{65,33},{97,65},{2,98}... | collective-permute-start | bytes 638984 | tf_op jit(solution)/shard_map/ppermute | solution.py:309
  83.6 0.0 collective-permute-done.1.refs_2_
  83.6 0.0 copy-start.5
  83.6 0.0 collective-permute-done.2.refs_3_
  83.6 0.0 copy-start.6
  83.6 0.0 all-to-all-done.3.back_ref
  83.6 0.0 copy-start.1
  83.6 0.0 copy-done.4
  83.7 0.6 copy-done.5
  84.3 0.1 copy-done.6
  84.4 7.4 %all-to-all-start.2 = ((bf16[32,72,256]{2,1,0:T(8,128)(2,1)}), bf16[32,72,256]{2,1,0:T(8,128)(2,1)S(1)}, u32[]{:S(2)}, u32[]{:S(2)}) async-start(bf16[32,72,256]{2,1,0:T(8,128)(2,1)} %get-tuple-element.50), calls=%async_computation.2 | async-start | bytes 2359296 | tf_op jit(solution)/shard_map/all_to_all | solution.py:317
  91.7 0.0 copy-done.1
  91.8 2.7 %combine.2 = (bf16[128,4096]{1,0:T(8,128)(2,1)}, bf16[128,4096]{1,0:T(8,128)(2,1)}) custom-call(bf16[128,144]{1,0:T(8,128)(2,1)} %get-tuple-element.40.turned_ref, bf16[32,72,256]{2,1,0:T(8,128)(2,1)} %copy-done.1), custom_call_target="tpu_custom_call" | custom-call | flops 1000000000 | bytes 3000000 | tf_op jit(solution)/shard_map/combine/pallas_call | solution.py:114
  94.5 0.0 collective-permute-done.3.refs_5_
  94.5 0.0 copy-start.7
  94.5 0.0 collective-permute-done.4.refs_6_
  94.5 0.0 copy-start.8
  94.5 0.0 collective-permute-done.5.refs_7_
  94.5 0.0 copy-start.9
  94.6 0.6 copy-done.7
  95.2 0.1 copy-done.8
  95.3 0.1 copy-done.9
  95.3 3.1 %add_shares.1 = (f32[208,512]{1,0:T(8,128)}, bf16[208,512]{1,0:T(8,128)(2,1)}) custom-call(s32[3]{0:T(128)} %pad_add_fusion.info, bf16[416,256]{1,0:T(8,128)(2,1)} %get-tuple-element.66.refs_0_, bf16[416,256]{1,0:T(8,128)(2,1)} %copy-done.4, bf16[416,256]{1,0:T(8,128)(2,1)} %copy-done.5, bf16[416,256]{1,0:T(8,128)(2,1)} %copy-done.6, ...), custom_call_target="tpu_custom_call" | custom-call | flops 100000000 | bytes 1000000 | tf_op jit(solution)/shard_map/add_shares/pallas_call | solution.py:278
  98.5 0.3 collective-permute-start.6
  98.8 1.4 %collective-permute-done.6 = bf16[208,512]{1,0:T(8,128)(2,1)S(1)} collective-permute-done((bf16[208,512]{1,0:T(8,128)(2,1)}, bf16[208,512]{1,0:T(8,128)(2,1)S(1)}, u32[]{:S(2)}, u32[]{:S(2)}) %collective-permute-start.6) | collective-permute-done | bytes 213024 | tf_op jit(solution)/shard_map/ppermute | solution.py:322
  100.2 1.1 convert_select_fusion.1
  101.3 0.1 fusion
  101.3 0.8 maximum_bitcast_fusion.1
  102.1 0.8 maximum_bitcast_fusion
  102.9 8.0 %all-to-all-done.2.back_ref = bf16[32,72,256]{2,1,0:T(8,128)(2,1)S(1)} async-done(((bf16[32,72,256]{2,1,0:T(8,128)(2,1)}), bf16[32,72,256]{2,1,0:T(8,128)(2,1)S(1)}, u32[]{:S(2)}, u32[]{:S(2)}) %all-to-all-start.2) | async-done | bytes 1179680 | tf_op jit(solution)/shard_map/all_to_all | solution.py:317
  110.9 0.0 copy-start
  110.9 1.0 copy-done
  111.9 2.7 %combine.3 = (bf16[128,4096]{1,0:T(8,128)(2,1)}, bf16[128,4096]{1,0:T(8,128)(2,1)}) custom-call(bf16[128,144]{1,0:T(8,128)(2,1)} %get-tuple-element.40.turned_ref, bf16[32,72,256]{2,1,0:T(8,128)(2,1)} %copy-done, bf16[128,4096]{1,0:T(8,128)(2,1)} %get-tuple-element.62.refs_0_, ...), custom_call_target="tpu_custom_call", output_to_operand_aliasing={{0}: (2, {}), {1}: (3, {})} | custom-call | flops 1000000000 | bytes 3000000 | tf_op jit(solution)/shard_map/combine/pallas_call | solution.py:114
Async XLA Ops:
  3.6 26.6 %all-to-all-start = ((bf16[32,72,256]{2,1,0:T(8,128)(2,1)}), bf16[32,72,256]{2,1,0:T(8,128)(2,1)S(1)}, u32[]{:S(2)}, u32[]{:S(2)}) async-start(bf16[32,72,256]{2,1,0:T(8,128)(2,1)} %get-tuple-element.41), calls=%async_computation | async-start | bytes 2359296 | tf_op jit(solution)/shard_map/all_to_all | solution.py:306
  30.2 4.0 %copy-start.2 = (bf16[32,72,256]{2,1,0:T(8,128)(2,1)}, bf16[32,72,256]{2,1,0:T(8,128)(2,1)S(1)}, u32[]{:S(2)}) copy-start(bf16[32,72,256]{2,1,0:T(8,128)(2,1)S(1)} %all-to-all-done.rows_ref) | copy-start | bytes 3538948
  30.2 25.9 %all-to-all-start.1 = ((bf16[32,72,256]{2,1,0:T(8,128)(2,1)}), bf16[32,72,256]{2,1,0:T(8,128)(2,1)S(1)}, u32[]{:S(2)}, u32[]{:S(2)}) async-start(bf16[32,72,256]{2,1,0:T(8,128)(2,1)} %dispatch.3), calls=%async_computation.1 | async-start | bytes 2359296 | tf_op jit(solution)/shard_map/all_to_all | solution.py:307
  49.6 31.8 %collective-permute-start = (bf16[416,256]{1,0:T(8,128)(2,1)}, bf16[416,256]{1,0:T(8,128)(2,1)S(1)}, u32[]{:S(2)}, u32[]{:S(2)}) collective-permute-start(bf16[416,256]{1,0:T(8,128)(2,1)} %get-tuple-element.47), channel_id=1, source_target_pairs={{0,32},{32,64},{64,96},{96,0},{1,33},{33,65},{65,97},{97,1},{2,34}... | collective-permute-start | bytes 638984 | tf_op jit(solution)/shard_map/ppermute | solution.py:309
  51.5 32.1 %collective-permute-start.1 = (bf16[416,256]{1,0:T(8,128)(2,1)}, bf16[416,256]{1,0:T(8,128)(2,1)S(1)}, u32[]{:S(2)}, u32[]{:S(2)}) collective-permute-start(bf16[416,256]{1,0:T(8,128)(2,1)} %get-tuple-element.48), channel_id=1, source_target_pairs={{0,64},{32,96},{64,0},{96,32},{1,65},{33,97},{65,1},{97,33},{2,66}... | collective-permute-start | bytes 638984 | tf_op jit(solution)/shard_map/ppermute | solution.py:309
  55.1 28.5 %collective-permute-start.2 = (bf16[416,256]{1,0:T(8,128)(2,1)}, bf16[416,256]{1,0:T(8,128)(2,1)S(1)}, u32[]{:S(2)}, u32[]{:S(2)}) collective-permute-start(bf16[416,256]{1,0:T(8,128)(2,1)} %get-tuple-element.49), channel_id=1, source_target_pairs={{0,96},{32,0},{64,32},{96,64},{1,97},{33,1},{65,33},{97,65},{2,98}... | collective-permute-start | bytes 638984 | tf_op jit(solution)/shard_map/ppermute | solution.py:309
  56.1 1.0 copy-start.3
  57.1 26.5 %all-to-all-start.3 = ((bf16[32,72,256]{2,1,0:T(8,128)(2,1)}), bf16[32,72,256]{2,1,0:T(8,128)(2,1)S(1)}, u32[]{:S(2)}, u32[]{:S(2)}) async-start(bf16[32,72,256]{2,1,0:T(8,128)(2,1)} %get-tuple-element.59), calls=%async_computation.3 | async-start | bytes 2359296 | tf_op jit(solution)/shard_map/all_to_all | solution.py:314
  79.9 14.6 %collective-permute-start.3 = (bf16[416,256]{1,0:T(8,128)(2,1)}, bf16[416,256]{1,0:T(8,128)(2,1)S(1)}, u32[]{:S(2)}, u32[]{:S(2)}) collective-permute-start(bf16[416,256]{1,0:T(8,128)(2,1)} %get-tuple-element.56), channel_id=1, source_target_pairs={{0,32},{32,64},{64,96},{96,0},{1,33},{33,65},{65,97},{97,1},{2,34}... | collective-permute-start | bytes 638984 | tf_op jit(solution)/shard_map/ppermute | solution.py:309
  80.9 13.6 %collective-permute-start.4 = (bf16[416,256]{1,0:T(8,128)(2,1)}, bf16[416,256]{1,0:T(8,128)(2,1)S(1)}, u32[]{:S(2)}, u32[]{:S(2)}) collective-permute-start(bf16[416,256]{1,0:T(8,128)(2,1)} %get-tuple-element.57), channel_id=1, source_target_pairs={{0,64},{32,96},{64,0},{96,32},{1,65},{33,97},{65,1},{97,33},{2,66}... | collective-permute-start | bytes 638984 | tf_op jit(solution)/shard_map/ppermute | solution.py:309
  81.4 2.3 %copy-start.4 = (bf16[416,256]{1,0:T(8,128)(2,1)}, bf16[416,256]{1,0:T(8,128)(2,1)S(1)}, u32[]{:S(2)}) copy-start(bf16[416,256]{1,0:T(8,128)(2,1)S(1)} %collective-permute-done.refs_1_) | copy-start | bytes 638980
  81.4 13.2 %collective-permute-start.5 = (bf16[416,256]{1,0:T(8,128)(2,1)}, bf16[416,256]{1,0:T(8,128)(2,1)S(1)}, u32[]{:S(2)}, u32[]{:S(2)}) collective-permute-start(bf16[416,256]{1,0:T(8,128)(2,1)} %get-tuple-element.58), channel_id=1, source_target_pairs={{0,96},{32,0},{64,32},{96,64},{1,97},{33,1},{65,33},{97,65},{2,98}... | collective-permute-start | bytes 638984 | tf_op jit(solution)/shard_map/ppermute | solution.py:309
  83.6 0.7 copy-start.5
  83.6 0.7 copy-start.6
  83.6 8.1 %copy-start.1 = (bf16[32,72,256]{2,1,0:T(8,128)(2,1)}, bf16[32,72,256]{2,1,0:T(8,128)(2,1)S(1)}, u32[]{:S(2)}) copy-start(bf16[32,72,256]{2,1,0:T(8,128)(2,1)S(1)} %all-to-all-done.3.back_ref) | copy-start | bytes 3538948
  84.4 26.5 %all-to-all-start.2 = ((bf16[32,72,256]{2,1,0:T(8,128)(2,1)}), bf16[32,72,256]{2,1,0:T(8,128)(2,1)S(1)}, u32[]{:S(2)}, u32[]{:S(2)}) async-start(bf16[32,72,256]{2,1,0:T(8,128)(2,1)} %get-tuple-element.50), calls=%async_computation.2 | async-start | bytes 2359296 | tf_op jit(solution)/shard_map/all_to_all | solution.py:317
  94.5 0.7 copy-start.7
  94.5 0.7 copy-start.8
  94.5 0.8 copy-start.9
  98.5 1.7 %collective-permute-start.6 = (bf16[208,512]{1,0:T(8,128)(2,1)}, bf16[208,512]{1,0:T(8,128)(2,1)S(1)}, u32[]{:S(2)}, u32[]{:S(2)}) collective-permute-start(bf16[208,512]{1,0:T(8,128)(2,1)} %get-tuple-element.75), channel_id=1, source_target_pairs={{0,16},{16,0},{1,17},{17,1},{2,18},{18,2},{3,19},{19,3},{4,20},{20... | collective-permute-start | bytes 638984 | tf_op jit(solution)/shard_map/ppermute | solution.py:322
  110.9 1.0 copy-start

commit v3 on v2

--- a/solution.py
+++ b/solution.py
@@ -16,7 +16,10 @@
 BF16 = jnp.bfloat16
 ROWS_LAST = (((1,), (1,)), ((), ()))
 LIMIT = 60 * 2**20
+SMALL = 16 * 2**20
+ATTEND_LIMITS = (32 * 2**20, 56 * 2**20)
 WAYS = 9
+TURNS = (3, 5, 5)
 
 
 def token_slots(ids, tile_num):
@@ -123,18 +126,20 @@
         out_shape=[jax.ShapeDtypeStruct(shape, BF16)] * 2,
         scratch_shapes=[pltpu.VMEM((2, tile_num * GROUP, HEAD_WIDTH), F32)],
         input_output_aliases={2: 0, 3: 1} if earlier else {},
-        compiler_params=pltpu.CompilerParams(vmem_limit_bytes=LIMIT),
-        cost_estimate=pl.CostEstimate(flops=10**9, bytes_accessed=3 * 10**6, transcendentals=0),
+        compiler_params=pltpu.CompilerParams(vmem_limit_bytes=SMALL),
+        cost_estimate=pl.CostEstimate(flops=10**6, bytes_accessed=10**5, transcendentals=0),
         name="combine",
     )(turned, back, *earlier)
 
 
-def attend_kernel(info, rows_ref, key_ref, value_ref, back_ref, *refs, ways):
-    scratch = refs[-(10 + 3 * ways) :]
+def attend_kernel(info, rows_ref, key_ref, value_ref, back_ref, *refs, ways, depth):
+    scratch = refs[-(10 + sum(TURNS)) :]
     shares = refs[: -len(scratch)]
     query_s, grad_s, out_s, query_grad_s, key_fill, key_zero, value_ones = scratch[:7]
     key_grad_s, value_grad_s, grads_s = scratch[7:10]
-    score_s, prob_s, slope_s = (scratch[10 + i * ways : 10 + (i + 1) * ways] for i in range(3))
+    buffers = list(scratch[10:])
+    turns = [[buffers.pop(0) for _ in range(turn)] for turn in TURNS]
+    score_s, prob_s, slope_s = ([turn[w % len(turn)] for w in range(ways)] for turn in turns)
     device_num, slot_rows, _ = rows_ref.shape
     patches = key_ref.shape[1]
     width = HEAD_WIDTH
@@ -206,28 +211,30 @@
         back_ref[i, :, :width] = out_s[own, :].astype(BF16)
         back_ref[i, :, width:] = query_grad_s[own, :].astype(BF16)
     live = lax.broadcasted_iota(jnp.int32, (width, patches), 1) < info[2]
-    key_grad_s[...] = jnp.where(live, key_grad_s[...] * inv_root, 0.0)
-    value_grad_s[...] = jnp.where(live, value_grad_s[...], 0.0)
-    grads_s[:, :width] = key_grad_s[...].T
-    grads_s[:, width:] = value_grad_s[...].T
+    grads_s[:, :width] = jnp.where(live, key_grad_s[...] * inv_root, 0.0).T
+    grads_s[:, width:] = jnp.where(live, value_grad_s[...], 0.0).T
     for i, share in enumerate(shares):
-        part = lax.rem(info[1] + i, len(shares))
         size = share.shape[0]
-        share[...] = grads_s[pl.ds(pl.multiple_of(part * size, size), size), :].astype(BF16)
-
-
-def attend(info, rows, keys, values, part, share_num):
+        split = len(shares) // depth
+        place = lax.rem(info[1] + i // split, depth) * split
+        if split == 2:
+            place = place + (info[0] if i % 2 == 0 else 1 - info[0])
+        share[...] = grads_s[pl.ds(pl.multiple_of(place * size, size), size), :].astype(BF16)
+
+
+def attend(info, rows, keys, values, depth, split):
     device_num, slot_rows, both = rows.shape
     patches = keys.shape[1]
+    share_num = depth * split
     total = device_num * slot_rows
     width = HEAD_WIDTH
     share = patches // share_num
     ways = WAYS
     block_rows = total // ways
-    tile = pl.BlockSpec((1, patches, width), lambda i, info: (0, 0, 2 * info[0] + part))
+    tile = pl.BlockSpec((1, patches, width), lambda i, info: (0, 0, 0))
     whole = pl.BlockSpec(rows.shape, lambda i, info: (0, 0, 0))
     return pl.pallas_call(
-        functools.partial(attend_kernel, ways=ways),
+        functools.partial(attend_kernel, ways=ways, depth=depth),
         grid_spec=pltpu.PrefetchScalarGridSpec(
             num_scalar_prefetch=1,
             grid=(1,),
@@ -245,12 +252,12 @@
                 pltpu.VMEM((width, patches), F32),
                 pltpu.VMEM((patches, both), F32),
             ]
-            + [pltpu.VMEM((block_rows, patches), F32)] * ways
-            + [pltpu.VMEM((block_rows, patches), BF16)] * (2 * ways),
+            + [pltpu.VMEM((block_rows, patches), F32)] * TURNS[0]
+            + [pltpu.VMEM((block_rows, patches), BF16)] * (TURNS[1] + TURNS[2]),
         ),
         out_shape=[jax.ShapeDtypeStruct(rows.shape, BF16)]
         + [jax.ShapeDtypeStruct((share, both), BF16)] * share_num,
-        compiler_params=pltpu.CompilerParams(vmem_limit_bytes=LIMIT),
+        compiler_params=pltpu.CompilerParams(vmem_limit_bytes=ATTEND_LIMITS[split - 1]),
         cost_estimate=pl.CostEstimate(
             flops=60 * total * patches * width,
             bytes_accessed=4 * 10**6,
@@ -262,35 +269,60 @@
 
 def add_kernel(info, *refs):
     shares, (mine_ref, theirs_ref) = refs[:-2], refs[-2:]
-    half, both = mine_ref.shape[0], shares[0].shape[1]
-    for part in range(2):
-        of_part = shares[part * len(shares) // 2 : (part + 1) * len(shares) // 2]
-        lanes = slice(part * both, (part + 1) * both)
-        for target, core in ((mine_ref, info[0]), (theirs_ref, 1 - info[0])):
-            rows = pl.ds(pl.multiple_of(core * half, half), half)
-            total = sum(share[rows, :].astype(F32) for share in of_part)
-            target[:, lanes] = total.astype(target.dtype)
+    half = mine_ref.shape[0]
+    for target, core in ((mine_ref, info[0]), (theirs_ref, 1 - info[0])):
+        rows = pl.ds(pl.multiple_of(core * half, half), half)
+        target[...] = sum(share[rows, :].astype(F32) for share in shares).astype(target.dtype)
 
 
 def add_shares(info, shares):
     rows, both = shares[0].shape
     half = rows // 2
+    fixed = lambda size: pl.BlockSpec((size, both), lambda i, info: (0, 0))
     return pl.pallas_call(
         add_kernel,
         grid_spec=pltpu.PrefetchScalarGridSpec(
             num_scalar_prefetch=1,
             grid=(1,),
-            in_specs=[pl.BlockSpec((rows, both), lambda i, info: (0, 0))] * len(shares),
-            out_specs=[pl.BlockSpec((half, 2 * both), lambda i, info: (0, 0))] * 2,
+            in_specs=[fixed(rows)] * len(shares),
+            out_specs=[fixed(half)] * 2,
         ),
-        out_shape=[
-            jax.ShapeDtypeStruct((half, 2 * both), F32),
-            jax.ShapeDtypeStruct((half, 2 * both), BF16),
-        ],
-        compiler_params=pltpu.CompilerParams(vmem_limit_bytes=LIMIT),
-        cost_estimate=pl.CostEstimate(flops=10**8, bytes_accessed=10**6, transcendentals=0),
+        out_shape=[jax.ShapeDtypeStruct((half, both), dtype) for dtype in (F32, BF16)],
+        compiler_params=pltpu.CompilerParams(vmem_limit_bytes=SMALL),
+        cost_estimate=pl.CostEstimate(flops=10**6, bytes_accessed=10**5, transcendentals=0),
         name="add_shares",
     )(info, *shares)
+
+
+def place_kernel(info, *refs):
+    (mine, other, *shares), (key_ref, value_ref) = refs[:-2], refs[-2:]
+    width = HEAD_WIDTH
+    parts = [(mine[...], other[...].astype(F32))]
+    parts.append([sum(share[...].astype(F32) for share in shares[i::2]) for i in range(2)])
+    for part, (own, theirs) in enumerate(parts):
+        for core in range(2):
+            chosen = jnp.where(info[0] == core, own, theirs)
+            group = 2 * core + part
+            for first, target in ((0, key_ref), (width, value_ref)):
+                target[0, :, group * width : (group + 1) * width] = chosen[:, first : first + width]
+
+
+def place(info, mine, other, shares):
+    rows, both = mine.shape
+    out = (1, rows, 2 * both)
+    return pl.pallas_call(
+        place_kernel,
+        grid_spec=pltpu.PrefetchScalarGridSpec(
+            num_scalar_prefetch=1,
+            grid=(1,),
+            in_specs=[pl.BlockSpec((rows, both), lambda i, info: (0, 0))] * (2 + len(shares)),
+            out_specs=[pl.BlockSpec(out, lambda i, info: (0, 0, 0))] * 2,
+        ),
+        out_shape=[jax.ShapeDtypeStruct(out, F32)] * 2,
+        compiler_params=pltpu.CompilerParams(vmem_limit_bytes=SMALL),
+        cost_estimate=pl.CostEstimate(flops=10**6, bytes_accessed=10**5, transcendentals=0),
+        name="place",
+    )(info, mine, other, *shares)
 
 
 def local(queries, tile_ids, keys, values, patch_counts, output_gradient):
@@ -303,33 +335,30 @@
     ids = tile_ids.reshape(1, -1)
     sent, slots, turned = dispatch(ids, queries, output_gradient, 0, tile_num)
     (later,) = dispatch(slots, queries, output_gradient, 1, tile_num)
-    rows, later = lax.optimization_barrier((exchange(sent), later))
+    first = 2 * lax.axis_index("core") * HEAD_WIDTH
+    tiles = [
+        [lax.dynamic_slice_in_dim(a, first + part * HEAD_WIDTH, HEAD_WIDTH, 2) for a in (keys, values)]
+        for part in range(2)
+    ]
+    rows, later, tiles = lax.optimization_barrier((exchange(sent), later, tiles))
     rows = [rows, exchange(later)]
-    along_z = lambda shares: [
-        lax.ppermute(shares[s], "z", [(i, (i + s) % depth) for i in range(depth)])
-        for s in range(1, depth)
-    ]
-    back, own, *shares = attend(info, rows[0], keys, values, 0, depth)
-    sums = [own, *along_z([own, *shares])]
+    back, *shares = attend(info, rows[0], *tiles[0], depth, 1)
     first_back = exchange(back)
-    back, own, *shares = attend(info, rows[1], keys, values, 1, depth)
-    back, sums = lax.optimization_barrier((back, sums))
+    shares, rows = lax.optimization_barrier((shares, rows))
+    for i in range(1, depth):
+        shares[i] = lax.ppermute(shares[i], "z", [(z, (z + i) % depth) for z in range(depth)])
+    back, *later = attend(info, rows[1], *tiles[1], depth, 2)
+    back, shares = lax.optimization_barrier((back, shares))
     second_back = exchange(back)
+    for i in range(1, 2 * depth):
+        to = lambda z, core: ((z + i // 2) % depth) * 2 + (core + i) % 2
+        pairs = [(2 * z + core, to(z, core)) for z in range(depth) for core in range(2)]
+        later[i] = lax.ppermute(later[i], ("z", "core"), pairs)
+    mine, given = add_shares(info, shares)
+    other = lax.ppermute(given, "core", [(0, 1), (1, 0)])
     outputs = combine(turned, first_back, 0, (), queries.shape)
-    sums = sums + [own, *along_z([own, *shares])]
-    sums, outputs = lax.optimization_barrier((sums, outputs))
-    mine, given = add_shares(info, sums)
-    other = lax.ppermute(given, "core", [(0, 1), (1, 0)]).astype(F32)
+    grads = place(info, mine, other, later)
     outputs = combine(turned, second_back, 1, outputs, queries.shape)
-    core = lax.axis_index("core")
-    sides = (jnp.where(core == 0, mine, other), jnp.where(core == 0, other, mine))
-    width = HEAD_WIDTH
-    grads = [
-        jnp.concatenate(
-            [side[:, a : a + width] for side in sides for a in (first, first + 2 * width)], axis=1
-        )[None]
-        for first in (0, width)
-    ]
     return (*outputs, *grads)
 
 

time: 115 us -> 109 us (0.948)
  starting transfers between devices: 36.5 us -> 43.2 us
  Pallas kernels: 45 us -> 40.6 us
  waiting for transfers between devices: 24.8 us -> 20.5 us
  other arithmetic: 3.26 us -> 0.08 us
    ppermute x7 -> x11, starting transfers between devices: 10.5 us -> 19.7 us  [the longest x7 8.22 us: local(): later[i] = lax.ppermute(later[i], ('z', 'core'), pairs)]
    all_to_all x1, waiting for transfers between devices: 8 us -> 1.96 us  [local(): second_back = exchange(back)]
    all_to_all x1, waiting for transfers between devices: 0.01 us -> 5.05 us  [local(): rows = [rows, exchange(later)]]
    unnamed x20 -> x12, local copies, waits for them, and re-layouts: 3.56 us -> 0.02 us
    all_to_all x1, starting transfers between devices: 7.31 us -> 3.94 us  [local(): first_back = exchange(back)]
    pallas_call x1, Pallas kernels: 3.14 us -> 0.65 us  [add_shares(): pl.pallas_call(add_kernel, grid_spec=pltpu.PrefetchScalarGridSpec(num_sca...]
    dynamic_slice x0 -> x1, local copies, waits for them, and re-layouts: none -> 2.44 us  [local(): lax.dynamic_slice_in_dim(a, first + part * HEAD_WIDTH, HEAD_WIDTH, 2)]
    pallas_call x2, Pallas kernels: 5.48 us -> 3.31 us  [combine(): pl.pallas_call(combine_kernel, grid=(2,), in_specs=[pl.BlockSpec(turned.s...]
  transfers between devices with their start and end apart: 11 -> 15, of which waited for: 3 -> 3; matrix products, arithmetic and copies ran while one was open for 3% -> 2% of each run, Pallas kernels for 34% -> 33%
where the time goes in v3:
time: 109 us; the launch traced here: 108 us
  starting transfers between devices  43.2 us (40%)
  Pallas kernels  40.6 us (37%)
  waiting for transfers between devices  20.5 us (19%)
  local copies, waits for them, and re-layouts  2.47 us (2%)
  between operations  1.45 us (1%)
    pallas_call x2, Pallas kernels, attend(): pl.pallas_call(functools.partial(attend_kernel, ways=ways, depth=depth),...  29.5 us
    all_to_all x1, waiting for transfers between devices, local(): exchange(sent)  13.5 us
    ppermute x7, starting transfers between devices, local(): later[i] = lax.ppermute(later[i], ('z', 'core'), pairs)  8.22 us
    all_to_all x1, starting transfers between devices, local(): second_back = exchange(back)  7.45 us
    all_to_all x1, starting transfers between devices, local(): exchange(sent)  7.41 us
    ppermute x3, starting transfers between devices, local(): lax.ppermute(shares[i], 'z', [(z, (z + i) % depth) for z in range(depth)])  6.57 us
    pallas_call x2, Pallas kernels, dispatch(): pl.pallas_call(route_kernel if part == 0 else dispatch_kernel, grid=(2,),...  5.48 us
    all_to_all x1, waiting for transfers between devices, local(): rows = [rows, exchange(later)]  5.05 us
  transfers between devices with their start and end apart: 15, of which 3 were waited for; matrix products, arithmetic and copies ran while one was open for 2% of the time, Pallas kernels for 33%

profile of v3, /device:TPU:0, one launch (start us, length us, event | category | flops | bytes accessed | tf_op | source)
XLA Modules:
  0.0 108.2 jit_solution(12359613911111529244)
XLA Ops:
  0.6 3.0 %dispatch.2 = (bf16[32,72,256]{2,1,0:T(8,128)(2,1)}, bf16[144,128]{1,0:T(8,128)(2,1)}, bf16[128,144]{1,0:T(8,128)(2,1)}) custom-call(s32[1,128]{1,0:T(1,128)} %bitcast.3, bf16[128,4096]{1,0:T(8,128)(2,1)} %query_ref.3, bf16[128,4096]{1,0:T(8,128)(2,1)} %grad_ref.3), custom_call_target="tpu_custom_call" | custom-call | flops 1000000000 | bytes 3000000 | tf_op jit(solution)/shard_map/dispatch/pallas_call | solution.py:78
  3.6 7.4 %all-to-all-start = ((bf16[32,72,256]{2,1,0:T(8,128)(2,1)}), bf16[32,72,256]{2,1,0:T(8,128)(2,1)S(1)}, u32[]{:S(2)}, u32[]{:S(2)}) async-start(bf16[32,72,256]{2,1,0:T(8,128)(2,1)} %get-tuple-element.46), calls=%async_computation | async-start | bytes 2359296 | tf_op jit(solution)/shard_map/all_to_all | solution.py:343
  11.7 2.5 %dispatch.3 = bf16[32,72,256]{2,1,0:T(8,128)(2,1)} custom-call(bf16[144,128]{1,0:T(8,128)(2,1)} %get-tuple-element.47.slots_ref, bf16[128,4096]{1,0:T(8,128)(2,1)} %query_ref.3, bf16[128,4096]{1,0:T(8,128)(2,1)} %grad_ref.3), custom_call_target="tpu_custom_call" | custom-call | flops 1000000000 | bytes 3000000 | tf_op jit(solution)/shard_map/dispatch/pallas_call | solution.py:78
  14.2 0.1 pad_add_fusion.info
  14.3 0.0 copy-start.2
  14.3 2.4 %constant_dynamic-slice_fusion = (bf16[1,1664,128]{2,1,0:T(8,128)(2,1)}, bf16[1,1664,128]{2,1,0:T(8,128)(2,1)S(1)}, bf16[1,1664,128]{2,1,0:T(8,128)(2,1)S(1)}, bf16[1,1664,128]{2,1,0:T(8,128)(2,1)}) fusion(bf16[1,1664,512]{2,1,0:T(8,128)(2,1)} %param.9, s32[]{:T(128)S(6)} %select_n.9, s32[]{:T(128)S(6)} %select_n.8, bf16[1,1664,512]{2,1,0:T(8,128)(2,1)} %param.8), kind=kLoop, calls=%fused_computation | loop fusion | bytes 3407880 | tf_op jit(solution)/shard_map/dynamic_slice | solution.py:340
  16.7 13.5 %all-to-all-done.rows_ref = bf16[32,72,256]{2,1,0:T(8,128)(2,1)S(1)} async-done(((bf16[32,72,256]{2,1,0:T(8,128)(2,1)}), bf16[32,72,256]{2,1,0:T(8,128)(2,1)S(1)}, u32[]{:S(2)}, u32[]{:S(2)}) %all-to-all-start) | async-done | bytes 1179680 | tf_op jit(solution)/shard_map/all_to_all | solution.py:343
  30.2 4.7 %all-to-all-start.1 = ((bf16[32,72,256]{2,1,0:T(8,128)(2,1)}), bf16[32,72,256]{2,1,0:T(8,128)(2,1)}, u32[]{:S(2)}, u32[]{:S(2)}) async-start(bf16[32,72,256]{2,1,0:T(8,128)(2,1)} %dispatch.3), calls=%async_computation.1 | async-start | bytes 2359296 | tf_op jit(solution)/shard_map/all_to_all | solution.py:344
  34.8 0.0 copy-done.2
  34.9 14.1 %attend.2 = (bf16[32,72,256]{2,1,0:T(8,128)(2,1)}, bf16[416,256]{1,0:T(8,128)(2,1)S(1)}, bf16[416,256]{1,0:T(8,128)(2,1)}, bf16[416,256]{1,0:T(8,128)(2,1)}, bf16[416,256]{1,0:T(8,128)(2,1)S(1)}) custom-call(s32[3]{0:T(128)S(1)} %pad_add_fusion.info, bf16[32,72,256]{2,1,0:T(8,128)(2,1)S(1)} %all-to-all-done.rows_ref, ...), custom_call_target="tpu_custom_call" | custom-call | flops 29444014080 | bytes 4000000 | tf_op jit(solution)/shard_map/attend/pallas_call | solution.py:236
  49.0 5.0 %all-to-all-done.1.rows_ref = bf16[32,72,256]{2,1,0:T(8,128)(2,1)} async-done(((bf16[32,72,256]{2,1,0:T(8,128)(2,1)}), bf16[32,72,256]{2,1,0:T(8,128)(2,1)}, u32[]{:S(2)}, u32[]{:S(2)}) %all-to-all-start.1) | async-done | bytes 1179680 | tf_op jit(solution)/shard_map/all_to_all | solution.py:344
  54.0 3.9 %all-to-all-start.3 = ((bf16[32,72,256]{2,1,0:T(8,128)(2,1)}), bf16[32,72,256]{2,1,0:T(8,128)(2,1)S(1)}, u32[]{:S(2)}, u32[]{:S(2)}) async-start(bf16[32,72,256]{2,1,0:T(8,128)(2,1)} %get-tuple-element.65), calls=%async_computation.3 | async-start | bytes 2359296 | tf_op jit(solution)/shard_map/all_to_all | solution.py:346
  58.0 2.0 %collective-permute-start = (bf16[416,256]{1,0:T(8,128)(2,1)}, bf16[416,256]{1,0:T(8,128)(2,1)S(1)}, u32[]{:S(2)}, u32[]{:S(2)}) collective-permute-start(bf16[416,256]{1,0:T(8,128)(2,1)} %get-tuple-element.61), channel_id=1, source_target_pairs={{0,32},{32,64},{64,96},{96,0},{1,33},{33,65},{65,97},{97,1},{2,34}... | collective-permute-start | bytes 638984 | tf_op jit(solution)/shard_map/ppermute | solution.py:349
  59.9 3.6 %collective-permute-start.1 = (bf16[416,256]{1,0:T(8,128)(2,1)}, bf16[416,256]{1,0:T(8,128)(2,1)S(1)}, u32[]{:S(2)}, u32[]{:S(2)}) collective-permute-start(bf16[416,256]{1,0:T(8,128)(2,1)} %get-tuple-element.62), channel_id=1, source_target_pairs={{0,64},{32,96},{64,0},{96,32},{1,65},{33,97},{65,1},{97,33},{2,66}... | collective-permute-start | bytes 638984 | tf_op jit(solution)/shard_map/ppermute | solution.py:349
  63.5 1.0 collective-permute-start.2
  64.5 15.4 %attend.3 = (bf16[32,72,256]{2,1,0:T(8,128)(2,1)}, bf16[208,256]{1,0:T(8,128)(2,1)}, bf16[208,256]{1,0:T(8,128)(2,1)}, bf16[208,256]{1,0:T(8,128)(2,1)}, bf16[20...) custom-call(s32[3]{0:T(128)} %copy-done.2, ...), custom_call_target="tpu_custom_call" | custom-call | flops 29444014080 | bytes 4000000 | tf_op jit(solution)/shard_map/attend/pallas_call | solution.py:236
  79.9 0.0 collective-permute-done.refs_1_
  79.9 0.0 collective-permute-done.1.refs_2_
  79.9 0.0 collective-permute-done.2.refs_3_
  79.9 0.0 copy-start.3
  79.9 0.0 copy-start.5
  79.9 0.0 copy-start.4
  79.9 0.0 copy-start
  80.0 0.0 all-to-all-done.3.back_ref
  80.0 7.5 %all-to-all-start.2 = ((bf16[32,72,256]{2,1,0:T(8,128)(2,1)}), bf16[32,72,256]{2,1,0:T(8,128)(2,1)S(1)}, u32[]{:S(2)}, u32[]{:S(2)}) async-start(bf16[32,72,256]{2,1,0:T(8,128)(2,1)} %get-tuple-element.64), calls=%async_computation.2 | async-start | bytes 2359296 | tf_op jit(solution)/shard_map/all_to_all | solution.py:352
  87.4 0.0 copy-start.1
  87.4 0.4 collective-permute-start.4
  87.8 1.0 collective-permute-start.5
  88.8 0.0 collective-permute-start.6
  88.8 3.2 %collective-permute-start.7 = (bf16[208,256]{1,0:T(8,128)(2,1)}, bf16[208,256]{1,0:T(8,128)(2,1)S(1)}, u32[]{:S(2)}, u32[]{:S(2)}) collective-permute-start(bf16[208,256]{1,0:T(8,128)(2,1)} %get-tuple-element.80), channel_id=1, source_target_pairs={{0,64},{16,80},{32,96},{48,112},{64,0},{80,16},{96,32},{112,48},{1... | collective-permute-start | bytes 319496 | tf_op jit(solution)/shard_map/ppermute | solution.py:356
  92.1 0.2 collective-permute-start.8
  92.3 0.0 copy-done.3
  92.3 0.6 add_shares.1
  92.9 0.0 collective-permute-done.4.refs_3_
  92.9 0.0 copy-done.5
  92.9 2.8 %collective-permute-start.9 = (bf16[208,256]{1,0:T(8,128)(2,1)S(1)}, bf16[208,256]{1,0:T(8,128)(2,1)S(1)}, u32[]{:S(2)}, u32[]{:S(2)}) collective-permute-start(bf16[208,256]{1,0:T(8,128)(2,1)S(1)} %copy-done.5), channel_id=1, source_target_pairs={{0,96},{16,112},{32,0},{48,16},{64,32},{80,48},{96,64},{112,80},{1... | collective-permute-start | bytes 319496 | tf_op jit(solution)/shard_map/ppermute | solution.py:356
  95.8 0.0 collective-permute-done.5.refs_4_
  95.8 0.0 copy-done.4
  95.8 0.6 collective-permute-start.10
  96.3 0.0 collective-permute-done.6.refs_5_
  96.3 4.9 %collective-permute-start.3 = (bf16[208,256]{1,0:T(8,128)(2,1)S(1)}, bf16[208,256]{1,0:T(8,128)(2,1)S(1)}, u32[]{:S(2)}, u32[]{:S(2)}) collective-permute-start(bf16[208,256]{1,0:T(8,128)(2,1)S(1)} %get-tuple-element.75), channel_id=1, source_target_pairs={{0,16},{16,0},{1,17},{17,1},{2,18},{18,2},{3,19},{19,3},{4,20},{20... | collective-permute-start | bytes 319496 | tf_op jit(solution)/shard_map/ppermute | solution.py:358
  101.3 0.0 copy-done
  101.3 1.7 %combine.2 = (bf16[128,4096]{1,0:T(8,128)(2,1)}, bf16[128,4096]{1,0:T(8,128)(2,1)}) custom-call(bf16[128,144]{1,0:T(8,128)(2,1)S(1)} %copy-done, bf16[32,72,256]{2,1,0:T(8,128)(2,1)S(1)} %all-to-all-done.3.back_ref), custom_call_target="tpu_custom_call" | custom-call | flops 1000000 | bytes 100000 | tf_op jit(solution)/shard_map/combine/pallas_call | solution.py:117
  102.9 0.0 collective-permute-done.7.refs_6_
  102.9 0.0 collective-permute-done.8.refs_7_
  103.0 0.0 collective-permute-done.9.refs_8_
  103.0 0.0 collective-permute-done.10.refs_9_
  103.0 0.0 collective-permute-done.3.refs_1_
  103.0 0.0 copy-done.1
  103.0 1.6 %place.1 = (f32[1,208,512]{2,1,0:T(8,128)}, f32[1,208,512]{2,1,0:T(8,128)}) custom-call(s32[3]{0:T(128)S(1)} %copy-done.3, f32[208,256]{1,0:T(8,128)S(1)} %get-tuple-element.74.refs_0_, bf16[208,256]{1,0:T(8,128)(2,1)S(1)} %collective-permute-done.3.refs_1_, bf16[208,256]{1,0:T(8,128)(2,1)S(1)} %copy-done.1, ...), custom_call_target="tpu_custom_call" | custom-call | flops 1000000 | bytes 100000 | tf_op jit(solution)/shard_map/place/pallas_call | solution.py:313
  104.6 2.0 %all-to-all-done.2.back_ref = bf16[32,72,256]{2,1,0:T(8,128)(2,1)S(1)} async-done(((bf16[32,72,256]{2,1,0:T(8,128)(2,1)}), bf16[32,72,256]{2,1,0:T(8,128)(2,1)S(1)}, u32[]{:S(2)}, u32[]{:S(2)}) %all-to-all-start.2) | async-done | bytes 1179680 | tf_op jit(solution)/shard_map/all_to_all | solution.py:352
  106.6 1.7 %combine.3 = (bf16[128,4096]{1,0:T(8,128)(2,1)}, bf16[128,4096]{1,0:T(8,128)(2,1)}) custom-call(bf16[128,144]{1,0:T(8,128)(2,1)S(1)} %copy-done, bf16[32,72,256]{2,1,0:T(8,128)(2,1)S(1)} %all-to-all-done.2.back_ref, bf16[128,4096]{1,0:T(8,128)(2,1)} %get-tuple-element.66.refs_0_, ...), custom_call_target="tpu_custom_call", output_to_operand_aliasing={{0}: (2, {}), {1}: (3, {})} | custom-call | flops 1000000 | bytes 100000 | tf_op jit(solution)/shard_map/combine/pallas_call | solution.py:117
Async XLA Ops:
  3.6 26.6 %all-to-all-start = ((bf16[32,72,256]{2,1,0:T(8,128)(2,1)}), bf16[32,72,256]{2,1,0:T(8,128)(2,1)S(1)}, u32[]{:S(2)}, u32[]{:S(2)}) async-start(bf16[32,72,256]{2,1,0:T(8,128)(2,1)} %get-tuple-element.46), calls=%async_computation | async-start | bytes 2359296 | tf_op jit(solution)/shard_map/all_to_all | solution.py:343
  14.3 20.6 %copy-start.2 = (s32[3]{0:T(128)}, s32[3]{0:T(128)S(1)}, u32[]{:S(2)}) copy-start(s32[3]{0:T(128)S(1)} %pad_add_fusion.info) | copy-start | bytes 40
  30.2 23.8 %all-to-all-start.1 = ((bf16[32,72,256]{2,1,0:T(8,128)(2,1)}), bf16[32,72,256]{2,1,0:T(8,128)(2,1)}, u32[]{:S(2)}, u32[]{:S(2)}) async-start(bf16[32,72,256]{2,1,0:T(8,128)(2,1)} %dispatch.3), calls=%async_computation.1 | async-start | bytes 2359296 | tf_op jit(solution)/shard_map/all_to_all | solution.py:344
  54.0 26.0 %all-to-all-start.3 = ((bf16[32,72,256]{2,1,0:T(8,128)(2,1)}), bf16[32,72,256]{2,1,0:T(8,128)(2,1)S(1)}, u32[]{:S(2)}, u32[]{:S(2)}) async-start(bf16[32,72,256]{2,1,0:T(8,128)(2,1)} %get-tuple-element.65), calls=%async_computation.3 | async-start | bytes 2359296 | tf_op jit(solution)/shard_map/all_to_all | solution.py:346
  58.0 21.9 %collective-permute-start = (bf16[416,256]{1,0:T(8,128)(2,1)}, bf16[416,256]{1,0:T(8,128)(2,1)S(1)}, u32[]{:S(2)}, u32[]{:S(2)}) collective-permute-start(bf16[416,256]{1,0:T(8,128)(2,1)} %get-tuple-element.61), channel_id=1, source_target_pairs={{0,32},{32,64},{64,96},{96,0},{1,33},{33,65},{65,97},{97,1},{2,34}... | collective-permute-start | bytes 638984 | tf_op jit(solution)/shard_map/ppermute | solution.py:349
  59.9 20.0 %collective-permute-start.1 = (bf16[416,256]{1,0:T(8,128)(2,1)}, bf16[416,256]{1,0:T(8,128)(2,1)S(1)}, u32[]{:S(2)}, u32[]{:S(2)}) collective-permute-start(bf16[416,256]{1,0:T(8,128)(2,1)} %get-tuple-element.62), channel_id=1, source_target_pairs={{0,64},{32,96},{64,0},{96,32},{1,65},{33,97},{65,1},{97,33},{2,66}... | collective-permute-start | bytes 638984 | tf_op jit(solution)/shard_map/ppermute | solution.py:349
  63.5 16.4 %collective-permute-start.2 = (bf16[416,256]{1,0:T(8,128)(2,1)S(1)}, bf16[416,256]{1,0:T(8,128)(2,1)S(1)}, u32[]{:S(2)}, u32[]{:S(2)}) collective-permute-start(bf16[416,256]{1,0:T(8,128)(2,1)S(1)} %get-tuple-element.63), channel_id=1, source_target_pairs={{0,96},{32,0},{64,32},{96,64},{1,97},{33,1},{65,33},{97,65},{2,98}... | collective-permute-start | bytes 638984 | tf_op jit(solution)/shard_map/ppermute | solution.py:349
  79.9 12.3 %copy-start.3 = (s32[3]{0:T(128)S(1)}, s32[3]{0:T(128)}, u32[]{:S(2)}) copy-start(s32[3]{0:T(128)} %copy-done.2) | copy-start | bytes 40
  79.9 13.0 %copy-start.5 = (bf16[208,256]{1,0:T(8,128)(2,1)S(1)}, bf16[208,256]{1,0:T(8,128)(2,1)}, u32[]{:S(2)}) copy-start(bf16[208,256]{1,0:T(8,128)(2,1)} %get-tuple-element.82) | copy-start | bytes 319492
  79.9 15.8 %copy-start.4 = (bf16[208,256]{1,0:T(8,128)(2,1)S(1)}, bf16[208,256]{1,0:T(8,128)(2,1)}, u32[]{:S(2)}) copy-start(bf16[208,256]{1,0:T(8,128)(2,1)} %get-tuple-element.83) | copy-start | bytes 319492
  79.9 21.3 %copy-start = (bf16[128,144]{1,0:T(8,128)(2,1)S(1)}, bf16[128,144]{1,0:T(8,128)(2,1)}, u32[]{:S(2)}) copy-start(bf16[128,144]{1,0:T(8,128)(2,1)} %get-tuple-element.45.turned_ref) | copy-start | bytes 110596
  80.0 26.6 %all-to-all-start.2 = ((bf16[32,72,256]{2,1,0:T(8,128)(2,1)}), bf16[32,72,256]{2,1,0:T(8,128)(2,1)S(1)}, u32[]{:S(2)}, u32[]{:S(2)}) async-start(bf16[32,72,256]{2,1,0:T(8,128)(2,1)} %get-tuple-element.64), calls=%async_computation.2 | async-start | bytes 2359296 | tf_op jit(solution)/shard_map/all_to_all | solution.py:352
  87.4 15.6 %copy-start.1 = (bf16[208,256]{1,0:T(8,128)(2,1)S(1)}, bf16[208,256]{1,0:T(8,128)(2,1)}, u32[]{:S(2)}) copy-start(bf16[208,256]{1,0:T(8,128)(2,1)} %get-tuple-element.76.refs_2_) | copy-start | bytes 319492
  87.4 5.5 %collective-permute-start.4 = (bf16[208,256]{1,0:T(8,128)(2,1)}, bf16[208,256]{1,0:T(8,128)(2,1)S(1)}, u32[]{:S(2)}, u32[]{:S(2)}) collective-permute-start(bf16[208,256]{1,0:T(8,128)(2,1)} %get-tuple-element.77), channel_id=1, source_target_pairs={{0,16},{16,0},{32,48},{48,32},{64,80},{80,64},{96,112},{112,96},{1... | collective-permute-start | bytes 319496 | tf_op jit(solution)/shard_map/ppermute | solution.py:356
  87.8 8.0 %collective-permute-start.5 = (bf16[208,256]{1,0:T(8,128)(2,1)}, bf16[208,256]{1,0:T(8,128)(2,1)S(1)}, u32[]{:S(2)}, u32[]{:S(2)}) collective-permute-start(bf16[208,256]{1,0:T(8,128)(2,1)} %get-tuple-element.78), channel_id=1, source_target_pairs={{0,32},{16,48},{32,64},{48,80},{64,96},{80,112},{96,0},{112,16},{1... | collective-permute-start | bytes 319496 | tf_op jit(solution)/shard_map/ppermute | solution.py:356
  88.8 7.5 %collective-permute-start.6 = (bf16[208,256]{1,0:T(8,128)(2,1)}, bf16[208,256]{1,0:T(8,128)(2,1)S(1)}, u32[]{:S(2)}, u32[]{:S(2)}) collective-permute-start(bf16[208,256]{1,0:T(8,128)(2,1)} %get-tuple-element.79), channel_id=1, source_target_pairs={{0,48},{16,32},{32,80},{48,64},{64,112},{80,96},{96,16},{112,0},{1... | collective-permute-start | bytes 319496 | tf_op jit(solution)/shard_map/ppermute | solution.py:356
  88.8 14.1 %collective-permute-start.7 = (bf16[208,256]{1,0:T(8,128)(2,1)}, bf16[208,256]{1,0:T(8,128)(2,1)S(1)}, u32[]{:S(2)}, u32[]{:S(2)}) collective-permute-start(bf16[208,256]{1,0:T(8,128)(2,1)} %get-tuple-element.80), channel_id=1, source_target_pairs={{0,64},{16,80},{32,96},{48,112},{64,0},{80,16},{96,32},{112,48},{1... | collective-permute-start | bytes 319496 | tf_op jit(solution)/shard_map/ppermute | solution.py:356
  92.1 10.9 %collective-permute-start.8 = (bf16[208,256]{1,0:T(8,128)(2,1)}, bf16[208,256]{1,0:T(8,128)(2,1)S(1)}, u32[]{:S(2)}, u32[]{:S(2)}) collective-permute-start(bf16[208,256]{1,0:T(8,128)(2,1)} %get-tuple-element.81), channel_id=1, source_target_pairs={{0,80},{16,64},{32,112},{48,96},{64,16},{80,0},{96,48},{112,32},{1... | collective-permute-start | bytes 319496 | tf_op jit(solution)/shard_map/ppermute | solution.py:356
  92.9 10.0 %collective-permute-start.9 = (bf16[208,256]{1,0:T(8,128)(2,1)S(1)}, bf16[208,256]{1,0:T(8,128)(2,1)S(1)}, u32[]{:S(2)}, u32[]{:S(2)}) collective-permute-start(bf16[208,256]{1,0:T(8,128)(2,1)S(1)} %copy-done.5), channel_id=1, source_target_pairs={{0,96},{16,112},{32,0},{48,16},{64,32},{80,48},{96,64},{112,80},{1... | collective-permute-start | bytes 319496 | tf_op jit(solution)/shard_map/ppermute | solution.py:356
  95.8 7.2 %collective-permute-start.10 = (bf16[208,256]{1,0:T(8,128)(2,1)S(1)}, bf16[208,256]{1,0:T(8,128)(2,1)S(1)}, u32[]{:S(2)}, u32[]{:S(2)}) collective-permute-start(bf16[208,256]{1,0:T(8,128)(2,1)S(1)} %copy-done.4), channel_id=1, source_target_pairs={{0,112},{16,96},{32,16},{48,0},{64,48},{80,32},{96,80},{112,64},{1... | collective-permute-start | bytes 319496 | tf_op jit(solution)/shard_map/ppermute | solution.py:356
  96.3 6.6 %collective-permute-start.3 = (bf16[208,256]{1,0:T(8,128)(2,1)S(1)}, bf16[208,256]{1,0:T(8,128)(2,1)S(1)}, u32[]{:S(2)}, u32[]{:S(2)}) collective-permute-start(bf16[208,256]{1,0:T(8,128)(2,1)S(1)} %get-tuple-element.75), channel_id=1, source_target_pairs={{0,16},{16,0},{1,17},{17,1},{2,18},{18,2},{3,19},{19,3},{4,20},{20... | collective-permute-start | bytes 319496 | tf_op jit(solution)/shard_map/ppermute | solution.py:358

commit v4 on v3

--- a/solution.py
+++ b/solution.py
@@ -344,9 +344,13 @@
     rows = [rows, exchange(later)]
     back, *shares = attend(info, rows[0], *tiles[0], depth, 1)
     first_back = exchange(back)
-    shares, rows = lax.optimization_barrier((shares, rows))
-    for i in range(1, depth):
-        shares[i] = lax.ppermute(shares[i], "z", [(z, (z + i) % depth) for z in range(depth)])
+    along_z = lambda share, i: lax.ppermute(share, "z", [(z, (z + i) % depth) for z in range(depth)])
+    early, late = ((1, 3), (2,))
+    for i in early:
+        shares[i] = along_z(shares[i], i)
+    waiting, rows = lax.optimization_barrier(([shares[i] for i in late], rows))
+    for i, share in zip(late, waiting):
+        shares[i] = along_z(share, i)
     back, *later = attend(info, rows[1], *tiles[1], depth, 2)
     back, shares = lax.optimization_barrier((back, shares))
     second_back = exchange(back)

time: 109 us -> 107 us (0.982)
  waiting for transfers between devices: 20.5 us -> 18.3 us
    all_to_all x1, waiting for transfers between devices: 5.05 us -> 1 us  [local(): rows = [rows, exchange(later)]]
    all_to_all x1, starting transfers between devices: 3.94 us -> 6.24 us  [local(): first_back = exchange(back)]
    all_to_all x1, waiting for transfers between devices: 0.01 us -> 1.8 us  [local(): first_back = exchange(back)]
    all_to_all x1, starting transfers between devices: 7.45 us -> 5.71 us  [local(): second_back = exchange(back)]
  transfers between devices with their start and end apart: 15 -> 15, of which waited for: 3 -> 4; matrix products, arithmetic and copies ran while one was open for 2% -> 2% of each run, Pallas kernels for 33% -> 34%
where the time goes in v4:
time: 107 us; the launch traced here: 106 us
  starting transfers between devices  43.2 us (40%)
  Pallas kernels  40.6 us (38%)
  waiting for transfers between devices  18.3 us (17%)
  local copies, waits for them, and re-layouts  2.47 us (2%)
  between operations  1.44 us (1%)
    pallas_call x2, Pallas kernels, attend(): pl.pallas_call(functools.partial(attend_kernel, ways=ways, depth=depth),...  29.5 us
    all_to_all x1, waiting for transfers between devices, local(): exchange(sent)  13.5 us
    ppermute x7, starting transfers between devices, local(): later[i] = lax.ppermute(later[i], ('z', 'core'), pairs)  8.22 us
    all_to_all x1, starting transfers between devices, local(): exchange(sent)  7.41 us
    all_to_all x1, starting transfers between devices, local(): first_back = exchange(back)  6.24 us
    ppermute x3, starting transfers between devices, local(): lax.ppermute(share, 'z', [(z, (z + i) % depth) for z in range(depth)])  5.98 us
    all_to_all x1, starting transfers between devices, local(): second_back = exchange(back)  5.71 us
    pallas_call x2, Pallas kernels, dispatch(): pl.pallas_call(route_kernel if part == 0 else dispatch_kernel, grid=(2,),...  5.49 us
  transfers between devices with their start and end apart: 15, of which 4 were waited for; matrix products, arithmetic and copies ran while one was open for 2% of the time, Pallas kernels for 34%

profile of v4, /device:TPU:0, one launch (start us, length us, event | category | flops | bytes accessed | tf_op | source)
XLA Modules:
  0.0 106.0 jit_solution(11838945785898409120)
XLA Ops:
  0.6 3.0 %dispatch.2 = (bf16[32,72,256]{2,1,0:T(8,128)(2,1)}, bf16[144,128]{1,0:T(8,128)(2,1)}, bf16[128,144]{1,0:T(8,128)(2,1)}) custom-call(s32[1,128]{1,0:T(1,128)} %bitcast.3, bf16[128,4096]{1,0:T(8,128)(2,1)} %query_ref.3, bf16[128,4096]{1,0:T(8,128)(2,1)} %grad_ref.3), custom_call_target="tpu_custom_call" | custom-call | flops 1000000000 | bytes 3000000 | tf_op jit(solution)/shard_map/dispatch/pallas_call | solution.py:78
  3.6 7.4 %all-to-all-start = ((bf16[32,72,256]{2,1,0:T(8,128)(2,1)}), bf16[32,72,256]{2,1,0:T(8,128)(2,1)S(1)}, u32[]{:S(2)}, u32[]{:S(2)}) async-start(bf16[32,72,256]{2,1,0:T(8,128)(2,1)} %get-tuple-element.43), calls=%async_computation | async-start | bytes 2359296 | tf_op jit(solution)/shard_map/all_to_all | solution.py:343
  11.7 2.5 %dispatch.3 = bf16[32,72,256]{2,1,0:T(8,128)(2,1)} custom-call(bf16[144,128]{1,0:T(8,128)(2,1)} %get-tuple-element.44.slots_ref, bf16[128,4096]{1,0:T(8,128)(2,1)} %query_ref.3, bf16[128,4096]{1,0:T(8,128)(2,1)} %grad_ref.3), custom_call_target="tpu_custom_call" | custom-call | flops 1000000000 | bytes 3000000 | tf_op jit(solution)/shard_map/dispatch/pallas_call | solution.py:78
  14.2 0.1 pad_add_fusion.info
  14.3 0.0 copy-start.2
  14.3 2.4 %constant_dynamic-slice_fusion = (bf16[1,1664,128]{2,1,0:T(8,128)(2,1)}, bf16[1,1664,128]{2,1,0:T(8,128)(2,1)S(1)}, bf16[1,1664,128]{2,1,0:T(8,128)(2,1)S(1)}, bf16[1,1664,128]{2,1,0:T(8,128)(2,1)}) fusion(bf16[1,1664,512]{2,1,0:T(8,128)(2,1)} %param.9, s32[]{:T(128)S(6)} %select_n.9, s32[]{:T(128)S(6)} %select_n.8, bf16[1,1664,512]{2,1,0:T(8,128)(2,1)} %param.8), kind=kLoop, calls=%fused_computation | loop fusion | bytes 3407880 | tf_op jit(solution)/shard_map/dynamic_slice | solution.py:340
  16.7 13.5 %all-to-all-done.rows_ref = bf16[32,72,256]{2,1,0:T(8,128)(2,1)S(1)} async-done(((bf16[32,72,256]{2,1,0:T(8,128)(2,1)}), bf16[32,72,256]{2,1,0:T(8,128)(2,1)S(1)}, u32[]{:S(2)}, u32[]{:S(2)}) %all-to-all-start) | async-done | bytes 1179680 | tf_op jit(solution)/shard_map/all_to_all | solution.py:343
  30.2 4.7 %all-to-all-start.1 = ((bf16[32,72,256]{2,1,0:T(8,128)(2,1)}), bf16[32,72,256]{2,1,0:T(8,128)(2,1)}, u32[]{:S(2)}, u32[]{:S(2)}) async-start(bf16[32,72,256]{2,1,0:T(8,128)(2,1)} %dispatch.3), calls=%async_computation.1 | async-start | bytes 2359296 | tf_op jit(solution)/shard_map/all_to_all | solution.py:344
  34.8 0.0 copy-done.2
  34.9 14.1 %attend.2 = (bf16[32,72,256]{2,1,0:T(8,128)(2,1)}, bf16[416,256]{1,0:T(8,128)(2,1)S(1)}, bf16[416,256]{1,0:T(8,128)(2,1)}, bf16[416,256]{1,0:T(8,128)(2,1)S(1)}, bf16[416,256]{1,0:T(8,128)(2,1)}) custom-call(s32[3]{0:T(128)S(1)} %pad_add_fusion.info, bf16[32,72,256]{2,1,0:T(8,128)(2,1)S(1)} %all-to-all-done.rows_ref, ...), custom_call_target="tpu_custom_call" | custom-call | flops 29444014080 | bytes 4000000 | tf_op jit(solution)/shard_map/attend/pallas_call | solution.py:236
  49.0 1.9 %collective-permute-start = (bf16[416,256]{1,0:T(8,128)(2,1)}, bf16[416,256]{1,0:T(8,128)(2,1)S(1)}, u32[]{:S(2)}, u32[]{:S(2)}) collective-permute-start(bf16[416,256]{1,0:T(8,128)(2,1)} %get-tuple-element.55), channel_id=1, source_target_pairs={{0,32},{32,64},{64,96},{96,0},{1,33},{33,65},{65,97},{97,1},{2,34}... | collective-permute-start | bytes 638984 | tf_op jit(solution)/shard_map/ppermute | solution.py:347
  50.9 2.1 %collective-permute-start.2 = (bf16[416,256]{1,0:T(8,128)(2,1)}, bf16[416,256]{1,0:T(8,128)(2,1)S(1)}, u32[]{:S(2)}, u32[]{:S(2)}) collective-permute-start(bf16[416,256]{1,0:T(8,128)(2,1)} %get-tuple-element.57), channel_id=1, source_target_pairs={{0,96},{32,0},{64,32},{96,64},{1,97},{33,1},{65,33},{97,65},{2,98}... | collective-permute-start | bytes 638984 | tf_op jit(solution)/shard_map/ppermute | solution.py:347
  53.0 1.0 all-to-all-done.1.rows_ref
  54.0 6.2 %all-to-all-start.3 = ((bf16[32,72,256]{2,1,0:T(8,128)(2,1)}), bf16[32,72,256]{2,1,0:T(8,128)(2,1)S(1)}, u32[]{:S(2)}, u32[]{:S(2)}) async-start(bf16[32,72,256]{2,1,0:T(8,128)(2,1)} %get-tuple-element.59), calls=%async_computation.3 | async-start | bytes 2359296 | tf_op jit(solution)/shard_map/all_to_all | solution.py:346
  60.3 1.9 %collective-permute-start.1 = (bf16[416,256]{1,0:T(8,128)(2,1)S(1)}, bf16[416,256]{1,0:T(8,128)(2,1)S(1)}, u32[]{:S(2)}, u32[]{:S(2)}) collective-permute-start(bf16[416,256]{1,0:T(8,128)(2,1)S(1)} %get-tuple-element.56), channel_id=1, source_target_pairs={{0,64},{32,96},{64,0},{96,32},{1,65},{33,97},{65,1},{97,33},{2,66}... | collective-permute-start | bytes 638984 | tf_op jit(solution)/shard_map/ppermute | solution.py:347
  62.2 15.4 %attend.3 = (bf16[32,72,256]{2,1,0:T(8,128)(2,1)}, bf16[208,256]{1,0:T(8,128)(2,1)}, bf16[208,256]{1,0:T(8,128)(2,1)}, bf16[208,256]{1,0:T(8,128)(2,1)}, bf16[20...) custom-call(s32[3]{0:T(128)} %copy-done.2, ...), custom_call_target="tpu_custom_call" | custom-call | flops 29444014080 | bytes 4000000 | tf_op jit(solution)/shard_map/attend/pallas_call | solution.py:236
  77.6 0.0 collective-permute-done.refs_1_
  77.6 0.0 collective-permute-done.2.refs_3_
  77.6 0.0 collective-permute-done.1.refs_2_
  77.6 0.0 copy-start.3
  77.6 0.0 copy-start.5
  77.6 0.0 copy-start.4
  77.6 0.0 copy-start
  77.6 1.8 %all-to-all-done.3.back_ref = bf16[32,72,256]{2,1,0:T(8,128)(2,1)S(1)} async-done(((bf16[32,72,256]{2,1,0:T(8,128)(2,1)}), bf16[32,72,256]{2,1,0:T(8,128)(2,1)S(1)}, u32[]{:S(2)}, u32[]{:S(2)}) %all-to-all-start.3) | async-done | bytes 1179680 | tf_op jit(solution)/shard_map/all_to_all | solution.py:346
  79.4 5.7 %all-to-all-start.2 = ((bf16[32,72,256]{2,1,0:T(8,128)(2,1)}), bf16[32,72,256]{2,1,0:T(8,128)(2,1)S(1)}, u32[]{:S(2)}, u32[]{:S(2)}) async-start(bf16[32,72,256]{2,1,0:T(8,128)(2,1)} %get-tuple-element.58), calls=%async_computation.2 | async-start | bytes 2359296 | tf_op jit(solution)/shard_map/all_to_all | solution.py:356
  85.1 0.0 copy-start.1
  85.2 0.4 collective-permute-start.4
  85.5 1.0 collective-permute-start.5
  86.5 0.2 collective-permute-start.6
  86.7 3.1 %collective-permute-start.7 = (bf16[208,256]{1,0:T(8,128)(2,1)}, bf16[208,256]{1,0:T(8,128)(2,1)S(1)}, u32[]{:S(2)}, u32[]{:S(2)}) collective-permute-start(bf16[208,256]{1,0:T(8,128)(2,1)} %get-tuple-element.74), channel_id=1, source_target_pairs={{0,64},{16,80},{32,96},{48,112},{64,0},{80,16},{96,32},{112,48},{1... | collective-permute-start | bytes 319496 | tf_op jit(solution)/shard_map/ppermute | solution.py:360
  89.8 0.4 collective-permute-start.8
  90.1 0.0 copy-done.3
  90.1 0.6 add_shares.1
  90.8 0.0 collective-permute-done.4.refs_3_
  90.8 0.0 copy-done.5
  90.8 2.7 %collective-permute-start.9 = (bf16[208,256]{1,0:T(8,128)(2,1)S(1)}, bf16[208,256]{1,0:T(8,128)(2,1)S(1)}, u32[]{:S(2)}, u32[]{:S(2)}) collective-permute-start(bf16[208,256]{1,0:T(8,128)(2,1)S(1)} %copy-done.5), channel_id=1, source_target_pairs={{0,96},{16,112},{32,0},{48,16},{64,32},{80,48},{96,64},{112,80},{1... | collective-permute-start | bytes 319496 | tf_op jit(solution)/shard_map/ppermute | solution.py:360
  93.5 0.0 collective-permute-done.5.refs_4_
  93.5 0.0 copy-done.4
  93.5 0.6 collective-permute-start.10
  94.1 0.0 collective-permute-done.6.refs_5_
  94.1 4.9 %collective-permute-start.3 = (bf16[208,256]{1,0:T(8,128)(2,1)S(1)}, bf16[208,256]{1,0:T(8,128)(2,1)S(1)}, u32[]{:S(2)}, u32[]{:S(2)}) collective-permute-start(bf16[208,256]{1,0:T(8,128)(2,1)S(1)} %get-tuple-element.69), channel_id=1, source_target_pairs={{0,16},{16,0},{1,17},{17,1},{2,18},{18,2},{3,19},{19,3},{4,20},{20... | collective-permute-start | bytes 319496 | tf_op jit(solution)/shard_map/ppermute | solution.py:362
  99.0 0.0 copy-done
  99.0 1.7 %combine.2 = (bf16[128,4096]{1,0:T(8,128)(2,1)}, bf16[128,4096]{1,0:T(8,128)(2,1)}) custom-call(bf16[128,144]{1,0:T(8,128)(2,1)S(1)} %copy-done, bf16[32,72,256]{2,1,0:T(8,128)(2,1)S(1)} %all-to-all-done.3.back_ref), custom_call_target="tpu_custom_call" | custom-call | flops 1000000 | bytes 100000 | tf_op jit(solution)/shard_map/combine/pallas_call | solution.py:117
  100.7 0.0 collective-permute-done.7.refs_6_
  100.7 0.0 collective-permute-done.8.refs_7_
  100.7 0.0 collective-permute-done.9.refs_8_
  100.7 0.0 collective-permute-done.10.refs_9_
  100.7 0.0 collective-permute-done.3.refs_1_
  100.7 0.0 copy-done.1
  100.7 1.6 %place.1 = (f32[1,208,512]{2,1,0:T(8,128)}, f32[1,208,512]{2,1,0:T(8,128)}) custom-call(s32[3]{0:T(128)S(1)} %copy-done.3, f32[208,256]{1,0:T(8,128)S(1)} %get-tuple-element.68.refs_0_, bf16[208,256]{1,0:T(8,128)(2,1)S(1)} %collective-permute-done.3.refs_1_, bf16[208,256]{1,0:T(8,128)(2,1)S(1)} %copy-done.1, ...), custom_call_target="tpu_custom_call" | custom-call | flops 1000000 | bytes 100000 | tf_op jit(solution)/shard_map/place/pallas_call | solution.py:313
  102.3 2.0 %all-to-all-done.2.back_ref = bf16[32,72,256]{2,1,0:T(8,128)(2,1)S(1)} async-done(((bf16[32,72,256]{2,1,0:T(8,128)(2,1)}), bf16[32,72,256]{2,1,0:T(8,128)(2,1)S(1)}, u32[]{:S(2)}, u32[]{:S(2)}) %all-to-all-start.2) | async-done | bytes 1179680 | tf_op jit(solution)/shard_map/all_to_all | solution.py:356
  104.3 1.7 %combine.3 = (bf16[128,4096]{1,0:T(8,128)(2,1)}, bf16[128,4096]{1,0:T(8,128)(2,1)}) custom-call(bf16[128,144]{1,0:T(8,128)(2,1)S(1)} %copy-done, bf16[32,72,256]{2,1,0:T(8,128)(2,1)S(1)} %all-to-all-done.2.back_ref, bf16[128,4096]{1,0:T(8,128)(2,1)} %get-tuple-element.60.refs_0_, ...), custom_call_target="tpu_custom_call", output_to_operand_aliasing={{0}: (2, {}), {1}: (3, {})} | custom-call | flops 1000000 | bytes 100000 | tf_op jit(solution)/shard_map/combine/pallas_call | solution.py:117
Async XLA Ops:
  3.6 26.6 %all-to-all-start = ((bf16[32,72,256]{2,1,0:T(8,128)(2,1)}), bf16[32,72,256]{2,1,0:T(8,128)(2,1)S(1)}, u32[]{:S(2)}, u32[]{:S(2)}) async-start(bf16[32,72,256]{2,1,0:T(8,128)(2,1)} %get-tuple-element.43), calls=%async_computation | async-start | bytes 2359296 | tf_op jit(solution)/shard_map/all_to_all | solution.py:343
  14.3 20.6 %copy-start.2 = (s32[3]{0:T(128)}, s32[3]{0:T(128)S(1)}, u32[]{:S(2)}) copy-start(s32[3]{0:T(128)S(1)} %pad_add_fusion.info) | copy-start | bytes 40
  30.2 23.8 %all-to-all-start.1 = ((bf16[32,72,256]{2,1,0:T(8,128)(2,1)}), bf16[32,72,256]{2,1,0:T(8,128)(2,1)}, u32[]{:S(2)}, u32[]{:S(2)}) async-start(bf16[32,72,256]{2,1,0:T(8,128)(2,1)} %dispatch.3), calls=%async_computation.1 | async-start | bytes 2359296 | tf_op jit(solution)/shard_map/all_to_all | solution.py:344
  49.0 28.6 %collective-permute-start = (bf16[416,256]{1,0:T(8,128)(2,1)}, bf16[416,256]{1,0:T(8,128)(2,1)S(1)}, u32[]{:S(2)}, u32[]{:S(2)}) collective-permute-start(bf16[416,256]{1,0:T(8,128)(2,1)} %get-tuple-element.55), channel_id=1, source_target_pairs={{0,32},{32,64},{64,96},{96,0},{1,33},{33,65},{65,97},{97,1},{2,34}... | collective-permute-start | bytes 638984 | tf_op jit(solution)/shard_map/ppermute | solution.py:347
  50.9 26.7 %collective-permute-start.2 = (bf16[416,256]{1,0:T(8,128)(2,1)}, bf16[416,256]{1,0:T(8,128)(2,1)S(1)}, u32[]{:S(2)}, u32[]{:S(2)}) collective-permute-start(bf16[416,256]{1,0:T(8,128)(2,1)} %get-tuple-element.57), channel_id=1, source_target_pairs={{0,96},{32,0},{64,32},{96,64},{1,97},{33,1},{65,33},{97,65},{2,98}... | collective-permute-start | bytes 638984 | tf_op jit(solution)/shard_map/ppermute | solution.py:347
  54.0 25.4 %all-to-all-start.3 = ((bf16[32,72,256]{2,1,0:T(8,128)(2,1)}), bf16[32,72,256]{2,1,0:T(8,128)(2,1)S(1)}, u32[]{:S(2)}, u32[]{:S(2)}) async-start(bf16[32,72,256]{2,1,0:T(8,128)(2,1)} %get-tuple-element.59), calls=%async_computation.3 | async-start | bytes 2359296 | tf_op jit(solution)/shard_map/all_to_all | solution.py:346
  60.3 17.3 %collective-permute-start.1 = (bf16[416,256]{1,0:T(8,128)(2,1)S(1)}, bf16[416,256]{1,0:T(8,128)(2,1)S(1)}, u32[]{:S(2)}, u32[]{:S(2)}) collective-permute-start(bf16[416,256]{1,0:T(8,128)(2,1)S(1)} %get-tuple-element.56), channel_id=1, source_target_pairs={{0,64},{32,96},{64,0},{96,32},{1,65},{33,97},{65,1},{97,33},{2,66}... | collective-permute-start | bytes 638984 | tf_op jit(solution)/shard_map/ppermute | solution.py:347
  77.6 12.5 %copy-start.3 = (s32[3]{0:T(128)S(1)}, s32[3]{0:T(128)}, u32[]{:S(2)}) copy-start(s32[3]{0:T(128)} %copy-done.2) | copy-start | bytes 40
  77.6 13.2 %copy-start.5 = (bf16[208,256]{1,0:T(8,128)(2,1)S(1)}, bf16[208,256]{1,0:T(8,128)(2,1)}, u32[]{:S(2)}) copy-start(bf16[208,256]{1,0:T(8,128)(2,1)} %get-tuple-element.76) | copy-start | bytes 319492
  77.6 15.9 %copy-start.4 = (bf16[208,256]{1,0:T(8,128)(2,1)S(1)}, bf16[208,256]{1,0:T(8,128)(2,1)}, u32[]{:S(2)}) copy-start(bf16[208,256]{1,0:T(8,128)(2,1)} %get-tuple-element.77) | copy-start | bytes 319492
  77.6 21.4 %copy-start = (bf16[128,144]{1,0:T(8,128)(2,1)S(1)}, bf16[128,144]{1,0:T(8,128)(2,1)}, u32[]{:S(2)}) copy-start(bf16[128,144]{1,0:T(8,128)(2,1)} %get-tuple-element.42.turned_ref) | copy-start | bytes 110596
  79.4 24.9 %all-to-all-start.2 = ((bf16[32,72,256]{2,1,0:T(8,128)(2,1)}), bf16[32,72,256]{2,1,0:T(8,128)(2,1)S(1)}, u32[]{:S(2)}, u32[]{:S(2)}) async-start(bf16[32,72,256]{2,1,0:T(8,128)(2,1)} %get-tuple-element.58), calls=%async_computation.2 | async-start | bytes 2359296 | tf_op jit(solution)/shard_map/all_to_all | solution.py:356
  85.1 15.6 %copy-start.1 = (bf16[208,256]{1,0:T(8,128)(2,1)S(1)}, bf16[208,256]{1,0:T(8,128)(2,1)}, u32[]{:S(2)}) copy-start(bf16[208,256]{1,0:T(8,128)(2,1)} %get-tuple-element.70.refs_2_) | copy-start | bytes 319492
  85.2 5.6 %collective-permute-start.4 = (bf16[208,256]{1,0:T(8,128)(2,1)}, bf16[208,256]{1,0:T(8,128)(2,1)S(1)}, u32[]{:S(2)}, u32[]{:S(2)}) collective-permute-start(bf16[208,256]{1,0:T(8,128)(2,1)} %get-tuple-element.71), channel_id=1, source_target_pairs={{0,16},{16,0},{32,48},{48,32},{64,80},{80,64},{96,112},{112,96},{1... | collective-permute-start | bytes 319496 | tf_op jit(solution)/shard_map/ppermute | solution.py:360
  85.5 8.0 %collective-permute-start.5 = (bf16[208,256]{1,0:T(8,128)(2,1)}, bf16[208,256]{1,0:T(8,128)(2,1)S(1)}, u32[]{:S(2)}, u32[]{:S(2)}) collective-permute-start(bf16[208,256]{1,0:T(8,128)(2,1)} %get-tuple-element.72), channel_id=1, source_target_pairs={{0,32},{16,48},{32,64},{48,80},{64,96},{80,112},{96,0},{112,16},{1... | collective-permute-start | bytes 319496 | tf_op jit(solution)/shard_map/ppermute | solution.py:360
  86.5 7.5 %collective-permute-start.6 = (bf16[208,256]{1,0:T(8,128)(2,1)}, bf16[208,256]{1,0:T(8,128)(2,1)S(1)}, u32[]{:S(2)}, u32[]{:S(2)}) collective-permute-start(bf16[208,256]{1,0:T(8,128)(2,1)} %get-tuple-element.73), channel_id=1, source_target_pairs={{0,48},{16,32},{32,80},{48,64},{64,112},{80,96},{96,16},{112,0},{1... | collective-permute-start | bytes 319496 | tf_op jit(solution)/shard_map/ppermute | solution.py:360
  86.7 14.0 %collective-permute-start.7 = (bf16[208,256]{1,0:T(8,128)(2,1)}, bf16[208,256]{1,0:T(8,128)(2,1)S(1)}, u32[]{:S(2)}, u32[]{:S(2)}) collective-permute-start(bf16[208,256]{1,0:T(8,128)(2,1)} %get-tuple-element.74), channel_id=1, source_target_pairs={{0,64},{16,80},{32,96},{48,112},{64,0},{80,16},{96,32},{112,48},{1... | collective-permute-start | bytes 319496 | tf_op jit(solution)/shard_map/ppermute | solution.py:360
  89.8 10.9 %collective-permute-start.8 = (bf16[208,256]{1,0:T(8,128)(2,1)}, bf16[208,256]{1,0:T(8,128)(2,1)S(1)}, u32[]{:S(2)}, u32[]{:S(2)}) collective-permute-start(bf16[208,256]{1,0:T(8,128)(2,1)} %get-tuple-element.75), channel_id=1, source_target_pairs={{0,80},{16,64},{32,112},{48,96},{64,16},{80,0},{96,48},{112,32},{1... | collective-permute-start | bytes 319496 | tf_op jit(solution)/shard_map/ppermute | solution.py:360
  90.8 9.9 %collective-permute-start.9 = (bf16[208,256]{1,0:T(8,128)(2,1)S(1)}, bf16[208,256]{1,0:T(8,128)(2,1)S(1)}, u32[]{:S(2)}, u32[]{:S(2)}) collective-permute-start(bf16[208,256]{1,0:T(8,128)(2,1)S(1)} %copy-done.5), channel_id=1, source_target_pairs={{0,96},{16,112},{32,0},{48,16},{64,32},{80,48},{96,64},{112,80},{1... | collective-permute-start | bytes 319496 | tf_op jit(solution)/shard_map/ppermute | solution.py:360
  93.5 7.2 %collective-permute-start.10 = (bf16[208,256]{1,0:T(8,128)(2,1)S(1)}, bf16[208,256]{1,0:T(8,128)(2,1)S(1)}, u32[]{:S(2)}, u32[]{:S(2)}) collective-permute-start(bf16[208,256]{1,0:T(8,128)(2,1)S(1)} %copy-done.4), channel_id=1, source_target_pairs={{0,112},{16,96},{32,16},{48,0},{64,48},{80,32},{96,80},{112,64},{1... | collective-permute-start | bytes 319496 | tf_op jit(solution)/shard_map/ppermute | solution.py:360
  94.1 6.6 %collective-permute-start.3 = (bf16[208,256]{1,0:T(8,128)(2,1)S(1)}, bf16[208,256]{1,0:T(8,128)(2,1)S(1)}, u32[]{:S(2)}, u32[]{:S(2)}) collective-permute-start(bf16[208,256]{1,0:T(8,128)(2,1)S(1)} %get-tuple-element.69), channel_id=1, source_target_pairs={{0,16},{16,0},{1,17},{17,1},{2,18},{18,2},{3,19},{19,3},{4,20},{20... | collective-permute-start | bytes 319496 | tf_op jit(solution)/shard_map/ppermute | solution.py:362

commit v5 on v4

--- a/solution.py
+++ b/solution.py
@@ -17,7 +17,7 @@
 ROWS_LAST = (((1,), (1,)), ((), ()))
 LIMIT = 60 * 2**20
 SMALL = 16 * 2**20
-ATTEND_LIMITS = (32 * 2**20, 56 * 2**20)
+ATTEND_LIMITS = (32 * 2**20, 32 * 2**20)
 WAYS = 9
 TURNS = (3, 5, 5)
 
@@ -255,8 +255,7 @@
             + [pltpu.VMEM((block_rows, patches), F32)] * TURNS[0]
             + [pltpu.VMEM((block_rows, patches), BF16)] * (TURNS[1] + TURNS[2]),
         ),
-        out_shape=[jax.ShapeDtypeStruct(rows.shape, BF16)]
-        + [jax.ShapeDtypeStruct((share, both), BF16)] * share_num,
+        out_shape=[pltpu.HBM(rows.shape, BF16)] + [pltpu.HBM((share, both), BF16)] * share_num,
         compiler_params=pltpu.CompilerParams(vmem_limit_bytes=ATTEND_LIMITS[split - 1]),
         cost_estimate=pl.CostEstimate(
             flops=60 * total * patches * width,

time: 107 us -> 106 us (level)
  starting transfers between devices: 43.2 us -> 41.2 us
  local copies, waits for them, and re-layouts: 2.47 us -> 3.85 us
    pallas_call x2, Pallas kernels: 29.5 us -> 27.6 us  [attend(): pl.pallas_call(functools.partial(attend_kernel, ways=ways, depth=depth),...]
    unnamed x12 -> x26, local copies, waits for them, and re-layouts: 0.02 us -> 1.41 us
  transfers between devices with their start and end apart: 15 -> 15, of which waited for: 4 -> 4; matrix products, arithmetic and copies ran while one was open for 2% -> 2% of each run, Pallas kernels for 34% -> 33%
where the time goes in v5:
time: 106 us; the launch traced here: 105 us
  starting transfers between devices  41.2 us (39%)
  Pallas kernels  39.6 us (37%)
  waiting for transfers between devices  18.8 us (18%)
  local copies, waits for them, and re-layouts  3.85 us (4%)
  between operations  1.43 us (1%)
    pallas_call x2, Pallas kernels, attend(): pl.pallas_call(functools.partial(attend_kernel, ways=ways, depth=depth),...  27.6 us
    all_to_all x1, waiting for transfers between devices, local(): exchange(sent)  13.5 us
    ppermute x7, starting transfers between devices, local(): later[i] = lax.ppermute(later[i], ('z', 'core'), pairs)  8.22 us
    all_to_all x1, starting transfers between devices, local(): exchange(sent)  7.41 us
    all_to_all x1, starting transfers between devices, local(): first_back = exchange(back)  6.16 us
    ppermute x3, starting transfers between devices, local(): lax.ppermute(share, 'z', [(z, (z + i) % depth) for z in range(depth)])  5.98 us
    all_to_all x1, starting transfers between devices, local(): second_back = exchange(back)  5.48 us
    pallas_call x2, Pallas kernels, dispatch(): pl.pallas_call(route_kernel if part == 0 else dispatch_kernel, grid=(2,),...  5.47 us
  transfers between devices with their start and end apart: 15, of which 4 were waited for; matrix products, arithmetic and copies ran while one was open for 2% of the time, Pallas kernels for 33%

profile of v5, /device:TPU:0, one launch (start us, length us, event | category | flops | bytes accessed | tf_op | source)
XLA Modules:
  0.0 104.9 jit_solution(6736361139998554800)
XLA Ops:
  0.6 2.9 %dispatch.2 = (bf16[32,72,256]{2,1,0:T(8,128)(2,1)}, bf16[144,128]{1,0:T(8,128)(2,1)}, bf16[128,144]{1,0:T(8,128)(2,1)}) custom-call(s32[1,128]{1,0:T(1,128)} %bitcast.3, bf16[128,4096]{1,0:T(8,128)(2,1)} %query_ref.3, bf16[128,4096]{1,0:T(8,128)(2,1)} %grad_ref.3), custom_call_target="tpu_custom_call" | custom-call | flops 1000000000 | bytes 3000000 | tf_op jit(solution)/shard_map/dispatch/pallas_call | solution.py:78
  3.6 7.4 %all-to-all-start = ((bf16[32,72,256]{2,1,0:T(8,128)(2,1)}), bf16[32,72,256]{2,1,0:T(8,128)(2,1)S(1)}, u32[]{:S(2)}, u32[]{:S(2)}) async-start(bf16[32,72,256]{2,1,0:T(8,128)(2,1)} %get-tuple-element.43), calls=%async_computation | async-start | bytes 2359296 | tf_op jit(solution)/shard_map/all_to_all | solution.py:342
  11.6 2.5 %dispatch.3 = bf16[32,72,256]{2,1,0:T(8,128)(2,1)} custom-call(bf16[144,128]{1,0:T(8,128)(2,1)} %get-tuple-element.44.slots_ref, bf16[128,4096]{1,0:T(8,128)(2,1)} %query_ref.3, bf16[128,4096]{1,0:T(8,128)(2,1)} %grad_ref.3), custom_call_target="tpu_custom_call" | custom-call | flops 1000000000 | bytes 3000000 | tf_op jit(solution)/shard_map/dispatch/pallas_call | solution.py:78
  14.2 0.1 pad_add_fusion.info
  14.2 2.4 %constant_dynamic-slice_fusion = (bf16[1,1664,128]{2,1,0:T(8,128)(2,1)}, bf16[1,1664,128]{2,1,0:T(8,128)(2,1)S(1)}, bf16[1,1664,128]{2,1,0:T(8,128)(2,1)S(1)}, bf16[1,1664,128]{2,1,0:T(8,128)(2,1)}) fusion(bf16[1,1664,512]{2,1,0:T(8,128)(2,1)} %param.9, s32[]{:T(128)S(6)} %select_n.9, s32[]{:T(128)S(6)} %select_n.8, bf16[1,1664,512]{2,1,0:T(8,128)(2,1)} %param.8), kind=kLoop, calls=%fused_computation | loop fusion | bytes 3407880 | tf_op jit(solution)/shard_map/dynamic_slice | solution.py:339
  16.7 13.5 %all-to-all-done.rows_ref = bf16[32,72,256]{2,1,0:T(8,128)(2,1)S(1)} async-done(((bf16[32,72,256]{2,1,0:T(8,128)(2,1)}), bf16[32,72,256]{2,1,0:T(8,128)(2,1)S(1)}, u32[]{:S(2)}, u32[]{:S(2)}) %all-to-all-start) | async-done | bytes 1179680 | tf_op jit(solution)/shard_map/all_to_all | solution.py:342
  30.1 3.9 %all-to-all-start.1 = ((bf16[32,72,256]{2,1,0:T(8,128)(2,1)}), bf16[32,72,256]{2,1,0:T(8,128)(2,1)S(1)}, u32[]{:S(2)}, u32[]{:S(2)}) async-start(bf16[32,72,256]{2,1,0:T(8,128)(2,1)} %dispatch.3), calls=%async_computation.1 | async-start | bytes 2359296 | tf_op jit(solution)/shard_map/all_to_all | solution.py:343
  34.1 13.8 %attend.2 = (bf16[32,72,256]{2,1,0:T(8,128)(2,1)}, bf16[416,256]{1,0:T(8,128)(2,1)}, bf16[416,256]{1,0:T(8,128)(2,1)}, bf16[416,256]{1,0:T(8,128)(2,1)}, bf16[416,256]{1,0:T(8,128)(2,1)}) custom-call(s32[3]{0:T(128)S(1)} %pad_add_fusion.info, bf16[32,72,256]{2,1,0:T(8,128)(2,1)S(1)} %all-to-all-done.rows_ref, ...), custom_call_target="tpu_custom_call" | custom-call | flops 29444014080 | bytes 4000000 | tf_op jit(solution)/shard_map/attend/pallas_call | solution.py:236
  47.9 1.9 %collective-permute-start = (bf16[416,256]{1,0:T(8,128)(2,1)}, bf16[416,256]{1,0:T(8,128)(2,1)S(1)}, u32[]{:S(2)}, u32[]{:S(2)}) collective-permute-start(bf16[416,256]{1,0:T(8,128)(2,1)} %get-tuple-element.55), channel_id=1, source_target_pairs={{0,32},{32,64},{64,96},{96,0},{1,33},{33,65},{65,97},{97,1},{2,34}... | collective-permute-start | bytes 638984 | tf_op jit(solution)/shard_map/ppermute | solution.py:346
  49.9 2.1 %collective-permute-start.2 = (bf16[416,256]{1,0:T(8,128)(2,1)}, bf16[416,256]{1,0:T(8,128)(2,1)}, u32[]{:S(2)}, u32[]{:S(2)}) collective-permute-start(bf16[416,256]{1,0:T(8,128)(2,1)} %get-tuple-element.57), channel_id=1, source_target_pairs={{0,96},{32,0},{64,32},{96,64},{1,97},{33,1},{65,33},{97,65},{2,98}... | collective-permute-start | bytes 638984 | tf_op jit(solution)/shard_map/ppermute | solution.py:346
  52.0 1.3 %all-to-all-done.1.rows_ref = bf16[32,72,256]{2,1,0:T(8,128)(2,1)S(1)} async-done(((bf16[32,72,256]{2,1,0:T(8,128)(2,1)}), bf16[32,72,256]{2,1,0:T(8,128)(2,1)S(1)}, u32[]{:S(2)}, u32[]{:S(2)}) %all-to-all-start.1) | async-done | bytes 1179680 | tf_op jit(solution)/shard_map/all_to_all | solution.py:343
  53.3 0.0 copy-start
  53.3 0.0 copy-start.1
  53.3 6.2 %all-to-all-start.3 = ((bf16[32,72,256]{2,1,0:T(8,128)(2,1)}), bf16[32,72,256]{2,1,0:T(8,128)(2,1)S(1)}, u32[]{:S(2)}, u32[]{:S(2)}) async-start(bf16[32,72,256]{2,1,0:T(8,128)(2,1)} %get-tuple-element.59), calls=%async_computation.3 | async-start | bytes 2359296 | tf_op jit(solution)/shard_map/all_to_all | solution.py:345
  59.4 1.9 %collective-permute-start.1 = (bf16[416,256]{1,0:T(8,128)(2,1)}, bf16[416,256]{1,0:T(8,128)(2,1)S(1)}, u32[]{:S(2)}, u32[]{:S(2)}) collective-permute-start(bf16[416,256]{1,0:T(8,128)(2,1)} %get-tuple-element.56), channel_id=1, source_target_pairs={{0,64},{32,96},{64,0},{96,32},{1,65},{33,97},{65,1},{97,33},{2,66}... | collective-permute-start | bytes 638984 | tf_op jit(solution)/shard_map/ppermute | solution.py:346
  61.4 0.0 copy-done
  61.4 0.0 copy-done.1
  61.4 13.8 %attend.3 = (bf16[32,72,256]{2,1,0:T(8,128)(2,1)}, bf16[208,256]{1,0:T(8,128)(2,1)}, bf16[208,256]{1,0:T(8,128)(2,1)}, bf16[208,256]{1,0:T(8,128)(2,1)}, bf16[20...) custom-call(s32[3]{0:T(128)S(1)} %pad_add_fusion.info, ...), custom_call_target="tpu_custom_call" | custom-call | flops 29444014080 | bytes 4000000 | tf_op jit(solution)/shard_map/attend/pallas_call | solution.py:236
  75.1 0.0 collective-permute-done.refs_1_
  75.1 0.0 copy-start.4
  75.1 0.7 copy-done.4
  75.8 0.0 collective-permute-done.2.refs_3_
  75.8 0.0 collective-permute-done.1.refs_2_
  75.8 0.0 copy-start.6
  75.8 0.7 copy-done.6
  76.5 0.0 copy-start.12
  76.5 0.0 copy-start.11
  76.5 0.0 copy-start.7
  76.5 0.0 copy-start.10
  76.5 0.0 copy-start.9
  76.5 0.0 copy-start.2
  76.6 2.0 %all-to-all-done.3.back_ref = bf16[32,72,256]{2,1,0:T(8,128)(2,1)S(1)} async-done(((bf16[32,72,256]{2,1,0:T(8,128)(2,1)}), bf16[32,72,256]{2,1,0:T(8,128)(2,1)S(1)}, u32[]{:S(2)}, u32[]{:S(2)}) %all-to-all-start.3) | async-done | bytes 1179680 | tf_op jit(solution)/shard_map/all_to_all | solution.py:345
  78.6 5.5 %all-to-all-start.2 = ((bf16[32,72,256]{2,1,0:T(8,128)(2,1)}), bf16[32,72,256]{2,1,0:T(8,128)(2,1)S(1)}, u32[]{:S(2)}, u32[]{:S(2)}) async-start(bf16[32,72,256]{2,1,0:T(8,128)(2,1)} %get-tuple-element.58), calls=%async_computation.2 | async-start | bytes 2359296 | tf_op jit(solution)/shard_map/all_to_all | solution.py:355
  84.1 0.0 copy-start.8
  84.1 0.4 collective-permute-start.4
  84.5 1.0 collective-permute-start.5
  85.5 0.2 collective-permute-start.6
  85.6 0.0 copy-done.12
  85.6 3.1 %collective-permute-start.7 = (bf16[208,256]{1,0:T(8,128)(2,1)S(1)}, bf16[208,256]{1,0:T(8,128)(2,1)S(1)}, u32[]{:S(2)}, u32[]{:S(2)}) collective-permute-start(bf16[208,256]{1,0:T(8,128)(2,1)S(1)} %copy-done.12), channel_id=1, source_target_pairs={{0,64},{16,80},{32,96},{48,112},{64,0},{80,16},{96,32},{112,48},{1... | collective-permute-start | bytes 319496 | tf_op jit(solution)/shard_map/ppermute | solution.py:359
  88.7 0.0 copy-done.11
  88.7 0.3 collective-permute-start.8
  89.1 0.0 copy-done.3
  89.1 0.0 copy-done.5
  89.1 0.0 copy-done.7
  89.1 1.6 %add_shares.1 = (f32[208,256]{1,0:T(8,128)S(1)}, bf16[208,256]{1,0:T(8,128)(2,1)S(1)}) custom-call(s32[3]{0:T(128)S(1)} %pad_add_fusion.info, bf16[416,256]{1,0:T(8,128)(2,1)S(1)} %copy-done.3, bf16[416,256]{1,0:T(8,128)(2,1)S(1)} %copy-done.5, bf16[416,256]{1,0:T(8,128)(2,1)S(1)} %copy-done.7, bf16[416,256]{1,0:T(8,128)(2,1)} %collective-permute-done.2.refs_3_), custom_call_target="tpu_custom_call" | custom-call | flops 1000000 | bytes 100000 | tf_op jit(solution)/shard_map/add_shares/pallas_call | solution.py:281
  90.7 0.0 collective-permute-done.4.refs_3_
  90.7 0.0 copy-done.10
  90.7 2.7 %collective-permute-start.9 = (bf16[208,256]{1,0:T(8,128)(2,1)S(1)}, bf16[208,256]{1,0:T(8,128)(2,1)S(1)}, u32[]{:S(2)}, u32[]{:S(2)}) collective-permute-start(bf16[208,256]{1,0:T(8,128)(2,1)S(1)} %copy-done.10), channel_id=1, source_target_pairs={{0,96},{16,112},{32,0},{48,16},{64,32},{80,48},{96,64},{112,80},{1... | collective-permute-start | bytes 319496 | tf_op jit(solution)/shard_map/ppermute | solution.py:359
  93.4 0.0 collective-permute-done.5.refs_4_
  93.4 0.0 copy-done.9
  93.4 0.6 collective-permute-start.10
  93.9 0.0 collective-permute-done.6.refs_5_
  93.9 4.0 %collective-permute-start.3 = (bf16[208,256]{1,0:T(8,128)(2,1)S(1)}, bf16[208,256]{1,0:T(8,128)(2,1)S(1)}, u32[]{:S(2)}, u32[]{:S(2)}) collective-permute-start(bf16[208,256]{1,0:T(8,128)(2,1)S(1)} %get-tuple-element.69), channel_id=1, source_target_pairs={{0,16},{16,0},{1,17},{17,1},{2,18},{18,2},{3,19},{19,3},{4,20},{20... | collective-permute-start | bytes 319496 | tf_op jit(solution)/shard_map/ppermute | solution.py:361
  97.9 0.0 copy-done.2
  98.0 1.7 %combine.2 = (bf16[128,4096]{1,0:T(8,128)(2,1)}, bf16[128,4096]{1,0:T(8,128)(2,1)}) custom-call(bf16[128,144]{1,0:T(8,128)(2,1)S(1)} %copy-done.2, bf16[32,72,256]{2,1,0:T(8,128)(2,1)S(1)} %all-to-all-done.3.back_ref), custom_call_target="tpu_custom_call" | custom-call | flops 1000000 | bytes 100000 | tf_op jit(solution)/shard_map/combine/pallas_call | solution.py:117
  99.6 0.0 collective-permute-done.7.refs_6_
  99.6 0.0 collective-permute-done.8.refs_7_
  99.6 0.0 collective-permute-done.9.refs_8_
  99.6 0.0 collective-permute-done.10.refs_9_
  99.6 0.0 collective-permute-done.3.refs_1_
  99.6 0.0 copy-done.8
  99.7 1.6 %place.1 = (f32[1,208,512]{2,1,0:T(8,128)}, f32[1,208,512]{2,1,0:T(8,128)}) custom-call(s32[3]{0:T(128)S(1)} %pad_add_fusion.info, f32[208,256]{1,0:T(8,128)S(1)} %get-tuple-element.68.refs_0_, bf16[208,256]{1,0:T(8,128)(2,1)S(1)} %collective-permute-done.3.refs_1_, bf16[208,256]{1,0:T(8,128)(2,1)S(1)} %copy-done.8, ...), custom_call_target="tpu_custom_call" | custom-call | flops 1000000 | bytes 100000 | tf_op jit(solution)/shard_map/place/pallas_call | solution.py:312
  101.3 2.0 %all-to-all-done.2.back_ref = bf16[32,72,256]{2,1,0:T(8,128)(2,1)S(1)} async-done(((bf16[32,72,256]{2,1,0:T(8,128)(2,1)}), bf16[32,72,256]{2,1,0:T(8,128)(2,1)S(1)}, u32[]{:S(2)}, u32[]{:S(2)}) %all-to-all-start.2) | async-done | bytes 1179680 | tf_op jit(solution)/shard_map/all_to_all | solution.py:355
  103.3 1.7 %combine.3 = (bf16[128,4096]{1,0:T(8,128)(2,1)}, bf16[128,4096]{1,0:T(8,128)(2,1)}) custom-call(bf16[128,144]{1,0:T(8,128)(2,1)S(1)} %copy-done.2, bf16[32,72,256]{2,1,0:T(8,128)(2,1)S(1)} %all-to-all-done.2.back_ref, bf16[128,4096]{1,0:T(8,128)(2,1)} %get-tuple-element.60.refs_0_, ...), custom_call_target="tpu_custom_call", output_to_operand_aliasing={{0}: (2, {}), {1}: (3, {})} | custom-call | flops 1000000 | bytes 100000 | tf_op jit(solution)/shard_map/combine/pallas_call | solution.py:117
  (2 shorter events, 0.0 us)
Async XLA Ops:
  3.6 26.6 %all-to-all-start = ((bf16[32,72,256]{2,1,0:T(8,128)(2,1)}), bf16[32,72,256]{2,1,0:T(8,128)(2,1)S(1)}, u32[]{:S(2)}, u32[]{:S(2)}) async-start(bf16[32,72,256]{2,1,0:T(8,128)(2,1)} %get-tuple-element.43), calls=%async_computation | async-start | bytes 2359296 | tf_op jit(solution)/shard_map/all_to_all | solution.py:342
  30.1 23.1 %all-to-all-start.1 = ((bf16[32,72,256]{2,1,0:T(8,128)(2,1)}), bf16[32,72,256]{2,1,0:T(8,128)(2,1)S(1)}, u32[]{:S(2)}, u32[]{:S(2)}) async-start(bf16[32,72,256]{2,1,0:T(8,128)(2,1)} %dispatch.3), calls=%async_computation.1 | async-start | bytes 2359296 | tf_op jit(solution)/shard_map/all_to_all | solution.py:343
  47.9 27.2 %collective-permute-start = (bf16[416,256]{1,0:T(8,128)(2,1)}, bf16[416,256]{1,0:T(8,128)(2,1)S(1)}, u32[]{:S(2)}, u32[]{:S(2)}) collective-permute-start(bf16[416,256]{1,0:T(8,128)(2,1)} %get-tuple-element.55), channel_id=1, source_target_pairs={{0,32},{32,64},{64,96},{96,0},{1,33},{33,65},{65,97},{97,1},{2,34}... | collective-permute-start | bytes 638984 | tf_op jit(solution)/shard_map/ppermute | solution.py:346
  49.9 26.0 %collective-permute-start.2 = (bf16[416,256]{1,0:T(8,128)(2,1)}, bf16[416,256]{1,0:T(8,128)(2,1)}, u32[]{:S(2)}, u32[]{:S(2)}) collective-permute-start(bf16[416,256]{1,0:T(8,128)(2,1)} %get-tuple-element.57), channel_id=1, source_target_pairs={{0,96},{32,0},{64,32},{96,64},{1,97},{33,1},{65,33},{97,65},{2,98}... | collective-permute-start | bytes 638984 | tf_op jit(solution)/shard_map/ppermute | solution.py:346
  53.3 8.1 %copy-start = (bf16[1,1664,128]{2,1,0:T(8,128)(2,1)S(1)}, bf16[1,1664,128]{2,1,0:T(8,128)(2,1)}, u32[]{:S(2)}) copy-start(bf16[1,1664,128]{2,1,0:T(8,128)(2,1)} %get-tuple-element.52.value_ref) | copy-start | bytes 1277956
  53.3 8.1 %copy-start.1 = (bf16[1,1664,128]{2,1,0:T(8,128)(2,1)S(1)}, bf16[1,1664,128]{2,1,0:T(8,128)(2,1)}, u32[]{:S(2)}) copy-start(bf16[1,1664,128]{2,1,0:T(8,128)(2,1)} %get-tuple-element.51.key_ref) | copy-start | bytes 1277956
  53.3 25.3 %all-to-all-start.3 = ((bf16[32,72,256]{2,1,0:T(8,128)(2,1)}), bf16[32,72,256]{2,1,0:T(8,128)(2,1)S(1)}, u32[]{:S(2)}, u32[]{:S(2)}) async-start(bf16[32,72,256]{2,1,0:T(8,128)(2,1)} %get-tuple-element.59), calls=%async_computation.3 | async-start | bytes 2359296 | tf_op jit(solution)/shard_map/all_to_all | solution.py:345
  59.4 16.4 %collective-permute-start.1 = (bf16[416,256]{1,0:T(8,128)(2,1)}, bf16[416,256]{1,0:T(8,128)(2,1)S(1)}, u32[]{:S(2)}, u32[]{:S(2)}) collective-permute-start(bf16[416,256]{1,0:T(8,128)(2,1)} %get-tuple-element.56), channel_id=1, source_target_pairs={{0,64},{32,96},{64,0},{96,32},{1,65},{33,97},{65,1},{97,33},{2,66}... | collective-permute-start | bytes 638984 | tf_op jit(solution)/shard_map/ppermute | solution.py:346
  75.1 0.7 copy-start.4
  75.8 0.7 copy-start.6
  76.5 9.1 %copy-start.12 = (bf16[208,256]{1,0:T(8,128)(2,1)S(1)}, bf16[208,256]{1,0:T(8,128)(2,1)}, u32[]{:S(2)}) copy-start(bf16[208,256]{1,0:T(8,128)(2,1)} %get-tuple-element.74) | copy-start | bytes 319492
  76.5 12.2 %copy-start.11 = (bf16[208,256]{1,0:T(8,128)(2,1)S(1)}, bf16[208,256]{1,0:T(8,128)(2,1)}, u32[]{:S(2)}) copy-start(bf16[208,256]{1,0:T(8,128)(2,1)} %get-tuple-element.75) | copy-start | bytes 319492
  76.5 12.6 %copy-start.3 = (bf16[416,256]{1,0:T(8,128)(2,1)S(1)}, bf16[416,256]{1,0:T(8,128)(2,1)}, u32[]{:S(2)}) copy-start(bf16[416,256]{1,0:T(8,128)(2,1)} %get-tuple-element.64.refs_0_) | copy-start | bytes 638980
  76.5 12.6 %copy-start.5 = (bf16[416,256]{1,0:T(8,128)(2,1)S(1)}, bf16[416,256]{1,0:T(8,128)(2,1)}, u32[]{:S(2)}) copy-start(bf16[416,256]{1,0:T(8,128)(2,1)} %copy-done.4) | copy-start | bytes 638980
  76.5 12.6 %copy-start.7 = (bf16[416,256]{1,0:T(8,128)(2,1)S(1)}, bf16[416,256]{1,0:T(8,128)(2,1)}, u32[]{:S(2)}) copy-start(bf16[416,256]{1,0:T(8,128)(2,1)} %copy-done.6) | copy-start | bytes 638980
  76.5 14.1 %copy-start.10 = (bf16[208,256]{1,0:T(8,128)(2,1)S(1)}, bf16[208,256]{1,0:T(8,128)(2,1)}, u32[]{:S(2)}) copy-start(bf16[208,256]{1,0:T(8,128)(2,1)} %get-tuple-element.76) | copy-start | bytes 319492
  76.5 16.8 %copy-start.9 = (bf16[208,256]{1,0:T(8,128)(2,1)S(1)}, bf16[208,256]{1,0:T(8,128)(2,1)}, u32[]{:S(2)}) copy-start(bf16[208,256]{1,0:T(8,128)(2,1)} %get-tuple-element.77) | copy-start | bytes 319492
  76.5 21.4 %copy-start.2 = (bf16[128,144]{1,0:T(8,128)(2,1)S(1)}, bf16[128,144]{1,0:T(8,128)(2,1)}, u32[]{:S(2)}) copy-start(bf16[128,144]{1,0:T(8,128)(2,1)} %get-tuple-element.42.turned_ref) | copy-start | bytes 110596
  78.6 24.7 %all-to-all-start.2 = ((bf16[32,72,256]{2,1,0:T(8,128)(2,1)}), bf16[32,72,256]{2,1,0:T(8,128)(2,1)S(1)}, u32[]{:S(2)}, u32[]{:S(2)}) async-start(bf16[32,72,256]{2,1,0:T(8,128)(2,1)} %get-tuple-element.58), calls=%async_computation.2 | async-start | bytes 2359296 | tf_op jit(solution)/shard_map/all_to_all | solution.py:355
  84.1 15.6 %copy-start.8 = (bf16[208,256]{1,0:T(8,128)(2,1)S(1)}, bf16[208,256]{1,0:T(8,128)(2,1)}, u32[]{:S(2)}) copy-start(bf16[208,256]{1,0:T(8,128)(2,1)} %get-tuple-element.70.refs_2_) | copy-start | bytes 319492
  84.1 6.6 %collective-permute-start.4 = (bf16[208,256]{1,0:T(8,128)(2,1)}, bf16[208,256]{1,0:T(8,128)(2,1)S(1)}, u32[]{:S(2)}, u32[]{:S(2)}) collective-permute-start(bf16[208,256]{1,0:T(8,128)(2,1)} %get-tuple-element.71), channel_id=1, source_target_pairs={{0,16},{16,0},{32,48},{48,32},{64,80},{80,64},{96,112},{112,96},{1... | collective-permute-start | bytes 319496 | tf_op jit(solution)/shard_map/ppermute | solution.py:359
  84.5 8.9 %collective-permute-start.5 = (bf16[208,256]{1,0:T(8,128)(2,1)}, bf16[208,256]{1,0:T(8,128)(2,1)S(1)}, u32[]{:S(2)}, u32[]{:S(2)}) collective-permute-start(bf16[208,256]{1,0:T(8,128)(2,1)} %get-tuple-element.72), channel_id=1, source_target_pairs={{0,32},{16,48},{32,64},{48,80},{64,96},{80,112},{96,0},{112,16},{1... | collective-permute-start | bytes 319496 | tf_op jit(solution)/shard_map/ppermute | solution.py:359
  85.5 8.5 %collective-permute-start.6 = (bf16[208,256]{1,0:T(8,128)(2,1)}, bf16[208,256]{1,0:T(8,128)(2,1)S(1)}, u32[]{:S(2)}, u32[]{:S(2)}) collective-permute-start(bf16[208,256]{1,0:T(8,128)(2,1)} %get-tuple-element.73), channel_id=1, source_target_pairs={{0,48},{16,32},{32,80},{48,64},{64,112},{80,96},{96,16},{112,0},{1... | collective-permute-start | bytes 319496 | tf_op jit(solution)/shard_map/ppermute | solution.py:359
  85.6 14.0 %collective-permute-start.7 = (bf16[208,256]{1,0:T(8,128)(2,1)S(1)}, bf16[208,256]{1,0:T(8,128)(2,1)S(1)}, u32[]{:S(2)}, u32[]{:S(2)}) collective-permute-start(bf16[208,256]{1,0:T(8,128)(2,1)S(1)} %copy-done.12), channel_id=1, source_target_pairs={{0,64},{16,80},{32,96},{48,112},{64,0},{80,16},{96,32},{112,48},{1... | collective-permute-start | bytes 319496 | tf_op jit(solution)/shard_map/ppermute | solution.py:359
  88.7 10.9 %collective-permute-start.8 = (bf16[208,256]{1,0:T(8,128)(2,1)S(1)}, bf16[208,256]{1,0:T(8,128)(2,1)S(1)}, u32[]{:S(2)}, u32[]{:S(2)}) collective-permute-start(bf16[208,256]{1,0:T(8,128)(2,1)S(1)} %copy-done.11), channel_id=1, source_target_pairs={{0,80},{16,64},{32,112},{48,96},{64,16},{80,0},{96,48},{112,32},{1... | collective-permute-start | bytes 319496 | tf_op jit(solution)/shard_map/ppermute | solution.py:359
  90.7 8.9 %collective-permute-start.9 = (bf16[208,256]{1,0:T(8,128)(2,1)S(1)}, bf16[208,256]{1,0:T(8,128)(2,1)S(1)}, u32[]{:S(2)}, u32[]{:S(2)}) collective-permute-start(bf16[208,256]{1,0:T(8,128)(2,1)S(1)} %copy-done.10), channel_id=1, source_target_pairs={{0,96},{16,112},{32,0},{48,16},{64,32},{80,48},{96,64},{112,80},{1... | collective-permute-start | bytes 319496 | tf_op jit(solution)/shard_map/ppermute | solution.py:359
  93.4 6.2 %collective-permute-start.10 = (bf16[208,256]{1,0:T(8,128)(2,1)S(1)}, bf16[208,256]{1,0:T(8,128)(2,1)S(1)}, u32[]{:S(2)}, u32[]{:S(2)}) collective-permute-start(bf16[208,256]{1,0:T(8,128)(2,1)S(1)} %copy-done.9), channel_id=1, source_target_pairs={{0,112},{16,96},{32,16},{48,0},{64,48},{80,32},{96,80},{112,64},{1... | collective-permute-start | bytes 319496 | tf_op jit(solution)/shard_map/ppermute | solution.py:359
  93.9 5.7 %collective-permute-start.3 = (bf16[208,256]{1,0:T(8,128)(2,1)S(1)}, bf16[208,256]{1,0:T(8,128)(2,1)S(1)}, u32[]{:S(2)}, u32[]{:S(2)}) collective-permute-start(bf16[208,256]{1,0:T(8,128)(2,1)S(1)} %get-tuple-element.69), channel_id=1, source_target_pairs={{0,16},{16,0},{1,17},{17,1},{2,18},{18,2},{3,19},{19,3},{4,20},{20... | collective-permute-start | bytes 319496 | tf_op jit(solution)/shard_map/ppermute | solution.py:361

commit v6 on v5

--- a/solution.py
+++ b/solution.py
@@ -40,12 +40,18 @@
     return jnp.where(held == turn, 1.0, 0.0)
 
 
-def route_kernel(ids_ref, query_ref, grad_ref, sent_ref, slots_ref, turned_ref, ninth_ref):
+def route_kernel(ids_ref, query_ref, grad_ref, sent_ref, slots_ref, ninth_ref):
     @pl.when(pl.program_id(0) == 0)
     def _():
-        slots = token_slots(ids_ref[...], sent_ref.shape[0])
-        slots_ref[...] = slots.astype(BF16)
-        turned_ref[...] = slots.T.astype(BF16)
+        slots_ref[...] = token_slots(ids_ref[...], sent_ref.shape[0]).astype(BF16)
+
+    dispatch_kernel(slots_ref, query_ref, grad_ref, sent_ref, ninth_ref)
+
+
+def turn_kernel(slots_ref, query_ref, grad_ref, sent_ref, turned_ref, ninth_ref):
+    @pl.when(pl.program_id(0) == 0)
+    def _():
+        turned_ref[...] = slots_ref[...].astype(F32).T.astype(BF16)
 
     dispatch_kernel(slots_ref, query_ref, grad_ref, sent_ref, ninth_ref)
 
@@ -71,12 +77,11 @@
     fixed = lambda shape: pl.BlockSpec(shape, lambda i: (0, 0))
     out_specs = [pl.BlockSpec((tile_num, CAP * GROUP, 2 * HEAD_WIDTH), lambda i: (i, 0, 0))]
     out_shape = [jax.ShapeDtypeStruct((2 * tile_num, CAP * GROUP, 2 * HEAD_WIDTH), BF16)]
-    if part == 0:
-        for shape in ((tile_num * CAP, tokens), (tokens, tile_num * CAP)):
-            out_specs.append(fixed(shape))
-            out_shape.append(jax.ShapeDtypeStruct(shape, BF16))
-    return pl.pallas_call(
-        route_kernel if part == 0 else dispatch_kernel,
+    shape = (tile_num * CAP, tokens) if part == 0 else (tokens, tile_num * CAP)
+    out_specs.append(fixed(shape))
+    out_shape.append(jax.ShapeDtypeStruct(shape, BF16))
+    return pl.pallas_call(
+        route_kernel if part == 0 else turn_kernel,
         grid=(2,),
         in_specs=[fixed(routing.shape), block, block],
         out_specs=out_specs,
@@ -332,8 +337,8 @@
         lax.all_to_all, axis_name=("core", "img"), split_axis=0, concat_axis=0, tiled=True
     )
     ids = tile_ids.reshape(1, -1)
-    sent, slots, turned = dispatch(ids, queries, output_gradient, 0, tile_num)
-    (later,) = dispatch(slots, queries, output_gradient, 1, tile_num)
+    sent, slots = dispatch(ids, queries, output_gradient, 0, tile_num)
+    later, turned = dispatch(slots, queries, output_gradient, 1, tile_num)
     first = 2 * lax.axis_index("core") * HEAD_WIDTH
     tiles = [
         [lax.dynamic_slice_in_dim(a, first + part * HEAD_WIDTH, HEAD_WIDTH, 2) for a in (keys, values)]

time: 106 us -> 105 us (level)
  transfers between devices with their start and end apart: 15 -> 15, of which waited for: 4 -> 4; matrix products, arithmetic and copies ran while one was open for 2% -> 2% of each run, Pallas kernels for 33% -> 34%
where the time goes in v6:
time: 105 us
  starting transfers between devices  41.2 us (39%)
  Pallas kernels  39.6 us (38%)
  waiting for transfers between devices  18.7 us (18%)
  local copies, waits for them, and re-layouts  3.85 us (4%)
  between operations  1.43 us (1%)
    pallas_call x2, Pallas kernels, attend(): pl.pallas_call(functools.partial(attend_kernel, ways=ways, depth=depth),...  27.6 us
    all_to_all x1, waiting for transfers between devices, local(): exchange(sent)  13.4 us
    ppermute x7, starting transfers between devices, local(): later[i] = lax.ppermute(later[i], ('z', 'core'), pairs)  8.22 us
    all_to_all x1, starting transfers between devices, local(): exchange(sent)  7.41 us
    all_to_all x1, starting transfers between devices, local(): first_back = exchange(back)  6.16 us
    ppermute x3, starting transfers between devices, local(): lax.ppermute(share, 'z', [(z, (z + i) % depth) for z in range(depth)])  5.97 us
    all_to_all x1, starting transfers between devices, local(): second_back = exchange(back)  5.48 us
    pallas_call x2, Pallas kernels, dispatch(): pl.pallas_call(route_kernel if part == 0 else turn_kernel, grid=(2,), in_...  5.47 us
  transfers between devices with their start and end apart: 15, of which 4 were waited for; matrix products, arithmetic and copies ran while one was open for 2% of the time, Pallas kernels for 34%

profile of v6, /device:TPU:0, one launch (start us, length us, event | category | flops | bytes accessed | tf_op | source)
XLA Modules:
  0.0 104.8 jit_solution(2152152160790455358)
XLA Ops:
  0.6 2.8 %dispatch.2 = (bf16[32,72,256]{2,1,0:T(8,128)(2,1)}, bf16[144,128]{1,0:T(8,128)(2,1)}) custom-call(s32[1,128]{1,0:T(1,128)} %bitcast.3, bf16[128,4096]{1,0:T(8,128)(2,1)} %query_ref.3, bf16[128,4096]{1,0:T(8,128)(2,1)} %grad_ref.3), custom_call_target="tpu_custom_call" | custom-call | flops 1000000000 | bytes 3000000 | tf_op jit(solution)/shard_map/dispatch/pallas_call | solution.py:83
  3.5 7.4 %all-to-all-start = ((bf16[32,72,256]{2,1,0:T(8,128)(2,1)}), bf16[32,72,256]{2,1,0:T(8,128)(2,1)S(1)}, u32[]{:S(2)}, u32[]{:S(2)}) async-start(bf16[32,72,256]{2,1,0:T(8,128)(2,1)} %get-tuple-element.45), calls=%async_computation | async-start | bytes 2359296 | tf_op jit(solution)/shard_map/all_to_all | solution.py:347
  11.5 2.6 %dispatch.3 = (bf16[32,72,256]{2,1,0:T(8,128)(2,1)}, bf16[128,144]{1,0:T(8,128)(2,1)}) custom-call(bf16[144,128]{1,0:T(8,128)(2,1)} %get-tuple-element.43.slots_ref, bf16[128,4096]{1,0:T(8,128)(2,1)} %query_ref.3, bf16[128,4096]{1,0:T(8,128)(2,1)} %grad_ref.3), custom_call_target="tpu_custom_call" | custom-call | flops 1000000000 | bytes 3000000 | tf_op jit(solution)/shard_map/dispatch/pallas_call | solution.py:83
  14.2 0.1 pad_add_fusion.info
  14.2 2.4 %constant_dynamic-slice_fusion = (bf16[1,1664,128]{2,1,0:T(8,128)(2,1)}, bf16[1,1664,128]{2,1,0:T(8,128)(2,1)S(1)}, bf16[1,1664,128]{2,1,0:T(8,128)(2,1)S(1)}, bf16[1,1664,128]{2,1,0:T(8,128)(2,1)}) fusion(bf16[1,1664,512]{2,1,0:T(8,128)(2,1)} %param.9, s32[]{:T(128)S(6)} %select_n.9, s32[]{:T(128)S(6)} %select_n.8, bf16[1,1664,512]{2,1,0:T(8,128)(2,1)} %param.8), kind=kLoop, calls=%fused_computation | loop fusion | bytes 3407880 | tf_op jit(solution)/shard_map/dynamic_slice | solution.py:344
  16.7 13.4 %all-to-all-done.rows_ref = bf16[32,72,256]{2,1,0:T(8,128)(2,1)S(1)} async-done(((bf16[32,72,256]{2,1,0:T(8,128)(2,1)}), bf16[32,72,256]{2,1,0:T(8,128)(2,1)S(1)}, u32[]{:S(2)}, u32[]{:S(2)}) %all-to-all-start) | async-done | bytes 1179680 | tf_op jit(solution)/shard_map/all_to_all | solution.py:347
  30.0 3.9 %all-to-all-start.1 = ((bf16[32,72,256]{2,1,0:T(8,128)(2,1)}), bf16[32,72,256]{2,1,0:T(8,128)(2,1)S(1)}, u32[]{:S(2)}, u32[]{:S(2)}) async-start(bf16[32,72,256]{2,1,0:T(8,128)(2,1)} %get-tuple-element.51), calls=%async_computation.1 | async-start | bytes 2359296 | tf_op jit(solution)/shard_map/all_to_all | solution.py:348
  34.0 13.8 %attend.2 = (bf16[32,72,256]{2,1,0:T(8,128)(2,1)}, bf16[416,256]{1,0:T(8,128)(2,1)}, bf16[416,256]{1,0:T(8,128)(2,1)}, bf16[416,256]{1,0:T(8,128)(2,1)}, bf16[416,256]{1,0:T(8,128)(2,1)}) custom-call(s32[3]{0:T(128)S(1)} %pad_add_fusion.info, bf16[32,72,256]{2,1,0:T(8,128)(2,1)S(1)} %all-to-all-done.rows_ref, ...), custom_call_target="tpu_custom_call" | custom-call | flops 29444014080 | bytes 4000000 | tf_op jit(solution)/shard_map/attend/pallas_call | solution.py:241
  47.8 1.9 %collective-permute-start = (bf16[416,256]{1,0:T(8,128)(2,1)}, bf16[416,256]{1,0:T(8,128)(2,1)S(1)}, u32[]{:S(2)}, u32[]{:S(2)}) collective-permute-start(bf16[416,256]{1,0:T(8,128)(2,1)} %get-tuple-element.57), channel_id=1, source_target_pairs={{0,32},{32,64},{64,96},{96,0},{1,33},{33,65},{65,97},{97,1},{2,34}... | collective-permute-start | bytes 638984 | tf_op jit(solution)/shard_map/ppermute | solution.py:351
  49.7 2.1 %collective-permute-start.2 = (bf16[416,256]{1,0:T(8,128)(2,1)}, bf16[416,256]{1,0:T(8,128)(2,1)}, u32[]{:S(2)}, u32[]{:S(2)}) collective-permute-start(bf16[416,256]{1,0:T(8,128)(2,1)} %get-tuple-element.59), channel_id=1, source_target_pairs={{0,96},{32,0},{64,32},{96,64},{1,97},{33,1},{65,33},{97,65},{2,98}... | collective-permute-start | bytes 638984 | tf_op jit(solution)/shard_map/ppermute | solution.py:351
  51.9 1.3 %all-to-all-done.1.rows_ref = bf16[32,72,256]{2,1,0:T(8,128)(2,1)S(1)} async-done(((bf16[32,72,256]{2,1,0:T(8,128)(2,1)}), bf16[32,72,256]{2,1,0:T(8,128)(2,1)S(1)}, u32[]{:S(2)}, u32[]{:S(2)}) %all-to-all-start.1) | async-done | bytes 1179680 | tf_op jit(solution)/shard_map/all_to_all | solution.py:348
  53.2 0.0 copy-start
  53.2 0.0 copy-start.1
  53.2 6.2 %all-to-all-start.3 = ((bf16[32,72,256]{2,1,0:T(8,128)(2,1)}), bf16[32,72,256]{2,1,0:T(8,128)(2,1)S(1)}, u32[]{:S(2)}, u32[]{:S(2)}) async-start(bf16[32,72,256]{2,1,0:T(8,128)(2,1)} %get-tuple-element.61), calls=%async_computation.3 | async-start | bytes 2359296 | tf_op jit(solution)/shard_map/all_to_all | solution.py:350
  59.3 1.9 %collective-permute-start.1 = (bf16[416,256]{1,0:T(8,128)(2,1)}, bf16[416,256]{1,0:T(8,128)(2,1)S(1)}, u32[]{:S(2)}, u32[]{:S(2)}) collective-permute-start(bf16[416,256]{1,0:T(8,128)(2,1)} %get-tuple-element.58), channel_id=1, source_target_pairs={{0,64},{32,96},{64,0},{96,32},{1,65},{33,97},{65,1},{97,33},{2,66}... | collective-permute-start | bytes 638984 | tf_op jit(solution)/shard_map/ppermute | solution.py:351
  61.3 0.0 copy-done
  61.3 0.0 copy-done.1
  61.3 13.8 %attend.3 = (bf16[32,72,256]{2,1,0:T(8,128)(2,1)}, bf16[208,256]{1,0:T(8,128)(2,1)}, bf16[208,256]{1,0:T(8,128)(2,1)}, bf16[208,256]{1,0:T(8,128)(2,1)}, bf16[20...) custom-call(s32[3]{0:T(128)S(1)} %pad_add_fusion.info, ...), custom_call_target="tpu_custom_call" | custom-call | flops 29444014080 | bytes 4000000 | tf_op jit(solution)/shard_map/attend/pallas_call | solution.py:241
  75.0 0.0 collective-permute-done.refs_1_
  75.0 0.0 copy-start.4
  75.0 0.7 copy-done.4
  75.7 0.0 collective-permute-done.2.refs_3_
  75.7 0.0 collective-permute-done.1.refs_2_
  75.7 0.0 copy-start.6
  75.7 0.7 copy-done.6
  76.4 0.0 copy-start.12
  76.4 0.0 copy-start.11
  76.4 0.0 copy-start.7
  76.4 0.0 copy-start.10
  76.4 0.0 copy-start.9
  76.4 0.0 copy-start.2
  76.5 2.0 %all-to-all-done.3.back_ref = bf16[32,72,256]{2,1,0:T(8,128)(2,1)S(1)} async-done(((bf16[32,72,256]{2,1,0:T(8,128)(2,1)}), bf16[32,72,256]{2,1,0:T(8,128)(2,1)S(1)}, u32[]{:S(2)}, u32[]{:S(2)}) %all-to-all-start.3) | async-done | bytes 1179680 | tf_op jit(solution)/shard_map/all_to_all | solution.py:350
  78.5 5.5 %all-to-all-start.2 = ((bf16[32,72,256]{2,1,0:T(8,128)(2,1)}), bf16[32,72,256]{2,1,0:T(8,128)(2,1)S(1)}, u32[]{:S(2)}, u32[]{:S(2)}) async-start(bf16[32,72,256]{2,1,0:T(8,128)(2,1)} %get-tuple-element.60), calls=%async_computation.2 | async-start | bytes 2359296 | tf_op jit(solution)/shard_map/all_to_all | solution.py:360
  84.0 0.0 copy-start.8
  84.0 0.4 collective-permute-start.4
  84.4 1.0 collective-permute-start.5
  85.4 0.2 collective-permute-start.6
  85.5 0.0 copy-done.12
  85.5 3.1 %collective-permute-start.7 = (bf16[208,256]{1,0:T(8,128)(2,1)S(1)}, bf16[208,256]{1,0:T(8,128)(2,1)S(1)}, u32[]{:S(2)}, u32[]{:S(2)}) collective-permute-start(bf16[208,256]{1,0:T(8,128)(2,1)S(1)} %copy-done.12), channel_id=1, source_target_pairs={{0,64},{16,80},{32,96},{48,112},{64,0},{80,16},{96,32},{112,48},{1... | collective-permute-start | bytes 319496 | tf_op jit(solution)/shard_map/ppermute | solution.py:364
  88.6 0.0 copy-done.11
  88.6 0.4 collective-permute-start.8
  89.0 0.0 copy-done.3
  89.0 0.0 copy-done.5
  89.0 0.0 copy-done.7
  89.0 1.6 %add_shares.1 = (f32[208,256]{1,0:T(8,128)S(1)}, bf16[208,256]{1,0:T(8,128)(2,1)S(1)}) custom-call(s32[3]{0:T(128)S(1)} %pad_add_fusion.info, bf16[416,256]{1,0:T(8,128)(2,1)S(1)} %copy-done.3, bf16[416,256]{1,0:T(8,128)(2,1)S(1)} %copy-done.5, bf16[416,256]{1,0:T(8,128)(2,1)S(1)} %copy-done.7, bf16[416,256]{1,0:T(8,128)(2,1)} %collective-permute-done.2.refs_3_), custom_call_target="tpu_custom_call" | custom-call | flops 1000000 | bytes 100000 | tf_op jit(solution)/shard_map/add_shares/pallas_call | solution.py:286
  90.6 0.0 collective-permute-done.4.refs_3_
  90.6 0.0 copy-done.10
  90.6 2.7 %collective-permute-start.9 = (bf16[208,256]{1,0:T(8,128)(2,1)S(1)}, bf16[208,256]{1,0:T(8,128)(2,1)S(1)}, u32[]{:S(2)}, u32[]{:S(2)}) collective-permute-start(bf16[208,256]{1,0:T(8,128)(2,1)S(1)} %copy-done.10), channel_id=1, source_target_pairs={{0,96},{16,112},{32,0},{48,16},{64,32},{80,48},{96,64},{112,80},{1... | collective-permute-start | bytes 319496 | tf_op jit(solution)/shard_map/ppermute | solution.py:364
  93.3 0.0 collective-permute-done.5.refs_4_
  93.3 0.0 copy-done.9
  93.3 0.6 collective-permute-start.10
  93.8 0.0 collective-permute-done.6.refs_5_
  93.8 4.0 %collective-permute-start.3 = (bf16[208,256]{1,0:T(8,128)(2,1)S(1)}, bf16[208,256]{1,0:T(8,128)(2,1)S(1)}, u32[]{:S(2)}, u32[]{:S(2)}) collective-permute-start(bf16[208,256]{1,0:T(8,128)(2,1)S(1)} %get-tuple-element.71), channel_id=1, source_target_pairs={{0,16},{16,0},{1,17},{17,1},{2,18},{18,2},{3,19},{19,3},{4,20},{20... | collective-permute-start | bytes 319496 | tf_op jit(solution)/shard_map/ppermute | solution.py:366
  97.8 0.0 copy-done.2
  97.8 1.7 %combine.2 = (bf16[128,4096]{1,0:T(8,128)(2,1)}, bf16[128,4096]{1,0:T(8,128)(2,1)}) custom-call(bf16[128,144]{1,0:T(8,128)(2,1)S(1)} %copy-done.2, bf16[32,72,256]{2,1,0:T(8,128)(2,1)S(1)} %all-to-all-done.3.back_ref), custom_call_target="tpu_custom_call" | custom-call | flops 1000000 | bytes 100000 | tf_op jit(solution)/shard_map/combine/pallas_call | solution.py:122
  99.5 0.0 collective-permute-done.7.refs_6_
  99.5 0.0 collective-permute-done.8.refs_7_
  99.5 0.0 collective-permute-done.9.refs_8_
  99.5 0.0 collective-permute-done.10.refs_9_
  99.5 0.0 collective-permute-done.3.refs_1_
  99.5 0.0 copy-done.8
  99.5 1.6 %place.1 = (f32[1,208,512]{2,1,0:T(8,128)}, f32[1,208,512]{2,1,0:T(8,128)}) custom-call(s32[3]{0:T(128)S(1)} %pad_add_fusion.info, f32[208,256]{1,0:T(8,128)S(1)} %get-tuple-element.70.refs_0_, bf16[208,256]{1,0:T(8,128)(2,1)S(1)} %collective-permute-done.3.refs_1_, bf16[208,256]{1,0:T(8,128)(2,1)S(1)} %copy-done.8, ...), custom_call_target="tpu_custom_call" | custom-call | flops 1000000 | bytes 100000 | tf_op jit(solution)/shard_map/place/pallas_call | solution.py:317
  101.2 2.0 %all-to-all-done.2.back_ref = bf16[32,72,256]{2,1,0:T(8,128)(2,1)S(1)} async-done(((bf16[32,72,256]{2,1,0:T(8,128)(2,1)}), bf16[32,72,256]{2,1,0:T(8,128)(2,1)S(1)}, u32[]{:S(2)}, u32[]{:S(2)}) %all-to-all-start.2) | async-done | bytes 1179680 | tf_op jit(solution)/shard_map/all_to_all | solution.py:360
  103.1 1.7 %combine.3 = (bf16[128,4096]{1,0:T(8,128)(2,1)}, bf16[128,4096]{1,0:T(8,128)(2,1)}) custom-call(bf16[128,144]{1,0:T(8,128)(2,1)S(1)} %copy-done.2, bf16[32,72,256]{2,1,0:T(8,128)(2,1)S(1)} %all-to-all-done.2.back_ref, bf16[128,4096]{1,0:T(8,128)(2,1)} %get-tuple-element.62.refs_0_, ...), custom_call_target="tpu_custom_call", output_to_operand_aliasing={{0}: (2, {}), {1}: (3, {})} | custom-call | flops 1000000 | bytes 100000 | tf_op jit(solution)/shard_map/combine/pallas_call | solution.py:122
  (2 shorter events, 0.0 us)
Async XLA Ops:
  3.5 26.6 %all-to-all-start = ((bf16[32,72,256]{2,1,0:T(8,128)(2,1)}), bf16[32,72,256]{2,1,0:T(8,128)(2,1)S(1)}, u32[]{:S(2)}, u32[]{:S(2)}) async-start(bf16[32,72,256]{2,1,0:T(8,128)(2,1)} %get-tuple-element.45), calls=%async_computation | async-start | bytes 2359296 | tf_op jit(solution)/shard_map/all_to_all | solution.py:347
  30.0 23.1 %all-to-all-start.1 = ((bf16[32,72,256]{2,1,0:T(8,128)(2,1)}), bf16[32,72,256]{2,1,0:T(8,128)(2,1)S(1)}, u32[]{:S(2)}, u32[]{:S(2)}) async-start(bf16[32,72,256]{2,1,0:T(8,128)(2,1)} %get-tuple-element.51), calls=%async_computation.1 | async-start | bytes 2359296 | tf_op jit(solution)/shard_map/all_to_all | solution.py:348
  47.8 27.2 %collective-permute-start = (bf16[416,256]{1,0:T(8,128)(2,1)}, bf16[416,256]{1,0:T(8,128)(2,1)S(1)}, u32[]{:S(2)}, u32[]{:S(2)}) collective-permute-start(bf16[416,256]{1,0:T(8,128)(2,1)} %get-tuple-element.57), channel_id=1, source_target_pairs={{0,32},{32,64},{64,96},{96,0},{1,33},{33,65},{65,97},{97,1},{2,34}... | collective-permute-start | bytes 638984 | tf_op jit(solution)/shard_map/ppermute | solution.py:351
  49.7 26.0 %collective-permute-start.2 = (bf16[416,256]{1,0:T(8,128)(2,1)}, bf16[416,256]{1,0:T(8,128)(2,1)}, u32[]{:S(2)}, u32[]{:S(2)}) collective-permute-start(bf16[416,256]{1,0:T(8,128)(2,1)} %get-tuple-element.59), channel_id=1, source_target_pairs={{0,96},{32,0},{64,32},{96,64},{1,97},{33,1},{65,33},{97,65},{2,98}... | collective-permute-start | bytes 638984 | tf_op jit(solution)/shard_map/ppermute | solution.py:351
  53.2 8.1 %copy-start = (bf16[1,1664,128]{2,1,0:T(8,128)(2,1)S(1)}, bf16[1,1664,128]{2,1,0:T(8,128)(2,1)}, u32[]{:S(2)}) copy-start(bf16[1,1664,128]{2,1,0:T(8,128)(2,1)} %get-tuple-element.54.value_ref) | copy-start | bytes 1277956
  53.2 8.1 %copy-start.1 = (bf16[1,1664,128]{2,1,0:T(8,128)(2,1)S(1)}, bf16[1,1664,128]{2,1,0:T(8,128)(2,1)}, u32[]{:S(2)}) copy-start(bf16[1,1664,128]{2,1,0:T(8,128)(2,1)} %get-tuple-element.53.key_ref) | copy-start | bytes 1277956
  53.2 25.3 %all-to-all-start.3 = ((bf16[32,72,256]{2,1,0:T(8,128)(2,1)}), bf16[32,72,256]{2,1,0:T(8,128)(2,1)S(1)}, u32[]{:S(2)}, u32[]{:S(2)}) async-start(bf16[32,72,256]{2,1,0:T(8,128)(2,1)} %get-tuple-element.61), calls=%async_computation.3 | async-start | bytes 2359296 | tf_op jit(solution)/shard_map/all_to_all | solution.py:350
  59.3 16.4 %collective-permute-start.1 = (bf16[416,256]{1,0:T(8,128)(2,1)}, bf16[416,256]{1,0:T(8,128)(2,1)S(1)}, u32[]{:S(2)}, u32[]{:S(2)}) collective-permute-start(bf16[416,256]{1,0:T(8,128)(2,1)} %get-tuple-element.58), channel_id=1, source_target_pairs={{0,64},{32,96},{64,0},{96,32},{1,65},{33,97},{65,1},{97,33},{2,66}... | collective-permute-start | bytes 638984 | tf_op jit(solution)/shard_map/ppermute | solution.py:351
  75.0 0.7 copy-start.4
  75.7 0.7 copy-start.6
  76.4 9.1 %copy-start.12 = (bf16[208,256]{1,0:T(8,128)(2,1)S(1)}, bf16[208,256]{1,0:T(8,128)(2,1)}, u32[]{:S(2)}) copy-start(bf16[208,256]{1,0:T(8,128)(2,1)} %get-tuple-element.76) | copy-start | bytes 319492
  76.4 12.2 %copy-start.11 = (bf16[208,256]{1,0:T(8,128)(2,1)S(1)}, bf16[208,256]{1,0:T(8,128)(2,1)}, u32[]{:S(2)}) copy-start(bf16[208,256]{1,0:T(8,128)(2,1)} %get-tuple-element.77) | copy-start | bytes 319492
  76.4 12.6 %copy-start.3 = (bf16[416,256]{1,0:T(8,128)(2,1)S(1)}, bf16[416,256]{1,0:T(8,128)(2,1)}, u32[]{:S(2)}) copy-start(bf16[416,256]{1,0:T(8,128)(2,1)} %get-tuple-element.66.refs_0_) | copy-start | bytes 638980
  76.4 12.6 %copy-start.5 = (bf16[416,256]{1,0:T(8,128)(2,1)S(1)}, bf16[416,256]{1,0:T(8,128)(2,1)}, u32[]{:S(2)}) copy-start(bf16[416,256]{1,0:T(8,128)(2,1)} %copy-done.4) | copy-start | bytes 638980
  76.4 12.6 %copy-start.7 = (bf16[416,256]{1,0:T(8,128)(2,1)S(1)}, bf16[416,256]{1,0:T(8,128)(2,1)}, u32[]{:S(2)}) copy-start(bf16[416,256]{1,0:T(8,128)(2,1)} %copy-done.6) | copy-start | bytes 638980
  76.4 14.1 %copy-start.10 = (bf16[208,256]{1,0:T(8,128)(2,1)S(1)}, bf16[208,256]{1,0:T(8,128)(2,1)}, u32[]{:S(2)}) copy-start(bf16[208,256]{1,0:T(8,128)(2,1)} %get-tuple-element.78) | copy-start | bytes 319492
  76.4 16.8 %copy-start.9 = (bf16[208,256]{1,0:T(8,128)(2,1)S(1)}, bf16[208,256]{1,0:T(8,128)(2,1)}, u32[]{:S(2)}) copy-start(bf16[208,256]{1,0:T(8,128)(2,1)} %get-tuple-element.79) | copy-start | bytes 319492
  76.4 21.4 %copy-start.2 = (bf16[128,144]{1,0:T(8,128)(2,1)S(1)}, bf16[128,144]{1,0:T(8,128)(2,1)}, u32[]{:S(2)}) copy-start(bf16[128,144]{1,0:T(8,128)(2,1)} %get-tuple-element.44.turned_ref) | copy-start | bytes 110596
  78.5 24.7 %all-to-all-start.2 = ((bf16[32,72,256]{2,1,0:T(8,128)(2,1)}), bf16[32,72,256]{2,1,0:T(8,128)(2,1)S(1)}, u32[]{:S(2)}, u32[]{:S(2)}) async-start(bf16[32,72,256]{2,1,0:T(8,128)(2,1)} %get-tuple-element.60), calls=%async_computation.2 | async-start | bytes 2359296 | tf_op jit(solution)/shard_map/all_to_all | solution.py:360
  84.0 15.6 %copy-start.8 = (bf16[208,256]{1,0:T(8,128)(2,1)S(1)}, bf16[208,256]{1,0:T(8,128)(2,1)}, u32[]{:S(2)}) copy-start(bf16[208,256]{1,0:T(8,128)(2,1)} %get-tuple-element.72.refs_2_) | copy-start | bytes 319492
  84.0 6.6 %collective-permute-start.4 = (bf16[208,256]{1,0:T(8,128)(2,1)}, bf16[208,256]{1,0:T(8,128)(2,1)S(1)}, u32[]{:S(2)}, u32[]{:S(2)}) collective-permute-start(bf16[208,256]{1,0:T(8,128)(2,1)} %get-tuple-element.73), channel_id=1, source_target_pairs={{0,16},{16,0},{32,48},{48,32},{64,80},{80,64},{96,112},{112,96},{1... | collective-permute-start | bytes 319496 | tf_op jit(solution)/shard_map/ppermute | solution.py:364
  84.4 8.9 %collective-permute-start.5 = (bf16[208,256]{1,0:T(8,128)(2,1)}, bf16[208,256]{1,0:T(8,128)(2,1)S(1)}, u32[]{:S(2)}, u32[]{:S(2)}) collective-permute-start(bf16[208,256]{1,0:T(8,128)(2,1)} %get-tuple-element.74), channel_id=1, source_target_pairs={{0,32},{16,48},{32,64},{48,80},{64,96},{80,112},{96,0},{112,16},{1... | collective-permute-start | bytes 319496 | tf_op jit(solution)/shard_map/ppermute | solution.py:364
  85.4 8.4 %collective-permute-start.6 = (bf16[208,256]{1,0:T(8,128)(2,1)}, bf16[208,256]{1,0:T(8,128)(2,1)S(1)}, u32[]{:S(2)}, u32[]{:S(2)}) collective-permute-start(bf16[208,256]{1,0:T(8,128)(2,1)} %get-tuple-element.75), channel_id=1, source_target_pairs={{0,48},{16,32},{32,80},{48,64},{64,112},{80,96},{96,16},{112,0},{1... | collective-permute-start | bytes 319496 | tf_op jit(solution)/shard_map/ppermute | solution.py:364
  85.5 14.0 %collective-permute-start.7 = (bf16[208,256]{1,0:T(8,128)(2,1)S(1)}, bf16[208,256]{1,0:T(8,128)(2,1)S(1)}, u32[]{:S(2)}, u32[]{:S(2)}) collective-permute-start(bf16[208,256]{1,0:T(8,128)(2,1)S(1)} %copy-done.12), channel_id=1, source_target_pairs={{0,64},{16,80},{32,96},{48,112},{64,0},{80,16},{96,32},{112,48},{1... | collective-permute-start | bytes 319496 | tf_op jit(solution)/shard_map/ppermute | solution.py:364
  88.6 10.9 %collective-permute-start.8 = (bf16[208,256]{1,0:T(8,128)(2,1)S(1)}, bf16[208,256]{1,0:T(8,128)(2,1)S(1)}, u32[]{:S(2)}, u32[]{:S(2)}) collective-permute-start(bf16[208,256]{1,0:T(8,128)(2,1)S(1)} %copy-done.11), channel_id=1, source_target_pairs={{0,80},{16,64},{32,112},{48,96},{64,16},{80,0},{96,48},{112,32},{1... | collective-permute-start | bytes 319496 | tf_op jit(solution)/shard_map/ppermute | solution.py:364
  90.6 8.9 %collective-permute-start.9 = (bf16[208,256]{1,0:T(8,128)(2,1)S(1)}, bf16[208,256]{1,0:T(8,128)(2,1)S(1)}, u32[]{:S(2)}, u32[]{:S(2)}) collective-permute-start(bf16[208,256]{1,0:T(8,128)(2,1)S(1)} %copy-done.10), channel_id=1, source_target_pairs={{0,96},{16,112},{32,0},{48,16},{64,32},{80,48},{96,64},{112,80},{1... | collective-permute-start | bytes 319496 | tf_op jit(solution)/shard_map/ppermute | solution.py:364
  93.3 6.2 %collective-permute-start.10 = (bf16[208,256]{1,0:T(8,128)(2,1)S(1)}, bf16[208,256]{1,0:T(8,128)(2,1)S(1)}, u32[]{:S(2)}, u32[]{:S(2)}) collective-permute-start(bf16[208,256]{1,0:T(8,128)(2,1)S(1)} %copy-done.9), channel_id=1, source_target_pairs={{0,112},{16,96},{32,16},{48,0},{64,48},{80,32},{96,80},{112,64},{1... | collective-permute-start | bytes 319496 | tf_op jit(solution)/shard_map/ppermute | solution.py:364
  93.8 5.7 %collective-permute-start.3 = (bf16[208,256]{1,0:T(8,128)(2,1)S(1)}, bf16[208,256]{1,0:T(8,128)(2,1)S(1)}, u32[]{:S(2)}, u32[]{:S(2)}) collective-permute-start(bf16[208,256]{1,0:T(8,128)(2,1)S(1)} %get-tuple-element.71), channel_id=1, source_target_pairs={{0,16},{16,0},{1,17},{17,1},{2,18},{18,2},{3,19},{19,3},{4,20},{20... | collective-permute-start | bytes 319496 | tf_op jit(solution)/shard_map/ppermute | solution.py:366
